TPU v7x, 32 devices: a whole 2x2x4 slice. The times are simulated.
32 devices in a mesh: lon: 4 (over y, x), batch: 8 (over z, core).
Axes of the slice: x: 2, y: 2, z: 4, core: 2. Of those that a mesh axis runs over, the one named last changes fastest.
Arguments:
- frames: bfloat16 [32, 32, 32, 256], P('batch', None, 'lon'), may hold values from -6 to 6
- latent_init: bfloat16 [32, 32, 32, 32], P('batch', None, 'lon'), may hold values from -0.8984375 to 0.8984375
- crop_band: int32 [32, 2], P('batch'), may hold values from 0 to 32, as said below
- cotangent: bfloat16 [32, 32, 32, 256], P('batch', None, 'lon'), may hold values from -6 to 6
- triple_weight: float32 [2, 256, 768], replicated, may hold values from -0.375 to 0.375
- triple_moment: float32 [2, 256, 768], replicated, may hold values from -0.75 to 0.75
- triple_average: float32 [2, 256, 768], replicated, may hold values from -0.375 to 0.375
- output_weight: float32 [2, 256, 256], replicated, may hold values from -1 to 1
- output_moment: float32 [2, 256, 256], replicated, may hold values from -0.75 to 0.75
- output_average: float32 [2, 256, 256], replicated, may hold values from -1 to 1
- expand_weight: float32 [2, 256, 1024], replicated, may hold values from -0.375 to 0.375
- expand_moment: float32 [2, 256, 1024], replicated, may hold values from -0.75 to 0.75
- expand_average: float32 [2, 256, 1024], replicated, may hold values from -0.375 to 0.375
- shrink_weight: float32 [2, 1024, 256], replicated, may hold values from -0.1875 to 0.1875
- shrink_moment: float32 [2, 1024, 256], replicated, may hold values from -0.75 to 0.75
- shrink_average: float32 [2, 1024, 256], replicated, may hold values from -0.1875 to 0.1875
- recurrent_weight: float32 [2, 288, 32], replicated, may hold values from -0.375 to 0.375
- recurrent_moment: float32 [2, 288, 32], replicated, may hold values from -0.75 to 0.75
- recurrent_average: float32 [2, 288, 32], replicated, may hold values from -0.375 to 0.375
- readout_weight: float32 [2, 32, 256], replicated, may hold values from -1 to 1
- readout_moment: float32 [2, 32, 256], replicated, may hold values from -0.75 to 0.75
- readout_average: float32 [2, 32, 256], replicated, may hold values from -1 to 1
- gains_weight: float32 [2, 3, 256], replicated, may hold values from 0.5 to 1.5
- gains_moment: float32 [2, 3, 256], replicated, may hold values from -1.5 to 1.5
- gains_average: float32 [2, 3, 256], replicated, may hold values from 0.5 to 1.5
- table_weight: float32 [2, 8, 225], replicated, may hold values from -3 to 3
- table_moment: float32 [2, 8, 225], replicated, may hold values from -1.5 to 1.5
- table_average: float32 [2, 8, 225], replicated, may hold values from -3 to 3
Outputs:
- activations: bfloat16 [32, 32, 32, 256], P('batch', None, 'lon')
- input_grad: float32 [32, 32, 32, 256], P('batch', None, 'lon')
- triple_updated: float32 [2, 256, 768], replicated
- triple_velocity: float32 [2, 256, 768], replicated
- triple_smoothed: float32 [2, 256, 768], replicated
- output_updated: float32 [2, 256, 256], replicated
- output_velocity: float32 [2, 256, 256], replicated
- output_smoothed: float32 [2, 256, 256], replicated
- expand_updated: float32 [2, 256, 1024], replicated
- expand_velocity: float32 [2, 256, 1024], replicated
- expand_smoothed: float32 [2, 256, 1024], replicated
- shrink_updated: float32 [2, 1024, 256], replicated
- shrink_velocity: float32 [2, 1024, 256], replicated
- shrink_smoothed: float32 [2, 1024, 256], replicated
- recurrent_updated: float32 [2, 288, 32], replicated
- recurrent_velocity: float32 [2, 288, 32], replicated
- recurrent_smoothed: float32 [2, 288, 32], replicated
- readout_updated: float32 [2, 32, 256], replicated
- readout_velocity: float32 [2, 32, 256], replicated
- readout_smoothed: float32 [2, 32, 256], replicated
- gains_updated: float32 [2, 3, 256], replicated
- gains_velocity: float32 [2, 3, 256], replicated
- gains_smoothed: float32 [2, 3, 256], replicated
- table_updated: float32 [2, 8, 225], replicated
- table_velocity: float32 [2, 8, 225], replicated
- table_smoothed: float32 [2, 8, 225], replicated
Inputs may be any that keep to these rules, and one draw needn't show every extreme that they name: Frames of even index are whole: crop_band is 0 and 32. For the others the first valid row is at most 8 and the end at least 24.
All inputs are finite; a program needn't handle non-finite values.
Results may differ from a plain program's by a relative error of at most 0.018.
Values may be sent and summed in bfloat16 or wider, within the bound.
A program may use at most 192 MiB of HBM per device.

v0:
```python
import jax
import jax.numpy as jnp
from jax import lax
from jax.sharding import PartitionSpec as P

WINDOW = 8


learn_rate = 0.2
momentum_rate = 0.9
average_decay = 0.5
norm_eps = 1e-05
mask_fill = -100.0
highest = lax.Precision.HIGHEST


def from_behind(array, axis, by):
    peers = lax.axis_size(axis)
    return lax.ppermute(array, axis, [(i, (i + by) % peers) for i in range(peers)])


def gelu_tanh(preact):
    return jax.nn.gelu(preact, approximate=True)


def gelu_back(preact, gradient):
    unused, pullback = jax.vjp(gelu_tanh, preact)
    return pullback(gradient)[0]


def norm_parts(stream):
    center = stream - jnp.mean(stream, axis=-1, keepdims=True)
    inverse = lax.rsqrt(jnp.mean(center * center, axis=-1, keepdims=True) + norm_eps)
    return (center * inverse, inverse)


def norm_back(upstream, gain_row, scaled, inverse):
    gain_grad = jnp.sum((upstream * scaled).reshape(-1, upstream.shape[-1]), axis=0)
    weighted = upstream * gain_row
    input_part = inverse * (
        weighted
        - jnp.mean(weighted, axis=-1, keepdims=True)
        - scaled * jnp.mean(weighted * scaled, axis=-1, keepdims=True)
    )
    return (gain_grad, input_part)


def token_outer(left, right):
    return lax.dot_general(
        left.reshape(-1, left.shape[-1]),
        right.reshape(-1, right.shape[-1]),
        (((0,), (0,)), ((), ())),
        preferred_element_type=jnp.float32,
    )


def windowize(tensor):
    frame_count, row_count, col_count, channels = tensor.shape
    tensor = tensor.reshape(
        frame_count, row_count // WINDOW, WINDOW, col_count // WINDOW, WINDOW, channels
    )
    return tensor.transpose(0, 1, 3, 2, 4, 5).reshape(-1, WINDOW * WINDOW, channels)


def unwindowize(tensor, frame_count, row_count, col_count):
    channels = tensor.shape[-1]
    tensor = tensor.reshape(
        frame_count, row_count // WINDOW, col_count // WINDOW, WINDOW, WINDOW, channels
    )
    return tensor.transpose(0, 1, 3, 2, 4, 5).reshape(frame_count, row_count, col_count, channels)


def offset_index():
    coords = jnp.arange(WINDOW * WINDOW, dtype=jnp.int32)
    row_of = coords // WINDOW
    col_of = coords % WINDOW
    return (
        (row_of[:, None] - row_of[None, :] + WINDOW - 1) * (2 * WINDOW - 1)
        + col_of[:, None]
        - col_of[None, :]
        + WINDOW
        - 1
    )


def pair_onehot():
    pair_count = (2 * WINDOW - 1) ** 2
    return (
        offset_index().reshape(-1)[:, None] == jnp.arange(pair_count, dtype=jnp.int32)[None, :]
    ).astype(jnp.float32)


def block_mask(crop_rows, shifted, frame_count, row_count, col_count):
    row_ids = jnp.arange(row_count, dtype=jnp.int32)
    half_window = WINDOW // 2
    if shifted:
        source = (row_ids + half_window) % row_count
        region = (row_ids >= row_count - WINDOW).astype(jnp.int32) + (
            row_ids >= row_count - half_window
        ).astype(jnp.int32)
    else:
        source = row_ids
        region = jnp.zeros_like(row_ids)
    in_crop = (
        (source[None, :] >= crop_rows[:, 0:1]) & (source[None, :] < crop_rows[:, 1:2])
    ).astype(jnp.int32)
    crop_grid = jnp.broadcast_to(in_crop[:, :, None, None], (frame_count, row_count, col_count, 1))
    region_grid = jnp.broadcast_to(
        region[None, :, None, None], (frame_count, row_count, col_count, 1)
    )
    crop_win = windowize(crop_grid)[:, :, 0]
    region_win = windowize(region_grid)[:, :, 0]
    allowed = (crop_win[:, None, :] > 0) & (region_win[:, :, None] == region_win[:, None, :])
    return jnp.where(allowed, 0.0, mask_fill).astype(jnp.float32)


def roll_ahead(tensor):
    half_window = WINDOW // 2
    tensor = jnp.roll(tensor, -half_window, axis=1)
    incoming = from_behind(tensor[:, :, :half_window], "lon", -1)
    return jnp.concatenate([tensor[:, :, half_window:], incoming], axis=2)


def roll_behind(tensor):
    half_window = WINDOW // 2
    tensor = jnp.roll(tensor, half_window, axis=1)
    incoming = from_behind(tensor[:, :, -half_window:], "lon", 1)
    return jnp.concatenate([incoming, tensor[:, :, :-half_window]], axis=2)


def grad_ahead(tensor):
    half_window = WINDOW // 2
    tensor = jnp.roll(tensor, -half_window, axis=1)
    incoming = from_behind(tensor[:, :, :half_window], "lon", -1)
    return jnp.concatenate([tensor[:, :, half_window:], incoming], axis=2)


def grad_behind(tensor):
    half_window = WINDOW // 2
    tensor = jnp.roll(tensor, half_window, axis=1)
    incoming = from_behind(tensor[:, :, -half_window:], "lon", 1)
    return jnp.concatenate([incoming, tensor[:, :, :-half_window]], axis=2)


def split_packed(packed, head_count):
    windows = windowize(packed)
    window_count, window_size, triple_width = windows.shape
    head_width = triple_width // (3 * head_count)
    split_heads = windows.reshape(window_count, window_size, 3, head_count, head_width)
    return (split_heads[:, :, 0], split_heads[:, :, 1], split_heads[:, :, 2])


def score_blocks(queries, key_heads, score_bias, score_mask):
    head_width = queries.shape[-1]
    scores = jnp.einsum(
        "wqhd,wkhd->whqk", queries, key_heads, preferred_element_type=jnp.float32
    ) * head_width ** (-0.5)
    return scores + score_bias[None] + score_mask[:, None]


def attend_forward(packed, score_bias, score_mask, head_count):
    queries, key_heads, value_heads = split_packed(packed, head_count)
    scores = score_blocks(queries, key_heads, score_bias, score_mask)
    row_max = jnp.max(scores, axis=-1, keepdims=True)
    exponent = jnp.exp(scores - row_max)
    row_total = jnp.sum(exponent, axis=-1, keepdims=True)
    attn_probs = (exponent / row_total).astype(jnp.bfloat16)
    logsum = row_max + jnp.log(row_total)
    context = jnp.einsum(
        "whqk,wkhd->wqhd", attn_probs, value_heads, preferred_element_type=jnp.float32
    )
    window_count, window_size = (context.shape[0], context.shape[1])
    return (context.astype(jnp.bfloat16).reshape(window_count, window_size, -1), logsum)


def attend_backward(packed, score_bias, score_mask, logsum, grad_windows, onehot):
    head_count = score_bias.shape[0]
    queries, key_heads, value_heads = split_packed(packed, head_count)
    window_count, window_size, head_width = (queries.shape[0], queries.shape[1], queries.shape[-1])
    scores = score_blocks(queries, key_heads, score_bias, score_mask)
    attn_probs = jnp.exp(scores - logsum)
    grad_heads = grad_windows.reshape(window_count, window_size, head_count, head_width)
    grad_values = jnp.einsum(
        "whqk,wqhd->wkhd",
        attn_probs.astype(jnp.bfloat16),
        grad_heads,
        preferred_element_type=jnp.float32,
    )
    grad_probs = jnp.einsum(
        "wqhd,wkhd->whqk", grad_heads, value_heads, preferred_element_type=jnp.float32
    )
    grad_scores = (
        attn_probs * (grad_probs - jnp.sum(grad_probs * attn_probs, axis=-1, keepdims=True))
    ).astype(jnp.bfloat16)
    summed = jnp.sum(grad_scores.astype(jnp.float32), axis=0).reshape(head_count, -1)
    table_grad = jnp.dot(summed, onehot, precision=highest)
    score_scale = head_width ** (-0.5)
    grad_queries = (
        jnp.einsum("whqk,wkhd->wqhd", grad_scores, key_heads, preferred_element_type=jnp.float32)
        * score_scale
    )
    grad_keys = (
        jnp.einsum("whqk,wqhd->wkhd", grad_scores, queries, preferred_element_type=jnp.float32)
        * score_scale
    )
    grad_packed = jnp.stack([grad_queries, grad_keys, grad_values], axis=2)
    return (grad_packed.reshape(window_count, window_size, -1).astype(jnp.bfloat16), table_grad)


def block_forward(stream, latent, weights, crop_rows, onehot, shifted):
    triple, output, expand, shrink, recurrent, readout, gain_rows, bias_table = weights
    frame_count, row_count, col_count, features = stream.shape
    head_count = bias_table.shape[0]
    window_size = WINDOW * WINDOW
    score_mask = block_mask(crop_rows, shifted, frame_count, row_count, col_count)
    score_bias = jnp.dot(bias_table, onehot.T, precision=highest).reshape(
        head_count, window_size, window_size
    )
    scaled_one, inverse_one = norm_parts(stream)
    normed = (scaled_one * gain_rows[0]).astype(jnp.bfloat16)
    if shifted:
        normed = roll_ahead(normed)
    packed = jnp.dot(normed, triple, preferred_element_type=jnp.float32).astype(jnp.bfloat16)
    context_win, logsum = attend_forward(packed, score_bias, score_mask, head_count)
    context = unwindowize(context_win, frame_count, row_count, col_count)
    if shifted:
        context = roll_behind(context)
    stream_one = stream + jnp.dot(context, output, preferred_element_type=jnp.float32)
    scaled_cell, inverse_cell = norm_parts(stream_one)
    cell_in = jnp.concatenate([(scaled_cell * gain_rows[2]).astype(jnp.bfloat16), latent], axis=-1)
    preact = jnp.dot(cell_in, recurrent, preferred_element_type=jnp.float32)
    tangent = jnp.tanh(preact)
    latent_new = tangent.astype(jnp.bfloat16)
    stream_two = stream_one + jnp.dot(latent_new, readout, preferred_element_type=jnp.float32)
    scaled_mlp, inverse_mlp = norm_parts(stream_two)
    hidden = (scaled_mlp * gain_rows[1]).astype(jnp.bfloat16)
    inner_pre = jnp.dot(hidden, expand, preferred_element_type=jnp.float32)
    activated = gelu_tanh(inner_pre).astype(jnp.bfloat16)
    stream_out = stream_two + jnp.dot(activated, shrink, preferred_element_type=jnp.float32)
    stored = dict(
        scaled_one=scaled_one,
        inverse_one=inverse_one,
        normed=normed,
        packed=packed,
        logsum=logsum,
        score_mask=score_mask,
        score_bias=score_bias,
        context=context,
        scaled_cell=scaled_cell,
        inverse_cell=inverse_cell,
        cell_in=cell_in,
        tangent=tangent,
        latent_new=latent_new,
        scaled_mlp=scaled_mlp,
        inverse_mlp=inverse_mlp,
        hidden=hidden,
        inner_pre=inner_pre,
        activated=activated,
    )
    return (stream_out, latent_new, stored)


def block_backward(grad_stream, grad_latent, stored, weights, onehot, shifted):
    triple, output, expand, shrink, recurrent, readout, gain_rows, bias_table = weights
    frame_count, row_count, col_count, features = grad_stream.shape
    grad_low = grad_stream.astype(jnp.bfloat16)
    shrink_grad = token_outer(stored["activated"], grad_low)
    grad_act = jnp.dot(grad_low, shrink.T, preferred_element_type=jnp.float32)
    grad_inner = gelu_back(stored["inner_pre"], grad_act).astype(jnp.bfloat16)
    expand_grad = token_outer(stored["hidden"], grad_inner)
    grad_hidden = jnp.dot(grad_inner, expand.T, preferred_element_type=jnp.float32)
    gain_mlp, grad_norm = norm_back(
        grad_hidden, gain_rows[1], stored["scaled_mlp"], stored["inverse_mlp"]
    )
    grad_stream = grad_stream + grad_norm
    grad_low = grad_stream.astype(jnp.bfloat16)
    readout_grad = token_outer(stored["latent_new"], grad_low)
    grad_state = jnp.dot(grad_low, readout.T, preferred_element_type=jnp.float32) + grad_latent
    tangent = stored["tangent"]
    grad_preact = (grad_state * (1.0 - tangent * tangent)).astype(jnp.bfloat16)
    recurrent_grad = token_outer(stored["cell_in"], grad_preact)
    grad_cell = jnp.dot(grad_preact, recurrent.T, preferred_element_type=jnp.float32)
    grad_prev = grad_cell[..., features:]
    gain_cell, grad_norm = norm_back(
        grad_cell[..., :features], gain_rows[2], stored["scaled_cell"], stored["inverse_cell"]
    )
    grad_stream = grad_stream + grad_norm
    grad_low = grad_stream.astype(jnp.bfloat16)
    output_grad = token_outer(stored["context"], grad_low)
    grad_context = jnp.dot(grad_low, output.T, preferred_element_type=jnp.float32).astype(
        jnp.bfloat16
    )
    if shifted:
        grad_context = grad_ahead(grad_context)
    grad_packed_win, table_grad = attend_backward(
        stored["packed"],
        stored["score_bias"],
        stored["score_mask"],
        stored["logsum"],
        windowize(grad_context),
        onehot,
    )
    grad_packed = unwindowize(grad_packed_win, frame_count, row_count, col_count)
    triple_grad = token_outer(stored["normed"], grad_packed)
    grad_normed = jnp.dot(grad_packed, triple.T, preferred_element_type=jnp.float32)
    if shifted:
        grad_normed = grad_behind(grad_normed.astype(jnp.bfloat16)).astype(jnp.float32)
    gain_attn, grad_norm = norm_back(
        grad_normed, gain_rows[0], stored["scaled_one"], stored["inverse_one"]
    )
    grad_stream = grad_stream + grad_norm
    gains_grad = jnp.stack([gain_attn, gain_mlp, gain_cell])
    return (
        grad_stream,
        grad_prev,
        (
            triple_grad,
            output_grad,
            expand_grad,
            shrink_grad,
            recurrent_grad,
            readout_grad,
            gains_grad,
            table_grad,
        ),
    )


def update(weight, moment, average, gradient):
    velocity = momentum_rate * moment + gradient
    updated = weight - learn_rate * (gradient + momentum_rate * velocity)
    smoothed = average_decay * average + (1.0 - average_decay) * updated
    return (updated, velocity, smoothed)


def per_device(
    frames,
    latent_init,
    crop_band,
    cotangent,
    triple_weight,
    triple_moment,
    triple_average,
    output_weight,
    output_moment,
    output_average,
    expand_weight,
    expand_moment,
    expand_average,
    shrink_weight,
    shrink_moment,
    shrink_average,
    recurrent_weight,
    recurrent_moment,
    recurrent_average,
    readout_weight,
    readout_moment,
    readout_average,
    gains_weight,
    gains_moment,
    gains_average,
    table_weight,
    table_moment,
    table_average,
):
    masters = (
        triple_weight,
        output_weight,
        expand_weight,
        shrink_weight,
        recurrent_weight,
        readout_weight,
    )
    lowered = tuple((master.astype(jnp.bfloat16) for master in masters)) + (
        gains_weight,
        table_weight,
    )
    frame_count, row_count, col_count, features = frames.shape
    layer_count = triple_weight.shape[0]
    onehot = pair_onehot()

    def run_layer(stream, latent, layer_index):
        weights = tuple((parameter[layer_index] for parameter in lowered))
        return block_forward(stream, latent, weights, crop_band, onehot, layer_index % 2 == 1)

    stream = frames.astype(jnp.float32)
    latent = latent_init
    layer_inputs = []
    kept_layers = []
    for layer_index in range(layer_count):
        layer_inputs.append((stream, latent))
        stream, latent, stored = run_layer(stream, latent, layer_index)
        kept_layers.append(stored)
    result = stream.astype(jnp.bfloat16)
    grad_stream = cotangent.astype(jnp.float32)
    grad_latent = jnp.zeros(latent_init.shape, jnp.float32)
    layer_grads = [None] * layer_count
    for layer_index in reversed(range(layer_count)):
        unused_stream, unused_latent, stored = run_layer(
            layer_inputs[layer_index][0], layer_inputs[layer_index][1], layer_index
        )
        weights = tuple((parameter[layer_index] for parameter in lowered))
        grad_stream, grad_latent, grads = block_backward(
            grad_stream, grad_latent, stored, weights, onehot, layer_index % 2 == 1
        )
        layer_grads[layer_index] = grads
    triple_sum = jnp.stack([layer_grads[index_layer][0] for index_layer in range(layer_count)])
    output_sum = jnp.stack([layer_grads[index_layer][1] for index_layer in range(layer_count)])
    expand_sum = jnp.stack([layer_grads[index_layer][2] for index_layer in range(layer_count)])
    shrink_sum = jnp.stack([layer_grads[index_layer][3] for index_layer in range(layer_count)])
    recurrent_sum = jnp.stack([layer_grads[index_layer][4] for index_layer in range(layer_count)])
    readout_sum = jnp.stack([layer_grads[index_layer][5] for index_layer in range(layer_count)])
    gains_sum = jnp.stack([layer_grads[index_layer][6] for index_layer in range(layer_count)])
    table_sum = jnp.stack([layer_grads[index_layer][7] for index_layer in range(layer_count)])
    (
        triple_sum,
        output_sum,
        expand_sum,
        shrink_sum,
        recurrent_sum,
        readout_sum,
        gains_sum,
        table_sum,
    ) = lax.psum(
        (
            triple_sum,
            output_sum,
            expand_sum,
            shrink_sum,
            recurrent_sum,
            readout_sum,
            gains_sum,
            table_sum,
        ),
        ("lon", "batch"),
    )
    scale_factor = float(
        frame_count * row_count * col_count * lax.axis_size("lon") * lax.axis_size("batch")
    ) ** (-0.5)
    triple_updated, triple_velocity, triple_smoothed = update(
        triple_weight, triple_moment, triple_average, triple_sum * scale_factor
    )
    output_updated, output_velocity, output_smoothed = update(
        output_weight, output_moment, output_average, output_sum * scale_factor
    )
    expand_updated, expand_velocity, expand_smoothed = update(
        expand_weight, expand_moment, expand_average, expand_sum * scale_factor
    )
    shrink_updated, shrink_velocity, shrink_smoothed = update(
        shrink_weight, shrink_moment, shrink_average, shrink_sum * scale_factor
    )
    recurrent_updated, recurrent_velocity, recurrent_smoothed = update(
        recurrent_weight, recurrent_moment, recurrent_average, recurrent_sum * scale_factor
    )
    readout_updated, readout_velocity, readout_smoothed = update(
        readout_weight, readout_moment, readout_average, readout_sum * scale_factor
    )
    gains_updated, gains_velocity, gains_smoothed = update(
        gains_weight, gains_moment, gains_average, gains_sum * scale_factor
    )
    table_updated, table_velocity, table_smoothed = update(
        table_weight, table_moment, table_average, table_sum * scale_factor
    )
    return (
        result,
        grad_stream,
        triple_updated,
        triple_velocity,
        triple_smoothed,
        output_updated,
        output_velocity,
        output_smoothed,
        expand_updated,
        expand_velocity,
        expand_smoothed,
        shrink_updated,
        shrink_velocity,
        shrink_smoothed,
        recurrent_updated,
        recurrent_velocity,
        recurrent_smoothed,
        readout_updated,
        readout_velocity,
        readout_smoothed,
        gains_updated,
        gains_velocity,
        gains_smoothed,
        table_updated,
        table_velocity,
        table_smoothed,
    )


def solution(mesh):
    placed = (
        P("batch", None, "lon", None),
        P("batch", None, "lon", None),
        P("batch", None),
        P("batch", None, "lon", None),
        P(),
        P(),
        P(),
        P(),
        P(),
        P(),
        P(),
        P(),
        P(),
        P(),
        P(),
        P(),
        P(),
        P(),
        P(),
        P(),
        P(),
        P(),
        P(),
        P(),
        P(),
        P(),
        P(),
        P(),
    )
    return jax.shard_map(
        per_device,
        mesh=mesh,
        in_specs=placed,
        out_specs=(
            P("batch", None, "lon", None),
            P("batch", None, "lon", None),
            P(),
            P(),
            P(),
            P(),
            P(),
            P(),
            P(),
            P(),
            P(),
            P(),
            P(),
            P(),
            P(),
            P(),
            P(),
            P(),
            P(),
            P(),
            P(),
            P(),
            P(),
            P(),
            P(),
            P(),
        ),
        check_vma=False,
    )
```

profile of v0, /device:TPU:0, one launch (start us, length us, event | category | flops | bytes accessed | tf_op | source)
XLA Modules:
  0.0 445.2 jit_solution(10139392635881953113)
XLA Ops:
  15.7 2.7 convolution_bitcast_fusion.1
  25.0 5.5 %reshape_reshape_transpose_reshape.8 = bf16[16,64,3,8,32]{4,3,2,1,0:T(8,128)(2,1)} reshape(bf16[4,32,8,768]{3,2,1,0:T(8,128)(2,1)S(1)} %convolution_convert_fusion.1) | data formatting | bytes 3145728 | tf_op jit(solution)/shard_map/reshape;reshape;transpose;reshape | solution.py:149
  30.5 5.5 %fusion.138 = (bf16[16,64,1,8,32]{4,3,2,1,0:T(8,128)(2,1)S(1)}, bf16[16,64,1,8,32]{4,3,2,1,0:T(8,128)(2,1)}, bf16[16,64,1,8,32]{4,3,2,1,0:T(8,128)(2,1)}) fusion(bf16[16,64,3,8,32]{4,3,2,1,0:T(8,128)(2,1)} %reshape_reshape_transpose_reshape.8), kind=kLoop, calls=%fused_computation.324 | loop fusion | bytes 3145728 | tf_op jit(solution)/shard_map/slice | solution.py:150
  52.2 14.1 %reshape_transpose_reshape_reshape.8 = bf16[4,32,8,256]{3,2,1,0:T(8,128)(2,1)} reshape(bf16[16,64,8,32]{3,2,1,0:T(8,128)(2,1)S(1)} %copy.185) | data formatting | bytes 1048576 | tf_op jit(solution)/shard_map/reshape;transpose;reshape;reshape | solution.py:70
  76.5 3.9 collective-permute-start
  81.0 2.8 convolution_bitcast_fusion
  94.9 5.5 %reshape_reshape_transpose_reshape.9 = bf16[16,64,3,8,32]{4,3,2,1,0:T(8,128)(2,1)} reshape(bf16[4,32,8,768]{3,2,1,0:T(8,128)(2,1)S(1)} %convolution_convert_fusion) | data formatting | bytes 3145728 | tf_op jit(solution)/shard_map/reshape;reshape;transpose;reshape | solution.py:149
  100.4 5.5 %fusion.137 = (bf16[16,64,1,8,32]{4,3,2,1,0:T(8,128)(2,1)S(1)}, bf16[16,64,1,8,32]{4,3,2,1,0:T(8,128)(2,1)}, bf16[16,64,1,8,32]{4,3,2,1,0:T(8,128)(2,1)}) fusion(bf16[16,64,3,8,32]{4,3,2,1,0:T(8,128)(2,1)} %reshape_reshape_transpose_reshape.9), kind=kLoop, calls=%fused_computation.323 | loop fusion | bytes 3145728 | tf_op jit(solution)/shard_map/slice | solution.py:150
  119.1 3.0 copy.191
  122.1 3.8 reshape_transpose_reshape_reshape.9
  132.1 5.1 %collective-permute-done.1 = bf16[4,32,4,256]{3,2,1,0:T(4,128)(2,1)S(1)} collective-permute-done((bf16[4,32,4,256]{3,2,1,0:T(4,128)(2,1)S(1)}, bf16[4,32,4,256]{3,2,1,0:T(4,128)(2,1)S(1)}, u32[]{:S(2)}, u32[]{:S(2)}) %collective-permute-start.1) | collective-permute-done | bytes 262176 | tf_op jit(solution)/shard_map/ppermute | solution.py:19
  143.4 3.2 fusion.13
  156.8 3.8 collective-permute-done.2
  165.1 3.5 fusion.45
  174.9 5.2 %copy.197 = bf16[16,64,3,8,32]{4,3,2,1,0:T(8,128)(2,1)} copy(bf16[16,64,3,8,32]{1,4,3,0,2:T(8,128)(2,1)S(1)} %pad_maximum_fusion) | data formatting | bytes 3145728 | tf_op jit(solution)/shard_map/stack | solution.py:206
  180.2 8.2 %convert_element_type.268 = bf16[4,32,8,768]{3,2,1,0:T(8,128)(2,1)} reshape(bf16[16,64,3,8,32]{4,3,2,1,0:T(8,128)(2,1)} %copy.197) | data formatting | bytes 3145728 | tf_op jit(solution)/shard_map/convert_element_type | solution.py:207
  193.8 3.7 copy.205
  197.5 4.8 %convert_element_type.281 = bf16[1024,768]{0,1:T(8,128)(2,1)S(1)} reshape(bf16[16,64,3,8,32]{1,0,4,3,2:T(8,128)(2,1)} %copy.205) | data formatting | bytes 3145728 | tf_op jit(solution)/shard_map/convert_element_type | solution.py:207
  208.5 3.2 fusion.6
  225.9 3.5 fusion.42
  236.7 3.7 copy.204
  240.4 5.5 %convert_element_type.280 = bf16[1024,768]{0,1:T(8,128)(2,1)} reshape(bf16[16,64,3,8,32]{1,0,4,3,2:T(8,128)(2,1)} %copy.204) | data formatting | bytes 3145728 | tf_op jit(solution)/shard_map/convert_element_type | solution.py:207
  245.9 3.1 pad_maximum_fusion.3
  255.0 4.9 %fusion.55 = bf16[4,32,8,256]{3,2,1,0:T(8,128)(2,1)} fusion(f32[4,32,8,256]{3,2,1,0:T(8,128)} %copy-done.10, bf16[2,1024,256]{2,1,0:T(8,128)(2,1)} %convert_element_type.246, f32[4,32,8,1024]{3,2,1,0:T(8,128)} %copy-done.38), kind=kOutput, calls=%fused_computation.104 | convolution fusion | flops 546832384 | bytes 6291456 | tf_op jit(solution)/shard_map/dot_general | solution.py:239
  263.8 5.2 %copy.203 = bf16[16,64,3,8,32]{4,3,2,1,0:T(8,128)(2,1)} copy(bf16[16,64,3,8,32]{1,4,3,0,2:T(8,128)(2,1)S(1)} %pad_maximum_fusion.1) | data formatting | bytes 3145728 | tf_op jit(solution)/shard_map/stack | solution.py:206
  270.0 8.4 %convert_element_type.279 = bf16[4,32,8,768]{3,2,1,0:T(8,128)(2,1)} reshape(bf16[16,64,3,8,32]{4,3,2,1,0:T(8,128)(2,1)} %copy.203) | data formatting | bytes 3145728 | tf_op jit(solution)/shard_map/convert_element_type | solution.py:207
  278.5 3.8 fusion.72
  283.8 41.2 %all-reduce = (f32[2,3,256]{2,1,0:T(4,128)S(1)}, f32[2,8,225]{2,1,0:T(8,128)S(1)}) all-reduce(f32[2,3,256]{2,1,0:T(4,128)S(1)} %pad_maximum_fusion.17, f32[2,8,225]{2,1,0:T(8,128)S(1)} %pad_maximum_fusion.16), channel_id=1, replica_groups=mesh['lon'=4,'batch'=8] {'lon','batch'}, use_global_device_ids=true, to_apply=%region_42.43 | all-reduce | flops 5136 | bytes 41088 | tf_op jit(solution)/shard_map/psum | solution.py:424
  333.2 84.3 %all-reduce.4.cloned.1.call-done = (f32[2,256,768]{2,1,0:T(8,128)}, f32[2,256,256]{2,1,0:T(8,128)}, f32[2,256,1024]{2,1,0:T(8,128)}, f32[2,1024,256]{2,1,0:T(8,1...) async-done(((f32[2,256,768]{2,1,0:T(8,128)}, f32[2,256,256]{2,1,0:T(8,128)}, f32[2,256,1024]{2,1,0:T(8,128)}, f32[2,1024,256]{2,1,0:T(8,128)}, f32[2,288,32]{1,2,0:T(8,128)}, ...) | async-done | bytes 6430736 | tf_op jit(solution)/shard_map/psum | solution.py:424
  423.5 4.5 %add_multiply_fusion.2 = (f32[2,256,768]{2,1,0:T(8,128)}, f32[2,256,768]{2,1,0:T(8,128)}, f32[2,256,768]{2,1,0:T(8,128)}) fusion(f32[2,256,768]{2,1,0:T(8,128)S(1)} %copy-done.68, f32[2,256,768]{2,1,0:T(8,128)S(1)} %copy-done.27, f32[2,256,768]{2,1,0:T(8,128)} %get-tuple-element.124, f32[2,256,768]{2,1,0:T(8,128)S(1)} %copy-done.69), kind=kLoop, calls=%fused_computation.70 | loop fusion | flops 3538944 | bytes 11010048 | tf_op jit(solution)/shard_map/add | solution.py:332
  429.2 4.4 add_multiply_fusion.1
  434.8 3.3 add_multiply_fusion
  (439 shorter events, 160.0 us)
Async XLA Ops:
  7.2 12.2 %copy-start.62 = (f32[2,256,256]{2,1,0:T(8,128)S(1)}, f32[2,256,256]{2,1,0:T(8,128)}, u32[]{:S(2)}) copy-start(f32[2,256,256]{2,1,0:T(8,128)} %param.35) | copy-start | bytes 1572868
  7.2 410.2 %all-reduce.4.cloned.1.call-start = ((), (), s32[]{:S(2)}) async-start(), calls=%async_computation | async-start | bytes 12910592 | tf_op jit(solution)/shard_map/psum | solution.py:424
  8.0 7.6 %copy-start.125 = (s32[4]{0:T(128)}, s32[4]{0:T(128)S(1)}, u32[]{:S(2)}) copy-start(s32[4]{0:T(128)S(1)} %get-tuple-element.176) | copy-start | bytes 52
  8.0 7.6 %copy-start.127 = (s32[4]{0:T(128)}, s32[4]{0:T(128)S(1)}, u32[]{:S(2)}) copy-start(s32[4]{0:T(128)S(1)} %get-tuple-element.177) | copy-start | bytes 52
  14.1 9.8 %copy-start.77 = (f32[4,32,8]{2,1,0:T(8,128)}, f32[4,32,8]{2,1,0:T(8,128)S(1)}, u32[]{:S(2)}) copy-start(f32[4,32,8]{2,1,0:T(8,128)S(1)} %broadcast_multiply_fusion.17) | copy-start | bytes 12292
  15.7 8.2 %copy-start.94 = (f32[4,32,8]{2,1,0:T(8,128)}, f32[4,32,8]{2,1,0:T(8,128)S(1)}, u32[]{:S(2)}) copy-start(f32[4,32,8]{2,1,0:T(8,128)S(1)} %add_rsqrt_fusion.5) | copy-start | bytes 12292
  21.6 71.6 %copy-start.28 = (bf16[2,256,768]{2,1,0:T(8,128)(2,1)}, bf16[2,256,768]{2,1,0:T(8,128)(2,1)S(1)}, u32[]{:S(2)}) copy-start(bf16[2,256,768]{2,1,0:T(8,128)(2,1)S(1)} %convert_element_type.232) | copy-start | bytes 2359300
  52.2 16.7 %copy-start.117 = (f32[1,1,256]{2,0,1:T(1,128)S(1)}, f32[1,1,256]{2,0,1:T(1,128)}, u32[]{:S(2)}) copy-start(f32[1,1,256]{2,0,1:T(1,128)} %get-tuple-element.174) | copy-start | bytes 3076
  74.6 62.6 %copy-start.6 = (f32[4,32,8,256]{3,2,1,0:T(8,128)}, f32[4,32,8,256]{3,2,1,0:T(8,128)S(1)}, u32[]{:S(2)}) copy-start(f32[4,32,8,256]{3,2,1,0:T(8,128)S(1)} %get-tuple-element.187) | copy-start | bytes 3145732
  74.7 9.2 %copy-start.90 = (f32[16,8,64]{2,1,0:T(8,128)S(1)}, f32[16,8,64]{2,1,0:T(8,128)}, u32[]{:S(2)}) copy-start(f32[16,8,64]{2,1,0:T(8,128)} %copy-done.89) | copy-start | bytes 98308
  74.7 9.2 %copy-start.104 = (f32[16,8,64]{2,1,0:T(8,128)S(1)}, f32[16,8,64]{2,1,0:T(8,128)}, u32[]{:S(2)}) copy-start(f32[16,8,64]{2,1,0:T(8,128)} %copy-done.103) | copy-start | bytes 98308
  75.1 10.4 %copy-start.126 = (s32[4]{0:T(128)S(1)}, s32[4]{0:T(128)}, u32[]{:S(2)}) copy-start(s32[4]{0:T(128)} %copy-done.125) | copy-start | bytes 52
  75.1 10.4 %copy-start.128 = (s32[4]{0:T(128)S(1)}, s32[4]{0:T(128)}, u32[]{:S(2)}) copy-start(s32[4]{0:T(128)} %copy-done.127) | copy-start | bytes 52
  75.1 10.5 %copy-start.37 = (bf16[16,64,8,32]{1,3,2,0:T(8,128)(2,1)S(1)}, bf16[16,64,8,32]{1,3,2,0:T(8,128)(2,1)}, u32[]{:S(2)}) copy-start(bf16[16,64,8,32]{1,3,2,0:T(8,128)(2,1)} %fusion.40) | copy-start | bytes 1572868
  76.5 16.7 %collective-permute-start = (bf16[4,32,4,256]{3,2,1,0:T(4,128)(2,1)}, bf16[4,32,4,256]{3,2,1,0:T(4,128)(2,1)}, u32[]{:S(2)}, u32[]{:S(2)}) collective-permute-start(bf16[4,32,4,256]{3,2,1,0:T(4,128)(2,1)} %get-tuple-element.168), channel_id=1, source_target_pairs={{0,24},{8,0},{16,8},{24,16},{1,25},{9,1},{17,9},{25,17},{2,26},{10... | collective-permute-start | bytes 786440 | tf_op jit(solution)/shard_map/ppermute | solution.py:19
  119.1 9.5 %copy-start.55 = (bf16[4,32,4,256]{3,2,1,0:T(4,128)(2,1)S(1)}, bf16[4,32,4,256]{3,2,1,0:T(4,128)(2,1)}, u32[]{:S(2)}) copy-start(bf16[4,32,4,256]{3,2,1,0:T(4,128)(2,1)} %get-tuple-element.167) | copy-start | bytes 786436
  125.9 11.3 %copy-start.51 = (bf16[2,256,256]{2,1,0:T(8,128)(2,1)S(1)}, bf16[2,256,256]{2,1,0:T(8,128)(2,1)}, u32[]{:S(2)}) copy-start(bf16[2,256,256]{2,1,0:T(8,128)(2,1)} %convert_element_type.238) | copy-start | bytes 786436
  128.1 9.1 %collective-permute-start.1 = (bf16[4,32,4,256]{3,2,1,0:T(4,128)(2,1)S(1)}, bf16[4,32,4,256]{3,2,1,0:T(4,128)(2,1)S(1)}, u32[]{:S(2)}, u32[]{:S(2)}) collective-permute-start(bf16[4,32,4,256]{3,2,1,0:T(4,128)(2,1)S(1)} %fusion.105), channel_id=1, source_target_pairs={{0,8},{8,16},{16,24},{24,0},{1,9},{9,17},{17,25},{25,1},{2,10},{10... | collective-permute-start | bytes 786440 | tf_op jit(solution)/shard_map/ppermute | solution.py:19
  139.2 10.9 %copy-start.10 = (f32[4,32,8,256]{3,2,1,0:T(8,128)}, f32[4,32,8,256]{3,2,1,0:T(8,128)S(1)}, u32[]{:S(2)}) copy-start(f32[4,32,8,256]{3,2,1,0:T(8,128)S(1)} %get-tuple-element.193) | copy-start | bytes 3145732
  153.6 7.1 %collective-permute-start.2 = (bf16[4,32,4,256]{3,2,1,0:T(4,128)(2,1)S(1)}, bf16[4,32,4,256]{3,2,1,0:T(4,128)(2,1)S(1)}, u32[]{:S(2)}, u32[]{:S(2)}) collective-permute-start(bf16[4,32,4,256]{3,2,1,0:T(4,128)(2,1)S(1)} %get-tuple-element.166), channel_id=1, source_target_pairs={{0,24},{8,0},{16,8},{24,16},{1,25},{9,1},{17,9},{25,17},{2,26},{10... | collective-permute-start | bytes 786440 | tf_op jit(solution)/shard_map/ppermute | solution.py:19
  192.3 12.6 %collective-permute-start.3 = (bf16[4,32,4,256]{3,2,1,0:T(4,128)(2,1)}, bf16[4,32,4,256]{3,2,1,0:T(4,128)(2,1)}, u32[]{:S(2)}, u32[]{:S(2)}) collective-permute-start(bf16[4,32,4,256]{3,2,1,0:T(4,128)(2,1)} %fusion.103), channel_id=1, source_target_pairs={{0,8},{8,16},{16,24},{24,0},{1,9},{9,17},{17,25},{25,1},{2,10},{10... | collective-permute-start | bytes 786440 | tf_op jit(solution)/shard_map/ppermute | solution.py:19
  270.0 8.4 %copy-start.129 = (f32[256]{0:T(256)S(1)}, f32[256]{0:T(256)}, u32[]{:S(2)}) copy-start(f32[256]{0:T(256)} %get-tuple-element.110) | copy-start | bytes 3076
  270.0 8.5 %copy-start.12 = (bf16[4,32,8,256]{3,2,1,0:T(8,128)(2,1)S(1)}, bf16[4,32,8,256]{3,2,1,0:T(8,128)(2,1)}, u32[]{:S(2)}) copy-start(bf16[4,32,8,256]{3,2,1,0:T(8,128)(2,1)} %param.28) | copy-start | bytes 1572868
  270.0 8.5 %copy-start.29 = (bf16[2,256,768]{2,1,0:T(8,128)(2,1)S(1)}, bf16[2,256,768]{2,1,0:T(8,128)(2,1)}, u32[]{:S(2)}) copy-start(bf16[2,256,768]{2,1,0:T(8,128)(2,1)} %copy-done.28) | copy-start | bytes 2359300
  270.0 8.5 %copy-start.78 = (f32[4,32,8]{2,1,0:T(8,128)S(1)}, f32[4,32,8]{2,1,0:T(8,128)}, u32[]{:S(2)}) copy-start(f32[4,32,8]{2,1,0:T(8,128)} %copy-done.77) | copy-start | bytes 12292
  270.0 8.5 %copy-start.95 = (f32[4,32,8]{2,1,0:T(8,128)S(1)}, f32[4,32,8]{2,1,0:T(8,128)}, u32[]{:S(2)}) copy-start(f32[4,32,8]{2,1,0:T(8,128)} %copy-done.94) | copy-start | bytes 12292
  270.0 8.5 %copy-start.123 = (f32[1,1,256]{2,0,1:T(1,128)S(1)}, f32[1,1,256]{2,0,1:T(1,128)}, u32[]{:S(2)}) copy-start(f32[1,1,256]{2,0,1:T(1,128)} %get-tuple-element.175) | copy-start | bytes 3076
  278.5 46.6 %copy-start.111 = (f32[2,3,256]{2,0,1:T(2,128)S(1)}, f32[2,3,256]{2,0,1:T(2,128)}, u32[]{:S(2)}) copy-start(f32[2,3,256]{2,0,1:T(2,128)} %param.50) | copy-start | bytes 18436
  278.5 52.1 %copy-start.41 = (f32[4,32,8,256]{3,2,1,0:T(8,128)S(1)}, f32[4,32,8,256]{3,2,1,0:T(8,128)}, u32[]{:S(2)}) copy-start(f32[4,32,8,256]{3,2,1,0:T(8,128)} %get-tuple-element.158) | copy-start | bytes 3145732
  282.4 138.6 %copy-start.63 = (f32[2,256,256]{2,1,0:T(8,128)S(1)}, f32[2,256,256]{2,1,0:T(8,128)}, u32[]{:S(2)}) copy-start(f32[2,256,256]{2,1,0:T(8,128)} %param.35) | copy-start | bytes 1572868
  282.4 138.6 %copy-start.97 = (f32[2,256,256]{2,1,0:T(8,128)S(1)}, f32[2,256,256]{2,1,0:T(8,128)}, u32[]{:S(2)}) copy-start(f32[2,256,256]{2,1,0:T(8,128)} %param.37) | copy-start | bytes 1572868
  333.2 90.3 %copy-start.27 = (f32[2,256,768]{2,1,0:T(8,128)S(1)}, f32[2,256,768]{2,1,0:T(8,128)}, u32[]{:S(2)}) copy-start(f32[2,256,768]{2,1,0:T(8,128)} %param.32) | copy-start | bytes 4718596
  (103 other events, 336.0 us)
Sparse Core Ops, SparseCore 0:
  255.1 162.3 all-reduce.3
where the time goes:
time: 450 us; the launch traced here: 445 us
  local copies, waits for them, and re-layouts  137 us (30%)
  waiting for transfers between devices  93.2 us (21%)
  matrix products  79.9 us (18%)
  other arithmetic  72.6 us (16%)
  blocking collectives  41.2 us (9%)
  between operations  16.1 us (4%)
  starting transfers between devices  5.23 us (1%)
    psum x1, waiting for transfers between devices, per_device(): lax.psum((triple_sum, output_sum, expand_sum, shrink_sum, recurrent_sum,...  84.3 us
    psum x1, blocking collectives, per_device(): lax.psum((triple_sum, output_sum, expand_sum, shrink_sum, recurrent_sum,...  41.2 us
    convert_element_type x4, local copies, waits for them, and re-layouts, attend_backward(): grad_packed.reshape(window_count, window_size, -1).astype(jnp.bfloat16)  26.9 us
    unnamed x269, local copies, waits for them, and re-layouts  25.4 us
    add x8, other arithmetic, update(): smoothed = average_decay * average + (1.0 - average_decay) * updated  20.4 us
    another operation x2, local copies, waits for them, and re-layouts, unwindowize(): tensor.transpose(0, 1, 3, 2, 4, 5)  17.9 us
    another operation x4, local copies, waits for them, and re-layouts, attend_backward(): grad_packed = jnp.stack([grad_queries, grad_keys, grad_values], axis=2)  17.8 us
    dot_general x12, matrix products, token_outer(): lax.dot_general(left.reshape(-1, left.shape[-1]), right.reshape(-1, right...  16.4 us
  transfers between devices with their start and end apart: 5, of which 3 were waited for; matrix products, arithmetic and copies ran while one was open for 15% of the time, Pallas kernels for 0%

commit v1 on v0

v1 whole, which is shorter than its diff:
```python
import functools

import jax
import jax.numpy as jnp
from jax import lax
from jax.experimental import pallas as pl
from jax.experimental.pallas import tpu as pltpu
from jax.sharding import PartitionSpec as P

WINDOW = 8
HALF = WINDOW // 2
SPAN = WINDOW * WINDOW
HEADS = 8
LANES = 128
LAYERS = 2
WIDTH = 256
HIDDEN = 1024
LATENT = 32
OFFSETS = 2 * WINDOW - 1
PAIRS = OFFSETS * OFFSETS

LEARN_RATE = 0.2
MOMENTUM_RATE = 0.9
AVERAGE_DECAY = 0.5
NORM_EPS = 1e-05
MASK_FILL = -100.0
HEAD_WIDTH = WIDTH // HEADS
HEADS_A_HALF = LANES // HEAD_WIDTH
SCALE = HEAD_WIDTH ** (-0.5)
GELU_C = 0.7978845608028654
GELU_A = 0.044715

F32 = jnp.float32
BF16 = jnp.bfloat16
MESH = pl.DeviceIdType.MESH

SMALL_ROWS = 256
SHRINK_AT, EXPAND_AT, OUTPUT_AT, TRIPLE_AT, SMALL_AT, GRAD_ROWS = (
    (4096 + 2048, 0),
    (4096 + 2048 + 2048, 2048),
    (4096 + 2048 + 4096, 4096),
    (4096 + 2048 + 4096 + 512, 4096 + 512),
    (4096 + 2048 + 4096 + 2048, 4096 + 2048 + 4096 + 2048 + SMALL_ROWS),
    4096 + 2048 + 4096 + 2048 + 2 * SMALL_ROWS,
)


def dot(a, b):
    return jnp.dot(a, b, preferred_element_type=F32)


def dot_nt(a, b):
    return lax.dot_general(a, b, (((1,), (1,)), ((), ())), preferred_element_type=F32)


def dot_tn(a, b):
    return lax.dot_general(a, b, (((0,), (0,)), ((), ())), preferred_element_type=F32)


def norm_parts(stream):
    center = stream - jnp.mean(stream, axis=-1, keepdims=True)
    inverse = lax.rsqrt(jnp.mean(center * center, axis=-1, keepdims=True) + NORM_EPS)
    return center * inverse, inverse


def norm_back(upstream, gain_row, scaled, inverse):
    product = upstream * scaled
    rows, features = product.shape
    gain_part = jnp.sum(product.reshape(rows // 8, 8, features), axis=0)
    weighted = upstream * gain_row
    along = jnp.mean(product * gain_row, axis=-1, keepdims=True)
    inner = weighted - jnp.mean(weighted, axis=-1, keepdims=True) - scaled * along
    return gain_part, inverse * inner


def lower_slots(shape):
    return lax.broadcasted_iota(jnp.int32, shape, 1) < HALF


def pack_half(own):
    tokens, features = own.shape
    rows = own.reshape(tokens // WINDOW, WINDOW, features)
    count = tokens // WINDOW // 2
    moved = pltpu.roll(rows[count:], HALF, axis=1)
    return jnp.where(lower_slots(moved.shape), rows[:count], moved).reshape(tokens // 2, features)


def unpack_half(packed, own):
    tokens, features = own.shape
    pairs = packed.reshape(tokens // WINDOW // 2, WINDOW, features)
    full = jnp.concatenate([pairs, pltpu.roll(pairs, HALF, axis=1)], axis=0)
    rows = own.reshape(tokens // WINDOW, WINDOW, features)
    return jnp.where(lower_slots(full.shape), full, rows).reshape(tokens, features)


def rows_ahead(value):
    cut = HALF * WINDOW
    return jnp.concatenate([value[cut:], value[:cut]], axis=0)


def rows_behind(value):
    cut = value.shape[0] - HALF * WINDOW
    return jnp.concatenate([value[cut:], value[:cut]], axis=0)


def head_of_lane(shape):
    return lax.broadcasted_iota(jnp.int32, shape, 1) // HEAD_WIDTH


def spread_heads(block):
    lane_head = head_of_lane(block.shape)
    zero = jnp.zeros_like(block)
    return jnp.concatenate(
        [jnp.where(lane_head == head, block, zero) for head in range(HEADS_A_HALF)], axis=0
    )


def gather_heads(stacked):
    count = stacked.shape[0] // HEADS_A_HALF
    lane_head = head_of_lane((count, LANES))
    out = stacked[:count]
    for head in range(1, HEADS_A_HALF):
        out = jnp.where(lane_head == head, stacked[head * count : (head + 1) * count], out)
    return out


def half_lanes(half):
    return slice(half * LANES, (half + 1) * LANES)


def half_scores(half):
    return slice(half * HEADS_A_HALF * SPAN, (half + 1) * HEADS_A_HALF * SPAN)


def score_mask(crop_start, crop_end, shifted, window, row_count):
    shape = (SPAN, HEADS_A_HALF * SPAN)
    key_row = lax.broadcasted_iota(jnp.int32, shape, 0) // WINDOW
    source = key_row + window * WINDOW
    if shifted:
        source = source + HALF
        if window == row_count // WINDOW - 1:
            source = jnp.where(source >= row_count, source - row_count, source)
    allowed = (source >= crop_start) & (source < crop_end)
    if shifted and window == row_count // WINDOW - 1:
        query_row = lax.broadcasted_iota(jnp.int32, shape, 1) % SPAN // WINDOW
        allowed = allowed & ((key_row < HALF) == (query_row < HALF))
    return jnp.where(allowed, 0.0, MASK_FILL).astype(F32)


def offset_onehot(shifted):
    shape = (WIDTH, WINDOW * LANES)
    lane = lax.broadcasted_iota(jnp.int32, shape, 1)
    key_col = lane // LANES
    row_offset = lane % LANES // WINDOW
    query_col = lane % WINDOW
    if shifted:
        key_col = (key_col + HALF) % WINDOW
        query_col = (query_col + HALF) % WINDOW
    target = row_offset * OFFSETS + query_col - key_col + WINDOW - 1
    target = jnp.where(row_offset < OFFSETS, target, -1)
    pair = lax.broadcasted_iota(jnp.int32, shape, 0)
    return jnp.where(pair == target, 1.0, 0.0).astype(BF16)


def three_parts(value):
    high = value.astype(BF16)
    rest = value - high.astype(F32)
    middle = rest.astype(BF16)
    low = (rest - middle.astype(F32)).astype(BF16)
    return jnp.concatenate([high.astype(F32), middle.astype(F32), low.astype(F32)], axis=0).astype(BF16)


def swap_groups(tiles):
    return [jnp.concatenate([tile[b : b + 1] for tile in tiles], axis=0) for b in range(8)]


def bias_of_table(table, onehot):
    spread = dot(three_parts(table), onehot)
    spread = spread[:HEADS] + (spread[HEADS : 2 * HEADS] + spread[2 * HEADS :])
    tiles = swap_groups([spread[:, col * LANES : (col + 1) * LANES] for col in range(WINDOW)])
    lane = lax.broadcasted_iota(jnp.int32, (WINDOW, LANES), 1)
    blocks = []
    for key_row in range(WINDOW):
        back = (WINDOW - 1 - key_row) * WINDOW
        pieces = []
        for pair in range(HEADS // 2):
            even = pltpu.roll(tiles[2 * pair], (LANES - back) % LANES, axis=1)
            odd = pltpu.roll(tiles[2 * pair + 1], (LANES + SPAN - back) % LANES, axis=1)
            pieces.append(jnp.where(lane < SPAN, even, odd))
        blocks.append(jnp.concatenate(pieces, axis=1))
    return jnp.concatenate(blocks, axis=0)


def table_of_bias(gathered, onehot):
    lane = lax.broadcasted_iota(jnp.int32, (WINDOW, LANES), 1)
    zero = jnp.zeros((WINDOW, LANES), F32)
    tiles = []
    for head in range(HEADS):
        total = None
        for key_row in range(WINDOW):
            forth = (WINDOW - 1 - key_row) * WINDOW
            block = gathered[key_row * WINDOW : (key_row + 1) * WINDOW, half_lanes(head // 2)]
            if head % 2 == 0:
                moved = pltpu.roll(jnp.where(lane < SPAN, block, zero), forth, axis=1)
            else:
                moved = pltpu.roll(jnp.where(lane < SPAN, zero, block), (forth + SPAN) % LANES, axis=1)
            total = moved if total is None else total + moved
        tiles.append(total)
    spread = jnp.concatenate(swap_groups(tiles), axis=1)
    parts = dot_nt(three_parts(spread), onehot)
    return parts[:HEADS] + (parts[HEADS : 2 * HEADS] + parts[2 * HEADS :])


def attend_forward(qkv, bias_ref, layer, crop, probs_ref, frame, row_count):
    shifted = layer % 2 == 1
    windows = []
    for window in range(row_count // WINDOW):
        rows = slice(window * SPAN, (window + 1) * SPAN)
        mask = score_mask(crop[0], crop[1], shifted, window, row_count)
        halves = []
        for half in range(2):
            queries = qkv[rows, half * LANES : (half + 1) * LANES]
            keys = qkv[rows, WIDTH + half * LANES : WIDTH + (half + 1) * LANES]
            values = qkv[rows, 2 * WIDTH + half * LANES : 2 * WIDTH + (half + 1) * LANES]
            scores = dot_nt(keys, spread_heads(queries)) * SCALE
            scores = scores + bias_ref[layer, :, half_scores(half)] + mask
            exponent = jnp.exp(scores - jnp.max(scores, axis=0, keepdims=True))
            probs = exponent * (1.0 / jnp.sum(exponent, axis=0, keepdims=True))
            probs = probs.astype(BF16)
            at = (frame * (row_count // WINDOW) + window) * SPAN
            probs_ref[layer, pl.ds(pl.multiple_of(at, SPAN), SPAN), half_scores(half)] = probs
            halves.append(gather_heads(dot_tn(probs, values)))
        windows.append(jnp.concatenate(halves, axis=1))
    return jnp.concatenate(windows, axis=0)


def attend_backward(qkv, dcontext, layer, probs_ref, frame, gathered_ref, row_count):
    parts = []
    for window in range(row_count // WINDOW):
        rows = slice(window * SPAN, (window + 1) * SPAN)
        dqs, dks, dvs = [], [], []
        for half in range(2):
            queries = qkv[rows, half * LANES : (half + 1) * LANES]
            keys = qkv[rows, WIDTH + half * LANES : WIDTH + (half + 1) * LANES]
            values = qkv[rows, 2 * WIDTH + half * LANES : 2 * WIDTH + (half + 1) * LANES]
            dcs = spread_heads(dcontext[rows, half_lanes(half)])
            at = (frame * (row_count // WINDOW) + window) * SPAN
            low = probs_ref[layer, pl.ds(pl.multiple_of(at, SPAN), SPAN), half_scores(half)]
            probs = low.astype(F32)
            dvs.append(dot(low, dcs))
            dprobs = dot_nt(values, dcs)
            dscores = probs * (dprobs - jnp.sum(probs * dprobs, axis=0, keepdims=True))
            gathered_ref[layer, :, half_scores(half)] += dscores
            dscores = dscores.astype(BF16)
            dks.append(dot(dscores, spread_heads(queries)) * SCALE)
            dqs.append(gather_heads(dot_tn(dscores, keys)) * SCALE)
        parts.append([jnp.concatenate(d, axis=1) for d in (dqs, dks, dvs)])
    return [
        jnp.concatenate([part[i] for part in parts], axis=0).astype(BF16) for i in range(3)
    ]


def kernel(
    lon_count,
    crop_ref,
    frames_ref,
    latent_ref,
    cotangent_ref,
    triple_ref,
    output_ref,
    expand_ref,
    shrink_ref,
    recurrent_ref,
    readout_ref,
    gains_ref,
    table_ref,
    act_out_ref,
    input_grad_ref,
    grads_ref,
    triple_low,
    output_low,
    expand_low,
    shrink_low,
    recurrent_low,
    readout_low,
    table_pad,
    bias_ref,
    onehot_ref,
    gathered_ref,
    gain_sums,
    stream_in,
    stream_one,
    stream_two,
    normed_ref,
    qkv_ref,
    probs_ref,
    context_ref,
    cell_ref,
    tangent_ref,
    state_ref,
    hidden_ref,
    active_ref,
    slope_ref,
    g_ref,
    gm_ref,
    gl_ref,
    gc_ref,
    gpre_ref,
    gstate_ref,
    dcontext_ref,
    dpacked_ref,
    out_halo,
    in_halo,
    send_sem,
    recv_sem,
):
    frame_count = crop_ref.shape[0]
    tokens = frames_ref.shape[0] // frame_count
    row_count = tokens // WINDOW
    me_lon = lax.axis_index("lon")
    ahead = lax.rem(me_lon + 1, lon_count)
    behind = lax.rem(me_lon + lon_count - 1, lon_count)

    barrier = pltpu.get_barrier_semaphore()
    for peer in (ahead, behind):
        pl.semaphore_signal(barrier, inc=1, device_id={"lon": peer}, device_id_type=MESH)
    pl.semaphore_wait(barrier, 2)

    def halo(exchange, frame):
        return pltpu.make_async_remote_copy(
            src_ref=out_halo.at[exchange, frame],
            dst_ref=in_halo.at[exchange, frame],
            send_sem=send_sem.at[exchange, frame],
            recv_sem=recv_sem.at[exchange, frame],
            device_id={"lon": behind if exchange % 2 == 0 else ahead},
            device_id_type=MESH,
        )

    def send_halo(exchange, frame, value):
        out_halo[exchange, frame] = pack_half(value).astype(BF16)
        halo(exchange, frame).start()

    def take_halo(exchange, frame, own):
        halo(exchange, frame).wait_recv()
        return unpack_half(in_halo[exchange, frame].astype(F32), own)

    for layer in range(LAYERS):
        triple_low[layer] = triple_ref[layer].astype(BF16)
        output_low[layer] = output_ref[layer].astype(BF16)
        expand_low[layer] = expand_ref[layer].astype(BF16)
        shrink_low[layer] = shrink_ref[layer].astype(BF16)
        recurrent_low[layer] = recurrent_ref[layer].astype(BF16)
        readout_low[layer] = readout_ref[layer].astype(BF16)
        table_pad[...] = jnp.zeros_like(table_pad)
        table_pad[:, :PAIRS] = table_ref[layer]
        onehot_ref[layer] = offset_onehot(layer % 2 == 1)
        bias_ref[layer] = bias_of_table(table_pad[...], onehot_ref[layer])
    gathered_ref[...] = jnp.zeros_like(gathered_ref)
    gain_sums[...] = jnp.zeros_like(gain_sums)

    def span(frame):
        return pl.ds(pl.multiple_of(frame * tokens, tokens), tokens)

    def gain(layer, which):
        return gains_ref[layer, which : which + 1, :]

    def attention_part(layer, frame, normed):
        at = span(frame)
        normed_ref[layer, at] = normed
        qkv = dot(normed, triple_low[layer]).astype(BF16)
        qkv_ref[layer, at] = qkv
        crop = (crop_ref[frame, 0], crop_ref[frame, 1])
        return attend_forward(qkv, bias_ref, layer, crop, probs_ref, frame, row_count)

    def middle(layer, frame, stream, context, latent):
        at = span(frame)
        context_ref[layer, at] = context
        one = stream + dot(context, output_low[layer])
        stream_one[layer, at] = one
        scaled, _ = norm_parts(one)
        cell = (scaled * gain(layer, 2)).astype(BF16)
        cell_ref[layer, at] = cell
        preact = dot(cell, recurrent_low[layer, :WIDTH]) + dot(latent, recurrent_low[layer, WIDTH:])
        tangent = jnp.tanh(preact)
        tangent_ref[layer, at] = tangent
        state = tangent.astype(BF16)
        state_ref[layer, at] = state
        two = one + dot(state, readout_low[layer])
        stream_two[layer, at] = two
        scaled, _ = norm_parts(two)
        hidden = (scaled * gain(layer, 1)).astype(BF16)
        hidden_ref[layer, at] = hidden
        for block in range(HIDDEN // WIDTH):
            cols = slice(block * WIDTH, (block + 1) * WIDTH)
            inner = dot(hidden, expand_low[layer, :, cols])
            square = inner * inner
            bend = GELU_C * (1.0 + GELU_A * square)
            gate = 0.5 * (1.0 + jnp.tanh(inner * bend))
            active = inner * gate
            slope = gate + active * (1.0 - gate) * (2.0 * GELU_C + 6.0 * GELU_C * GELU_A * square)
            active_ref[layer, at, cols] = active.astype(BF16)
            slope_ref[layer, at, cols] = slope.astype(BF16)
        return two + dot(active_ref[layer, at], shrink_low[layer])

    def middle_back(layer, frame, g, gstate):
        at = span(frame)
        gm = g.astype(BF16)
        gm_ref[at] = gm
        for block in range(HIDDEN // WIDTH):
            cols = slice(block * WIDTH, (block + 1) * WIDTH)
            dactive = dot_nt(gm, shrink_low[layer, cols])
            slope_ref[layer, at, cols] = (dactive * slope_ref[layer, at, cols].astype(F32)).astype(BF16)
        dhidden = dot_nt(slope_ref[layer, at], expand_low[layer])
        scaled, inverse = norm_parts(stream_two[layer, at])
        part, change = norm_back(dhidden, gain(layer, 1), scaled, inverse)
        gain_sums[layer, 1] += part
        g = g + change
        gl = g.astype(BF16)
        gl_ref[at] = gl
        dstate = dot_nt(gl, readout_low[layer])
        if gstate is not None:
            dstate = dstate + gstate
        tangent = tangent_ref[layer, at]
        gpre = (dstate * (1.0 - tangent * tangent)).astype(BF16)
        gpre_ref[at] = gpre
        if layer > 0:
            gstate_ref[at] = dot_nt(gpre, recurrent_low[layer, WIDTH:])
        scaled, inverse = norm_parts(stream_one[layer, at])
        dcell = dot_nt(gpre, recurrent_low[layer, :WIDTH])
        part, change = norm_back(dcell, gain(layer, 2), scaled, inverse)
        gain_sums[layer, 2] += part
        g = g + change
        gc = g.astype(BF16)
        gc_ref[at] = gc
        g_ref[at] = g
        return dot_nt(gc, output_low[layer])

    def attention_back(layer, frame, dcontext):
        at = span(frame)
        pieces = attend_backward(
            qkv_ref[layer, at], dcontext, layer, probs_ref, frame, gathered_ref, row_count
        )
        for which in range(3):
            dpacked_ref[at, which * WIDTH : (which + 1) * WIDTH] = pieces[which]
        return dot_nt(dpacked_ref[at], triple_low[layer])

    def stream_back(layer, frame, g, stream, dnormed):
        scaled, inverse = norm_parts(stream)
        part, change = norm_back(dnormed, gain(layer, 0), scaled, inverse)
        gain_sums[layer, 0] += part
        return g + change

    def put_blocks(start, value):
        rows = value.shape[0]
        for block in range(value.shape[1] // LANES):
            grads_ref[start + block * rows : start + (block + 1) * rows] = value[
                :, half_lanes(block)
            ].astype(BF16)

    def put_rows(start, total_rows, row, value):
        rows = value.shape[0]
        for block in range(value.shape[1] // LANES):
            at = start + block * total_rows + row
            grads_ref[at : at + rows] = value[:, half_lanes(block)].astype(BF16)

    def feed_grads(layer):
        for block in range(HIDDEN // WIDTH):
            cols = slice(block * WIDTH, (block + 1) * WIDTH)
            put_rows(
                SHRINK_AT[layer], HIDDEN, block * WIDTH, dot_tn(active_ref[layer, :, cols], gm_ref[...])
            )
        for block in range(HIDDEN // WIDTH):
            cols = slice(block * WIDTH, (block + 1) * WIDTH)
            put_blocks(
                EXPAND_AT[layer] + 2 * block * WIDTH, dot_tn(hidden_ref[layer], slope_ref[layer, :, cols])
            )

    def small_grads(layer, latent):
        low = dot_tn(cell_ref[layer], gpre_ref[...])
        high = dot_tn(latent, gpre_ref[...])
        recurrent = jnp.concatenate([low, high], axis=0)
        quarter = recurrent.shape[0] // 4
        recurrent = jnp.concatenate(
            [recurrent[i * quarter : (i + 1) * quarter] for i in range(4)], axis=1
        )
        readout = dot_tn(state_ref[layer], gl_ref[...])
        return [recurrent, readout[:, :LANES], readout[:, LANES:]]

    def put_small(layer, pieces):
        table = table_of_bias(gathered_ref[layer], onehot_ref[layer])
        gains = jnp.concatenate(
            [jnp.sum(gain_sums[layer, i], axis=0, keepdims=True) for i in range(3)]
            + [jnp.zeros((5, WIDTH), F32)],
            axis=0,
        )
        pieces = pieces + [table[:, :LANES], table[:, LANES:], gains[:, :LANES], gains[:, LANES:]]
        used = sum(piece.shape[0] for piece in pieces)
        pieces = pieces + [jnp.zeros((SMALL_ROWS - used, LANES), F32)]
        grads_ref[SMALL_AT[layer] : SMALL_AT[layer] + SMALL_ROWS] = jnp.concatenate(
            pieces, axis=0
        ).astype(BF16)

    def output_grads(layer):
        put_blocks(OUTPUT_AT[layer], dot_tn(context_ref[layer], gc_ref[...]))

    def triple_grads(layer):
        for block in range(3):
            cols = slice(block * WIDTH, (block + 1) * WIDTH)
            put_blocks(
                TRIPLE_AT[layer] + 2 * block * WIDTH, dot_tn(normed_ref[layer], dpacked_ref[:, cols])
            )

    def loop(body):
        lax.fori_loop(0, frame_count, lambda frame, unused: body(frame), None)

    def first_layer(frame):
        at = span(frame)
        stream = frames_ref[at].astype(F32)
        scaled, _ = norm_parts(stream)
        normed = (scaled * gain(0, 0)).astype(BF16)
        context = attention_part(0, frame, normed).astype(BF16)
        stream = middle(0, frame, stream, context, latent_ref[at])
        stream_in[at] = stream
        scaled, _ = norm_parts(stream)
        normed = scaled * gain(1, 0)
        normed_ref[1, at] = normed.astype(BF16)
        send_halo(0, frame, normed)

    loop(first_layer)

    def second_attention(frame):
        at = span(frame)
        normed = take_halo(0, frame, normed_ref[1, at].astype(F32))
        context = attention_part(1, frame, rows_ahead(normed).astype(BF16))
        context = rows_behind(context)
        context_ref[1, at] = context.astype(BF16)
        send_halo(1, frame, context)

    loop(second_attention)

    def second_middle(frame):
        at = span(frame)
        context = take_halo(1, frame, context_ref[1, at].astype(F32)).astype(BF16)
        stream = middle(1, frame, stream_in[at], context, state_ref[0, at])
        act_out_ref[at] = stream.astype(BF16)
        dcontext = middle_back(1, frame, cotangent_ref[at].astype(F32), None)
        dcontext_ref[at] = dcontext.astype(BF16)
        send_halo(2, frame, dcontext)

    loop(second_middle)
    feed_grads(1)
    output_grads(1)
    small_one = small_grads(1, state_ref[0])

    def second_back(frame):
        at = span(frame)
        dcontext = take_halo(2, frame, dcontext_ref[at].astype(F32))
        dnormed = attention_back(1, frame, rows_ahead(dcontext).astype(BF16))
        dnormed = rows_behind(dnormed)
        dcontext_ref[at] = dnormed.astype(BF16)
        send_halo(3, frame, dnormed)

    loop(second_back)
    triple_grads(1)

    def first_middle_back(frame):
        at = span(frame)
        dnormed = take_halo(3, frame, dcontext_ref[at].astype(F32))
        g = stream_back(1, frame, g_ref[at], stream_in[at], dnormed)
        dcontext_ref[at] = middle_back(0, frame, g, gstate_ref[at]).astype(BF16)

    loop(first_middle_back)
    put_small(1, small_one)
    feed_grads(0)
    output_grads(0)
    small_zero = small_grads(0, latent_ref[...])

    def first_back(frame):
        at = span(frame)
        dnormed = attention_back(0, frame, dcontext_ref[at])
        stream = frames_ref[at].astype(F32)
        input_grad_ref[at] = stream_back(0, frame, g_ref[at], stream, dnormed)

    loop(first_back)
    triple_grads(0)
    put_small(0, small_zero)

    def drain(frame, unused):
        for exchange in range(4):
            halo(exchange, frame).wait_send()

    lax.fori_loop(0, frame_count, drain, None)


def layers_step(frames, latent, crop_band, cotangent, weights, lon_count):
    frame_count, row_count, col_count, features = frames.shape
    count = frame_count * row_count * col_count
    tokens = row_count * col_count
    flat = lambda a: a.reshape(count, a.shape[-1])
    vmem = pl.BlockSpec(memory_space=pltpu.VMEM)
    both = lambda *shape: pltpu.VMEM((LAYERS,) + shape, BF16)
    one = lambda *shape: pltpu.VMEM(shape, BF16)
    wide = lambda *shape: pltpu.VMEM(shape, F32)
    scratch = [
        both(WIDTH, 3 * WIDTH),
        both(WIDTH, WIDTH),
        both(WIDTH, HIDDEN),
        both(HIDDEN, WIDTH),
        both(WIDTH + LATENT, LATENT),
        both(LATENT, WIDTH),
        wide(HEADS, WIDTH),
        wide(LAYERS, SPAN, HEADS * SPAN),
        both(WIDTH, WINDOW * LANES),
        wide(LAYERS, SPAN, HEADS * SPAN),
        wide(LAYERS, 3, 8, WIDTH),
        wide(count, WIDTH),
        wide(LAYERS, count, WIDTH),
        wide(LAYERS, count, WIDTH),
        both(count, WIDTH),
        both(count, 3 * WIDTH),
        both(count, HEADS * SPAN),
        both(count, WIDTH),
        both(count, WIDTH),
        wide(LAYERS, count, LATENT),
        both(count, LATENT),
        both(count, WIDTH),
        both(count, HIDDEN),
        both(count, HIDDEN),
        wide(count, WIDTH),
        one(count, WIDTH),
        one(count, WIDTH),
        one(count, WIDTH),
        one(count, LATENT),
        wide(count, LATENT),
        one(count, WIDTH),
        one(count, 3 * WIDTH),
        one(4, frame_count, tokens // 2, WIDTH),
        one(4, frame_count, tokens // 2, WIDTH),
        pltpu.SemaphoreType.DMA((4, frame_count)),
        pltpu.SemaphoreType.DMA((4, frame_count)),
    ]
    return pl.pallas_call(
        functools.partial(kernel, lon_count),
        out_shape=(
            jax.ShapeDtypeStruct((count, WIDTH), BF16),
            jax.ShapeDtypeStruct((count, WIDTH), F32),
            jax.ShapeDtypeStruct((GRAD_ROWS, LANES), BF16),
        ),
        in_specs=[pl.BlockSpec(memory_space=pltpu.SMEM)] + [vmem] * (3 + len(weights)),
        out_specs=(vmem, vmem, vmem),
        scratch_shapes=scratch,
        compiler_params=pltpu.CompilerParams(
            collective_id=0, has_side_effects=True, vmem_limit_bytes=60 * 1024 * 1024
        ),
        name="swin_step",
    )(crop_band, flat(frames), flat(latent), flat(cotangent), *weights)


def update(weight, moment, average, gradient):
    velocity = MOMENTUM_RATE * moment + gradient
    updated = weight - LEARN_RATE * (gradient + MOMENTUM_RATE * velocity)
    smoothed = AVERAGE_DECAY * average + (1.0 - AVERAGE_DECAY) * updated
    return (updated, velocity, smoothed)


def unblock(rows, shape):
    height, width = shape
    return rows.reshape(width // LANES, height, LANES).transpose(1, 0, 2).reshape(shape)


def split_grads(grads):
    def at(start, shape):
        count = shape[0] * shape[1] // LANES
        return unblock(grads[start : start + count], shape)

    def expand_at(start, blocks):
        return jnp.concatenate([at(start + 512 * i, (WIDTH, WIDTH)) for i in range(blocks)], axis=1)

    out = []
    for layer in range(LAYERS):
        small = grads[SMALL_AT[layer] : SMALL_AT[layer] + SMALL_ROWS]
        recurrent = jnp.concatenate(
            [small[:72, i * LATENT : (i + 1) * LATENT] for i in range(4)], axis=0
        )
        out.append(
            (
                expand_at(TRIPLE_AT[layer], 3),
                at(OUTPUT_AT[layer], (WIDTH, WIDTH)),
                expand_at(EXPAND_AT[layer], 4),
                at(SHRINK_AT[layer], (HIDDEN, WIDTH)),
                recurrent,
                unblock(small[72:136], (LATENT, WIDTH)),
                unblock(small[152:168], (8, WIDTH))[:3],
                unblock(small[136:152], (HEADS, WIDTH))[:, :PAIRS],
            )
        )
    return [jnp.stack(pair) for pair in zip(*out)]


def per_device(frames, latent_init, crop_band, cotangent, *parameters):
    weights, moments, averages = parameters[0::3], parameters[1::3], parameters[2::3]
    shape = frames.shape
    result, input_grad, grads = layers_step(
        frames, latent_init, crop_band, cotangent, weights, lax.axis_size("lon")
    )
    grads = lax.psum(grads, ("lon", "batch")).astype(F32)
    tokens = shape[0] * shape[1] * shape[2] * lax.axis_size("lon") * lax.axis_size("batch")
    scale = float(tokens) ** (-0.5)
    outs = [result.reshape(shape), input_grad.reshape(shape)]
    for weight, moment, average, gradient in zip(weights, moments, averages, split_grads(grads)):
        outs.extend(update(weight, moment, average, gradient * scale))
    return tuple(outs)


def solution(mesh):
    split = P("batch", None, "lon", None)
    return jax.shard_map(
        per_device,
        mesh=mesh,
        in_specs=(split, split, P("batch", None), split) + (P(),) * 24,
        out_specs=(split, split) + (P(),) * 24,
        check_vma=False,
    )
```

time: 450 us -> 279 us (0.62); the launches traced: 445 us -> 279 us
  local copies, waits for them, and re-layouts: 137 us -> 44.1 us
  matrix products: 79.9 us -> 0 us
  Pallas kernels: 0 us -> 65.8 us
  other arithmetic: 72.6 us -> 15.1 us
  waiting for transfers between devices: 93.2 us -> 139 us
  blocking collectives: 41.2 us -> 0 us
  starting transfers between devices: 5.23 us -> 0.04 us
    dot_general x52 -> x0, matrix products: 79.9 us -> none  [the longest x12 16.4 us: token_outer(): lax.dot_general(left.reshape(-1, left.shape[-1]), right.reshape(-1, right...]
    pallas_call x0 -> x1, Pallas kernels: none -> 65.8 us  [layers_step(): pl.pallas_call(functools.partial(kernel, lon_count), out_shape=(jax.Shape...]
    psum x1, waiting for transfers between devices: 84.3 us -> 139 us  [per_device(): grads = lax.psum(grads, ('lon', 'batch')).astype(F32)]
    another operation x13 -> x7, local copies, waits for them, and re-layouts: 56 us -> 9.14 us  [split_grads(): return [jnp.stack(pair) for pair in zip(*out)]]
    psum x1 -> x0, blocking collectives: 41.2 us -> none  [per_device(): lax.psum((triple_sum, output_sum, expand_sum, shrink_sum, recurrent_sum,...]
    convert_element_type x7 -> x0, local copies, waits for them, and re-layouts: 33.7 us -> none  [the longest x4 26.9 us: attend_backward(): grad_packed.reshape(window_count, window_size, -1).astype(jnp.bfloat16)]
    unnamed x269 -> x107, local copies, waits for them, and re-layouts: 25.4 us -> 9.86 us
    add x16 -> x8, other arithmetic: 28.9 us -> 14.2 us  [update(): smoothed = AVERAGE_DECAY * average + (1.0 - AVERAGE_DECAY) * updated]
  transfers between devices with their start and end apart: 5 -> 1, of which waited for: 3 -> 1; matrix products, arithmetic and copies ran while one was open for 15% -> 0% of each run, Pallas kernels for 0% -> 0%
where the time goes in v1:
time: 279 us
  waiting for transfers between devices  139 us (50%)
  Pallas kernels  65.8 us (24%)
  local copies, waits for them, and re-layouts  44.1 us (16%)
  other arithmetic  15.1 us (5%)
  between operations  14.7 us (5%)
    psum x1, waiting for transfers between devices, per_device(): grads = lax.psum(grads, ('lon', 'batch')).astype(F32)  139 us
    pallas_call x1, Pallas kernels, layers_step(): pl.pallas_call(functools.partial(kernel, lon_count), out_shape=(jax.Shape...  65.8 us
    add x8, other arithmetic, update(): smoothed = AVERAGE_DECAY * average + (1.0 - AVERAGE_DECAY) * updated  14.2 us
    unnamed x107, local copies, waits for them, and re-layouts  9.86 us
    another operation x7, local copies, waits for them, and re-layouts, split_grads(): return [jnp.stack(pair) for pair in zip(*out)]  9.14 us
    transpose x6, local copies, waits for them, and re-layouts, unblock(): rows.reshape(width // LANES, height, LANES).transpose(1, 0, 2)  8.43 us
    slice x9, local copies, waits for them, and re-layouts, split_grads(): small[:72, i * LATENT:(i + 1) * LATENT]  5.86 us
  transfers between devices with their start and end apart: 1, of which 1 were waited for; matrix products, arithmetic and copies ran while one was open for 0% of the time, Pallas kernels for 0%

profile of v1, /device:TPU:0, one launch (start us, length us, event | category | flops | bytes accessed | tf_op | source)
XLA Modules:
  0.0 278.9 jit_solution(917184542845743192)
XLA Ops:
  7.2 1.8 copy.86.recurrent_ref
  9.0 1.3 copy.87.gains_ref
  10.3 1.3 copy.85.crop_ref
  11.6 65.8 %swin_step.1 = (bf16[1024,256]{1,0:T(8,128)(2,1)}, f32[1024,256]{1,0:T(8,128)}, bf16[12800,128]{1,0:T(8,128)(2,1)}) custom-call(s32[4,2]{1,0:T(4,128)} %copy.85.crop_ref, bf16[1024,256]{1,0:T(8,128)(2,1)} %bitcast.169, bf16[1024,32]{1,0:T(8,128)(2,1)} %bitcast.171, bf16[1024,256]{1,0:T(8,128)(2,1)} %bitcast.170, f32[2,256,768]{2,1,0:T(8,128)} %triple_ref.1, ...), custom_call_target="tpu_custom_call" | custom-call | tf_op jit(solution)/shard_map/swin_step/pallas_call | solution.py:642
  77.5 139.0 %all-reduce.2.cloned.1.call-done = bf16[12800,128]{1,0:T(8,128)(2,1)} async-done(((bf16[12800,128]{1,0:T(8,128)(2,1)}), bf16[12800,128]{1,0:T(8,128)(2,1)}) %all-reduce.2.cloned.1.call-update) | async-done | bytes 3276816 | tf_op jit(solution)/shard_map/psum | solution.py:706
  216.5 1.0 fusion.1
  217.6 0.7 copy.107
  219.7 0.7 copy.110
  222.4 3.5 %fusion.3 = (f32[512,128]{1,0:T(8,128)}, f32[512,128]{1,0:T(8,128)}, f32[512,128]{1,0:T(8,128)}, f32[512,128]{1,0:T(8,128)}, f32[512,128]{1,0:T(8,128)}, /*index...) fusion(bf16[12800,128]{1,0:T(8,128)(2,1)} %all-reduce.2.cloned., ...), kind=kLoop, calls=%fused_computation.61 | loop fusion | bytes 8388608 | tf_op jit(solution)/shard_map/slice | solution.py:674
  225.9 0.7 copy.147
  226.6 0.7 copy.146
  227.3 0.9 copy.94
  228.2 1.2 stack_reshape.18
  229.4 1.9 copy.95
  231.3 1.9 stack_reshape.19
  235.4 1.1 fusion.2
  236.5 1.8 copy.104
  238.2 3.0 %stack_reshape.20 = f32[1,1024,256]{2,1,0:T(8,128)} reshape(f32[1024,2,128]{2,1,0:T(2,128)} %copy.104) | data formatting | bytes 2097152 | tf_op jit(solution)/shard_map/stack;reshape | solution.py:697
  241.3 3.0 %copy.105 = f32[1024,2,128]{2,1,0:T(2,128)} copy(f32[1024,2,128]{2,0,1:T(8,128)} %bitcast.147) | data formatting | bytes 2097152 | tf_op jit(solution)/shard_map/transpose | solution.py:668
  244.3 3.0 %stack_reshape.21 = f32[1,1024,256]{2,1,0:T(8,128)} reshape(f32[1024,2,128]{2,1,0:T(2,128)} %copy.105) | data formatting | bytes 2097152 | tf_op jit(solution)/shard_map/stack;reshape | solution.py:697
  248.0 0.9 copy.115
  248.9 1.1 copy_bitcast_fusion.4
  250.1 1.1 copy_bitcast_fusion.6
  252.6 0.7 add_multiply_fusion.4
  254.1 1.1 copy-done.1
  255.8 4.0 %add_multiply_fusion.1 = (f32[2,256,1024]{2,1,0:T(8,128)}, f32[2,256,1024]{2,1,0:T(8,128)}, f32[2,256,1024]{2,1,0:T(8,128)}) fusion(f32[2,256,1024]{2,1,0:T(8,128)S(1)} %copy-done.6, f32[2,256,1024]{2,1,0:T(8,128)S(1)} %copy-done.1, f32[1,256,1024]{2,1,0:T(8,128)S(1)} %maximum_bitcast_fusion.1, f32[1,256,1024]{2,1,0:T(8,128)S(1)} %maximum_bitcast_fusion, ...), kind=kLoop, calls=%fused_computation.5 | loop fusion | flops 5242880 | bytes 14680064 | tf_op jit(solution)/shard_map/add | solution.py:662
  259.8 2.9 %add_multiply_fusion.2 = (f32[2,256,768]{2,1,0:T(8,128)}, f32[2,256,768]{2,1,0:T(8,128)}, f32[2,256,768]{2,1,0:T(8,128)}) fusion(f32[2,256,768]{2,1,0:T(8,128)S(1)} %copy-done.11, f32[2,256,768]{2,1,0:T(8,128)S(1)} %copy-done.3, f32[1,256,768]{2,1,0:T(8,128)S(1)} %maximum_bitcast_fusion.3, f32[1,256,768]{2,1,0:T(8,128)S(1)} %maximum_bitcast_fusion.2, ...), kind=kLoop, calls=%fused_computation.9 | loop fusion | flops 3932160 | bytes 11010048 | tf_op jit(solution)/shard_map/add | solution.py:662
  262.9 1.3 add_multiply_fusion.3
  266.2 3.4 %add_multiply_fusion = (f32[2,1024,256]{2,1,0:T(8,128)}, f32[2,1024,256]{2,1,0:T(8,128)}, f32[2,1024,256]{2,1,0:T(8,128)}) fusion(f32[2,1024,256]{2,1,0:T(8,128)S(1)} %copy-done.8, f32[2,1024,256]{2,1,0:T(8,128)S(1)} %copy-done.2, f32[1,1024,256]{2,1,0:T(8,128)S(1)} %copy-done.5, f32[1,1024,256]{2,1,0:T(8,128)S(1)} %copy-done.4, f32[2,1024,256]{2,1,0:T(8,128)S(1)} %copy-done.9), kind=kLoop, calls=%fused_computation.2 | loop fusion | flops 5242880 | bytes 14680064 | tf_op jit(solution)/shard_map/add | solution.py:662
  269.6 0.7 add_multiply_fusion.5
  270.3 0.8 copy.151
  271.1 1.0 copy.152
  (131 shorter events, 11.0 us)
Async XLA Ops:
  7.2 209.3 %all-reduce.2.cloned.1.call-start = ((), (), s32[]{:S(2)}) async-start(), calls=%async_computation | async-start | bytes 6553600 | tf_op jit(solution)/shard_map/psum | solution.py:706
  222.4 10.7 %copy-start = (bf16[12800,128]{1,0:T(8,128)(2,1)S(1)}, bf16[12800,128]{1,0:T(8,128)(2,1)}, u32[]{:S(2)}) copy-start(bf16[12800,128]{1,0:T(8,128)(2,1)} %all-reduce.2.cloned.1.call-done) | copy-start | bytes 9830404
  247.9 3.3 %copy-start.21 = (f32[512,128]{1,0:T(8,128)S(1)}, f32[512,128]{1,0:T(8,128)}, u32[]{:S(2)}) copy-start(f32[512,128]{1,0:T(8,128)} %get-tuple-element.104) | copy-start | bytes 786436
  247.9 3.3 %copy-start.22 = (f32[512,128]{1,0:T(8,128)S(1)}, f32[512,128]{1,0:T(8,128)}, u32[]{:S(2)}) copy-start(f32[512,128]{1,0:T(8,128)} %get-tuple-element.105) | copy-start | bytes 786436
  247.9 3.4 %copy-start.19 = (f32[512,128]{1,0:T(8,128)S(1)}, f32[512,128]{1,0:T(8,128)}, u32[]{:S(2)}) copy-start(f32[512,128]{1,0:T(8,128)} %get-tuple-element.102) | copy-start | bytes 786436
  247.9 3.4 %copy-start.20 = (f32[512,128]{1,0:T(8,128)S(1)}, f32[512,128]{1,0:T(8,128)}, u32[]{:S(2)}) copy-start(f32[512,128]{1,0:T(8,128)} %get-tuple-element.103) | copy-start | bytes 786436
  248.9 2.5 copy-start.17
  248.9 2.5 copy-start.18
  253.4 2.4 copy-start.6
  255.7 4.0 %copy-start.3 = (f32[2,256,768]{2,1,0:T(8,128)S(1)}, f32[2,256,768]{2,1,0:T(8,128)}, u32[]{:S(2)}) copy-start(f32[2,256,768]{2,1,0:T(8,128)} %triple_ref.1) | copy-start | bytes 4718596
  255.8 4.0 %copy-start.11 = (f32[2,256,768]{2,1,0:T(8,128)S(1)}, f32[2,256,768]{2,1,0:T(8,128)}, u32[]{:S(2)}) copy-start(f32[2,256,768]{2,1,0:T(8,128)} %param.34) | copy-start | bytes 4718596
  255.8 4.0 %copy-start.12 = (f32[2,256,768]{2,1,0:T(8,128)S(1)}, f32[2,256,768]{2,1,0:T(8,128)}, u32[]{:S(2)}) copy-start(f32[2,256,768]{2,1,0:T(8,128)} %param.33) | copy-start | bytes 4718596
  259.8 3.0 %copy-start.10 = (f32[2,256,256]{2,1,0:T(8,128)S(1)}, f32[2,256,256]{2,1,0:T(8,128)}, u32[]{:S(2)}) copy-start(f32[2,256,256]{2,1,0:T(8,128)} %output_ref.1) | copy-start | bytes 1572868
  259.8 3.0 %copy-start.13 = (f32[1,256,256]{2,1,0:T(8,128)S(1)}, f32[1,256,256]{2,1,0:T(8,128)}, u32[]{:S(2)}) copy-start(f32[1,256,256]{2,1,0:T(8,128)} %stack_reshape.19) | copy-start | bytes 786436
  259.8 3.0 %copy-start.25 = (f32[2,256,256]{2,1,0:T(8,128)S(1)}, f32[2,256,256]{2,1,0:T(8,128)}, u32[]{:S(2)}) copy-start(f32[2,256,256]{2,1,0:T(8,128)} %param.37) | copy-start | bytes 1572868
  259.8 3.0 %copy-start.26 = (f32[2,256,256]{2,1,0:T(8,128)S(1)}, f32[2,256,256]{2,1,0:T(8,128)}, u32[]{:S(2)}) copy-start(f32[2,256,256]{2,1,0:T(8,128)} %param.36) | copy-start | bytes 1572868
  259.8 6.3 %copy-start.5 = (f32[1,1024,256]{2,1,0:T(8,128)S(1)}, f32[1,1024,256]{2,1,0:T(8,128)}, u32[]{:S(2)}) copy-start(f32[1,1024,256]{2,1,0:T(8,128)} %stack_reshape.21) | copy-start | bytes 3145732
  259.8 6.3 %copy-start.8 = (f32[2,1024,256]{2,1,0:T(8,128)S(1)}, f32[2,1024,256]{2,1,0:T(8,128)}, u32[]{:S(2)}) copy-start(f32[2,1024,256]{2,1,0:T(8,128)} %param.43) | copy-start | bytes 6291460
  259.8 6.3 %copy-start.9 = (f32[2,1024,256]{2,1,0:T(8,128)S(1)}, f32[2,1024,256]{2,1,0:T(8,128)}, u32[]{:S(2)}) copy-start(f32[2,1024,256]{2,1,0:T(8,128)} %param.42) | copy-start | bytes 6291460
  262.8 2.1 copy-start.45
  262.8 2.1 copy-start.46
  262.8 2.7 copy-start.44
  262.8 2.7 copy-start.47
  262.8 2.7 copy-start.48
  262.8 2.7 copy-start.49
  262.8 2.7 copy-start.50
  262.9 3.3 %copy-start.2 = (f32[2,1024,256]{2,1,0:T(8,128)S(1)}, f32[2,1024,256]{2,1,0:T(8,128)}, u32[]{:S(2)}) copy-start(f32[2,1024,256]{2,1,0:T(8,128)} %shrink_ref.1) | copy-start | bytes 6291460
  262.9 3.3 %copy-start.4 = (f32[1,1024,256]{2,1,0:T(8,128)S(1)}, f32[1,1024,256]{2,1,0:T(8,128)}, u32[]{:S(2)}) copy-start(f32[1,1024,256]{2,1,0:T(8,128)} %stack_reshape.20) | copy-start | bytes 3145732
  266.2 3.4 %copy-start.29 = (f32[2,32,256]{2,1,0:T(8,128)S(1)}, f32[2,32,256]{2,1,0:T(8,128)}, u32[]{:S(2)}) copy-start(f32[2,32,256]{2,1,0:T(8,128)} %readout_ref.1) | copy-start | bytes 196612
  266.2 3.4 %copy-start.40 = (f32[2,32,256]{2,1,0:T(8,128)S(1)}, f32[2,32,256]{2,1,0:T(8,128)}, u32[]{:S(2)}) copy-start(f32[2,32,256]{2,1,0:T(8,128)} %param.49) | copy-start | bytes 196612
  266.2 3.4 %copy-start.41 = (f32[2,32,256]{2,1,0:T(8,128)S(1)}, f32[2,32,256]{2,1,0:T(8,128)}, u32[]{:S(2)}) copy-start(f32[2,32,256]{2,1,0:T(8,128)} %param.48) | copy-start | bytes 196612
  266.2 4.1 %copy-start.27 = (bf16[1024,256]{1,0:T(8,128)(2,1)S(1)}, bf16[1024,256]{1,0:T(8,128)(2,1)}, u32[]{:S(2)}) copy-start(bf16[1024,256]{1,0:T(8,128)(2,1)} %get-tuple-element.29) | copy-start | bytes 1572868
  (20 other events, 22.8 us)
Sparse Core Ops, SparseCore 0:
  77.6 138.8 all-reduce.1

commit v2 on v1

--- a/solution.py
+++ b/solution.py
@@ -1,4 +1,5 @@
 import functools
+import math
 
 import jax
 import jax.numpy as jnp
@@ -35,14 +36,33 @@
 MESH = pl.DeviceIdType.MESH
 
 SMALL_ROWS = 256
-SHRINK_AT, EXPAND_AT, OUTPUT_AT, TRIPLE_AT, SMALL_AT, GRAD_ROWS = (
-    (4096 + 2048, 0),
-    (4096 + 2048 + 2048, 2048),
-    (4096 + 2048 + 4096, 4096),
-    (4096 + 2048 + 4096 + 512, 4096 + 512),
-    (4096 + 2048 + 4096 + 2048, 4096 + 2048 + 4096 + 2048 + SMALL_ROWS),
-    4096 + 2048 + 4096 + 2048 + 2 * SMALL_ROWS,
+FEED_ROWS = 2 * HIDDEN * WIDTH // LANES
+OUTPUT_ROWS = WIDTH * WIDTH // LANES
+TRIPLE_ROWS = 3 * OUTPUT_ROWS
+FEED_ONE, ATTEND_ONE, FEED_ZERO, ATTEND_ZERO = range(4)
+SECTION_ROWS = (
+    FEED_ROWS,
+    OUTPUT_ROWS + TRIPLE_ROWS,
+    FEED_ROWS,
+    OUTPUT_ROWS + TRIPLE_ROWS + LAYERS * SMALL_ROWS,
 )
+ROW_TILE = 16
+
+
+class Places:
+    def __init__(self, device_count):
+        unit = ROW_TILE * device_count
+        self.rows = [-(-rows // unit) * unit for rows in SECTION_ROWS]
+        self.starts = [sum(self.rows[:i]) for i in range(len(self.rows))]
+        self.total = sum(self.rows)
+        feed = (self.starts[FEED_ZERO], self.starts[FEED_ONE])
+        attend = (self.starts[ATTEND_ZERO], self.starts[ATTEND_ONE])
+        self.shrink = feed
+        self.expand = tuple(at + FEED_ROWS // 2 for at in feed)
+        self.output = attend
+        self.triple = tuple(at + OUTPUT_ROWS for at in attend)
+        small = attend[0] + OUTPUT_ROWS + TRIPLE_ROWS
+        self.small = tuple(small + i * SMALL_ROWS for i in range(LAYERS))
 
 
 def dot(a, b):
@@ -262,6 +282,8 @@
 
 def kernel(
     lon_count,
+    batch_count,
+    places,
     crop_ref,
     frames_ref,
     latent_ref,
@@ -276,7 +298,7 @@
     table_ref,
     act_out_ref,
     input_grad_ref,
-    grads_ref,
+    sums_out_ref,
     triple_low,
     output_low,
     expand_low,
@@ -311,20 +333,141 @@
     dpacked_ref,
     out_halo,
     in_halo,
+    grads_ref,
+    sums_ref,
+    core_in,
+    lon_in,
+    line_in,
     send_sem,
     recv_sem,
+    sum_send_sem,
+    sum_recv_sem,
+    out_sem,
 ):
-    frame_count = crop_ref.shape[0]
+    frame_count = crop_ref.shape[1]
     tokens = frames_ref.shape[0] // frame_count
     row_count = tokens // WINDOW
     me_lon = lax.axis_index("lon")
     ahead = lax.rem(me_lon + 1, lon_count)
     behind = lax.rem(me_lon + lon_count - 1, lon_count)
 
+    me_batch = lax.axis_index("batch")
+    core, line = lax.rem(me_batch, 2), lax.div(me_batch, 2)
+    line_count = batch_count // 2
+    lon_peers = [lax.rem(me_lon + by, lon_count) for by in range(1, lon_count)]
+    line_peers = [lax.rem(line + by, line_count) for by in range(1, line_count)]
+    neighbours = [{"batch": 2 * line + 1 - core}]
+    neighbours += [{"lon": peer} for peer in lon_peers]
+    neighbours += [{"batch": 2 * peer + core} for peer in line_peers]
+
     barrier = pltpu.get_barrier_semaphore()
-    for peer in (ahead, behind):
-        pl.semaphore_signal(barrier, inc=1, device_id={"lon": peer}, device_id_type=MESH)
-    pl.semaphore_wait(barrier, 2)
+    for peer in neighbours:
+        pl.semaphore_signal(barrier, inc=1, device_id=peer, device_id_type=MESH)
+    pl.semaphore_wait(barrier, len(neighbours))
+
+    def row_span(start, rows):
+        return pl.ds(pl.multiple_of(start, ROW_TILE), rows)
+
+    def sum_copies(section, phase):
+        half = places.rows[section] // 2
+        piece = half // lon_count
+        shard = piece // line_count
+        my_half = places.starts[section] + core * half
+        my_piece = my_half + me_lon * piece
+        my_shard = my_piece + line * shard
+        wide = places.starts[section]
+        first_sem = (0, 1, lon_count, lon_count + line_count - 1, lon_count + 2 * (line_count - 1), 2 * (lon_count + line_count - 1) - 1)[phase]
+        if phase == 0:
+            to = [(grads_ref, places.starts[section] + (1 - core) * half, core_in, wide // 2)]
+            rows, peers = half, neighbours[:1]
+        elif phase == 1:
+            to = [
+                (grads_ref, my_half + peer * piece, lon_in, (wide // 2 // lon_count) * (lon_count - 1) + i * piece)
+                for i, peer in enumerate(lon_peers)
+            ]
+            rows, peers = piece, neighbours[1:lon_count]
+        elif phase == 2:
+            to = [
+                (
+                    grads_ref,
+                    my_piece + peer * shard,
+                    line_in,
+                    (wide // 2 // lon_count // line_count) * (line_count - 1) + i * shard,
+                )
+                for i, peer in enumerate(line_peers)
+            ]
+            rows, peers = shard, neighbours[lon_count:]
+        elif phase == 3:
+            rows, peers = shard, neighbours[lon_count:]
+            to = [(sums_ref, my_shard, sums_ref, my_shard)] * len(peers)
+        elif phase == 4:
+            rows, peers = piece, neighbours[1:lon_count]
+            to = [(sums_ref, my_piece, sums_ref, my_piece)] * len(peers)
+        else:
+            rows, peers = half, neighbours[:1]
+            to = [(sums_ref, my_half, sums_ref, my_half)]
+        return [
+            pltpu.make_async_remote_copy(
+                src_ref=src.at[row_span(src_at, rows)],
+                dst_ref=dst.at[row_span(dst_at, rows)],
+                send_sem=sum_send_sem.at[section, first_sem + i],
+                recv_sem=sum_recv_sem.at[section, first_sem + i],
+                device_id=peer,
+                device_id_type=MESH,
+            )
+            for i, ((src, src_at, dst, dst_at), peer) in enumerate(zip(to, peers))
+        ]
+
+    def add_up(start, rows, source, source_at, count, target):
+        step = math.gcd(rows, LANES)
+
+        def body(i, unused):
+            at = row_span(start + i * step, step)
+            total = grads_ref[at].astype(F32)
+            for k in range(count):
+                total = total + source[row_span(source_at + k * rows + i * step, step)].astype(F32)
+            target[at] = total.astype(BF16)
+
+        lax.fori_loop(0, rows // step, body, None)
+
+    def sum_start(section, phase):
+        for copy in sum_copies(section, phase):
+            copy.start()
+
+    def sum_take(section, phase):
+        for copy in sum_copies(section, phase):
+            copy.wait_recv()
+        half = places.rows[section] // 2
+        piece = half // lon_count
+        shard = piece // line_count
+        my_half = places.starts[section] + core * half
+        my_piece = my_half + me_lon * piece
+        wide = places.starts[section] // 2
+        if phase == 0:
+            add_up(my_half, half, core_in, wide, 1, grads_ref)
+        elif phase == 1:
+            at = wide // lon_count * (lon_count - 1)
+            add_up(my_piece, piece, lon_in, at, lon_count - 1, grads_ref)
+        elif phase == 2:
+            at = wide // lon_count // line_count * (line_count - 1)
+            add_up(my_piece + line * shard, shard, line_in, at, line_count - 1, sums_ref)
+
+    def sum_step(section, phase):
+        sum_take(section, phase)
+        if phase < 5:
+            sum_start(section, phase + 1)
+        else:
+            sums_out(section).start()
+
+    def sums_out(section):
+        rows = pl.ds(places.starts[section], places.rows[section])
+        return pltpu.make_async_copy(sums_ref.at[rows], sums_out_ref.at[rows], out_sem.at[section])
+
+    def sum_drain(section):
+        for phase in range(6):
+            for copy in sum_copies(section, phase):
+                copy.wait_send()
+        sums_out(section).wait()
 
     def halo(exchange, frame):
         return pltpu.make_async_remote_copy(
@@ -362,14 +505,14 @@
         return pl.ds(pl.multiple_of(frame * tokens, tokens), tokens)
 
     def gain(layer, which):
-        return gains_ref[layer, which : which + 1, :]
+        return gains_ref[which, layer : layer + 1, :]
 
     def attention_part(layer, frame, normed):
         at = span(frame)
         normed_ref[layer, at] = normed
         qkv = dot(normed, triple_low[layer]).astype(BF16)
         qkv_ref[layer, at] = qkv
-        crop = (crop_ref[frame, 0], crop_ref[frame, 1])
+        crop = (crop_ref[0, frame], crop_ref[1, frame])
         return attend_forward(qkv, bias_ref, layer, crop, probs_ref, frame, row_count)
 
     def middle(layer, frame, stream, context, latent):
@@ -380,7 +523,7 @@
         scaled, _ = norm_parts(one)
         cell = (scaled * gain(layer, 2)).astype(BF16)
         cell_ref[layer, at] = cell
-        preact = dot(cell, recurrent_low[layer, :WIDTH]) + dot(latent, recurrent_low[layer, WIDTH:])
+        preact = dot_nt(cell, recurrent_low[layer, :, :WIDTH]) + dot_nt(latent, recurrent_low[layer, :, WIDTH:])
         tangent = jnp.tanh(preact)
         tangent_ref[layer, at] = tangent
         state = tangent.astype(BF16)
@@ -424,9 +567,9 @@
         gpre = (dstate * (1.0 - tangent * tangent)).astype(BF16)
         gpre_ref[at] = gpre
         if layer > 0:
-            gstate_ref[at] = dot_nt(gpre, recurrent_low[layer, WIDTH:])
+            gstate_ref[at] = dot(gpre, recurrent_low[layer, :, WIDTH:])
         scaled, inverse = norm_parts(stream_one[layer, at])
-        dcell = dot_nt(gpre, recurrent_low[layer, :WIDTH])
+        dcell = dot(gpre, recurrent_low[layer, :, :WIDTH])
         part, change = norm_back(dcell, gain(layer, 2), scaled, inverse)
         gain_sums[layer, 2] += part
         g = g + change
@@ -467,24 +610,20 @@
         for block in range(HIDDEN // WIDTH):
             cols = slice(block * WIDTH, (block + 1) * WIDTH)
             put_rows(
-                SHRINK_AT[layer], HIDDEN, block * WIDTH, dot_tn(active_ref[layer, :, cols], gm_ref[...])
+                places.shrink[layer], HIDDEN, block * WIDTH, dot_tn(active_ref[layer, :, cols], gm_ref[...])
             )
         for block in range(HIDDEN // WIDTH):
             cols = slice(block * WIDTH, (block + 1) * WIDTH)
             put_blocks(
-                EXPAND_AT[layer] + 2 * block * WIDTH, dot_tn(hidden_ref[layer], slope_ref[layer, :, cols])
+                places.expand[layer] + 2 * block * WIDTH, dot_tn(hidden_ref[layer], slope_ref[layer, :, cols])
             )
 
     def small_grads(layer, latent):
-        low = dot_tn(cell_ref[layer], gpre_ref[...])
-        high = dot_tn(latent, gpre_ref[...])
-        recurrent = jnp.concatenate([low, high], axis=0)
-        quarter = recurrent.shape[0] // 4
-        recurrent = jnp.concatenate(
-            [recurrent[i * quarter : (i + 1) * quarter] for i in range(4)], axis=1
-        )
+        near = dot_tn(gpre_ref[...], cell_ref[layer])
+        far = dot_tn(gpre_ref[...], latent)
+        far = jnp.concatenate([far, jnp.zeros((LATENT, LANES - LATENT), F32)], axis=1)
         readout = dot_tn(state_ref[layer], gl_ref[...])
-        return [recurrent, readout[:, :LANES], readout[:, LANES:]]
+        return [near[:, :LANES], near[:, LANES:], far, readout[:, :LANES], readout[:, LANES:]]
 
     def put_small(layer, pieces):
         table = table_of_bias(gathered_ref[layer], onehot_ref[layer])
@@ -496,22 +635,33 @@
         pieces = pieces + [table[:, :LANES], table[:, LANES:], gains[:, :LANES], gains[:, LANES:]]
         used = sum(piece.shape[0] for piece in pieces)
         pieces = pieces + [jnp.zeros((SMALL_ROWS - used, LANES), F32)]
-        grads_ref[SMALL_AT[layer] : SMALL_AT[layer] + SMALL_ROWS] = jnp.concatenate(
+        grads_ref[places.small[layer] : places.small[layer] + SMALL_ROWS] = jnp.concatenate(
             pieces, axis=0
         ).astype(BF16)
 
     def output_grads(layer):
-        put_blocks(OUTPUT_AT[layer], dot_tn(context_ref[layer], gc_ref[...]))
+        put_blocks(places.output[layer], dot_tn(context_ref[layer], gc_ref[...]))
 
     def triple_grads(layer):
         for block in range(3):
             cols = slice(block * WIDTH, (block + 1) * WIDTH)
             put_blocks(
-                TRIPLE_AT[layer] + 2 * block * WIDTH, dot_tn(normed_ref[layer], dpacked_ref[:, cols])
+                places.triple[layer] + 2 * block * WIDTH, dot_tn(normed_ref[layer], dpacked_ref[:, cols])
             )
 
-    def loop(body):
-        lax.fori_loop(0, frame_count, lambda frame, unused: body(frame), None)
+    def loop(body, steps=()):
+        def whole(frame, unused):
+            body(frame)
+            for after in range(frame_count):
+                here = [(section, phase) for when, section, phase in steps if when == after]
+                if here:
+
+                    @pl.when(frame == after)
+                    def _(here=here):
+                        for section, phase in here:
+                            sum_step(section, phase)
+
+        lax.fori_loop(0, frame_count, whole, None)
 
     def first_layer(frame):
         at = span(frame)
@@ -549,6 +699,7 @@
 
     loop(second_middle)
     feed_grads(1)
+    sum_start(FEED_ONE, 0)
     output_grads(1)
     small_one = small_grads(1, state_ref[0])
 
@@ -560,8 +711,9 @@
         dcontext_ref[at] = dnormed.astype(BF16)
         send_halo(3, frame, dnormed)
 
-    loop(second_back)
+    loop(second_back, ((0, FEED_ONE, 0), (3, FEED_ONE, 1)))
     triple_grads(1)
+    sum_start(ATTEND_ONE, 0)
 
     def first_middle_back(frame):
         at = span(frame)
@@ -569,9 +721,19 @@
         g = stream_back(1, frame, g_ref[at], stream_in[at], dnormed)
         dcontext_ref[at] = middle_back(0, frame, g, gstate_ref[at]).astype(BF16)
 
-    loop(first_middle_back)
+    loop(
+        first_middle_back,
+        (
+            (0, ATTEND_ONE, 0),
+            (1, FEED_ONE, 2),
+            (2, ATTEND_ONE, 1),
+            (2, FEED_ONE, 3),
+            (3, ATTEND_ONE, 2),
+        ),
+    )
+    feed_grads(0)
+    sum_start(FEED_ZERO, 0)
     put_small(1, small_one)
-    feed_grads(0)
     output_grads(0)
     small_zero = small_grads(0, latent_ref[...])
 
@@ -581,18 +743,45 @@
         stream = frames_ref[at].astype(F32)
         input_grad_ref[at] = stream_back(0, frame, g_ref[at], stream, dnormed)
 
-    loop(first_back)
+    loop(
+        first_back,
+        (
+            (0, FEED_ZERO, 0),
+            (0, ATTEND_ONE, 3),
+            (1, FEED_ONE, 4),
+            (2, ATTEND_ONE, 4),
+            (3, FEED_ZERO, 1),
+        ),
+    )
     triple_grads(0)
     put_small(0, small_zero)
+    sum_start(ATTEND_ZERO, 0)
+    for section, phase in (
+        (FEED_ONE, 5),
+        (ATTEND_ONE, 5),
+        (ATTEND_ZERO, 0),
+        (FEED_ZERO, 2),
+        (ATTEND_ZERO, 1),
+        (FEED_ZERO, 3),
+        (ATTEND_ZERO, 2),
+        (FEED_ZERO, 4),
+        (ATTEND_ZERO, 3),
+        (FEED_ZERO, 5),
+        (ATTEND_ZERO, 4),
+        (ATTEND_ZERO, 5),
+    ):
+        sum_step(section, phase)
 
     def drain(frame, unused):
         for exchange in range(4):
             halo(exchange, frame).wait_send()
 
     lax.fori_loop(0, frame_count, drain, None)
-
-
-def layers_step(frames, latent, crop_band, cotangent, weights, lon_count):
+    for section in range(len(places.rows)):
+        sum_drain(section)
+
+
+def layers_step(frames, latent, crop_band, cotangent, weights, lon_count, batch_count, places):
     frame_count, row_count, col_count, features = frames.shape
     count = frame_count * row_count * col_count
     tokens = row_count * col_count
@@ -601,12 +790,14 @@
     both = lambda *shape: pltpu.VMEM((LAYERS,) + shape, BF16)
     one = lambda *shape: pltpu.VMEM(shape, BF16)
     wide = lambda *shape: pltpu.VMEM(shape, F32)
+    line_count = batch_count // 2
+    sections = len(places.rows)
     scratch = [
         both(WIDTH, 3 * WIDTH),
         both(WIDTH, WIDTH),
         both(WIDTH, HIDDEN),
         both(HIDDEN, WIDTH),
-        both(WIDTH + LATENT, LATENT),
+        both(LATENT, WIDTH + LATENT),
         both(LATENT, WIDTH),
         wide(HEADS, WIDTH),
         wide(LAYERS, SPAN, HEADS * SPAN),
@@ -636,80 +827,200 @@
         one(count, 3 * WIDTH),
         one(4, frame_count, tokens // 2, WIDTH),
         one(4, frame_count, tokens // 2, WIDTH),
+        one(places.total, LANES),
+        one(places.total, LANES),
+        one(places.total // 2, LANES),
+        one(places.total // 2 // lon_count * (lon_count - 1), LANES),
+        one(places.total // 2 // lon_count // line_count * (line_count - 1), LANES),
         pltpu.SemaphoreType.DMA((4, frame_count)),
         pltpu.SemaphoreType.DMA((4, frame_count)),
+        pltpu.SemaphoreType.DMA((sections, 2 * (lon_count + line_count - 1))),
+        pltpu.SemaphoreType.DMA((sections, 2 * (lon_count + line_count - 1))),
+        pltpu.SemaphoreType.DMA((sections,)),
     ]
     return pl.pallas_call(
-        functools.partial(kernel, lon_count),
+        functools.partial(kernel, lon_count, batch_count, places),
         out_shape=(
             jax.ShapeDtypeStruct((count, WIDTH), BF16),
             jax.ShapeDtypeStruct((count, WIDTH), F32),
-            jax.ShapeDtypeStruct((GRAD_ROWS, LANES), BF16),
+            jax.ShapeDtypeStruct((places.total, LANES), BF16),
         ),
         in_specs=[pl.BlockSpec(memory_space=pltpu.SMEM)] + [vmem] * (3 + len(weights)),
-        out_specs=(vmem, vmem, vmem),
+        out_specs=(vmem, vmem, pl.BlockSpec(memory_space=pl.ANY)),
         scratch_shapes=scratch,
         compiler_params=pltpu.CompilerParams(
             collective_id=0, has_side_effects=True, vmem_limit_bytes=60 * 1024 * 1024
         ),
         name="swin_step",
-    )(crop_band, flat(frames), flat(latent), flat(cotangent), *weights)
-
-
-def update(weight, moment, average, gradient):
-    velocity = MOMENTUM_RATE * moment + gradient
-    updated = weight - LEARN_RATE * (gradient + MOMENTUM_RATE * velocity)
-    smoothed = AVERAGE_DECAY * average + (1.0 - AVERAGE_DECAY) * updated
-    return (updated, velocity, smoothed)
-
-
-def unblock(rows, shape):
-    height, width = shape
-    return rows.reshape(width // LANES, height, LANES).transpose(1, 0, 2).reshape(shape)
-
-
-def split_grads(grads):
-    def at(start, shape):
-        count = shape[0] * shape[1] // LANES
-        return unblock(grads[start : start + count], shape)
-
-    def expand_at(start, blocks):
-        return jnp.concatenate([at(start + 512 * i, (WIDTH, WIDTH)) for i in range(blocks)], axis=1)
-
-    out = []
-    for layer in range(LAYERS):
-        small = grads[SMALL_AT[layer] : SMALL_AT[layer] + SMALL_ROWS]
-        recurrent = jnp.concatenate(
-            [small[:72, i * LATENT : (i + 1) * LATENT] for i in range(4)], axis=0
-        )
-        out.append(
-            (
-                expand_at(TRIPLE_AT[layer], 3),
-                at(OUTPUT_AT[layer], (WIDTH, WIDTH)),
-                expand_at(EXPAND_AT[layer], 4),
-                at(SHRINK_AT[layer], (HIDDEN, WIDTH)),
-                recurrent,
-                unblock(small[72:136], (LATENT, WIDTH)),
-                unblock(small[152:168], (8, WIDTH))[:3],
-                unblock(small[136:152], (HEADS, WIDTH))[:, :PAIRS],
+    )(crop_band.T, flat(frames), flat(latent), flat(cotangent), *weights)
+
+
+def update_kernel(scale, places, sums_hbm, result_hbm, grad_hbm, *refs):
+    count = 24
+    given, result_out, grad_out = refs[:count], refs[count], refs[count + 1]
+    made = refs[count + 2 : 2 * count + 2]
+    sums, held = refs[2 * count + 2], refs[2 * count + 3 : 3 * count + 3]
+    sums_sem, pass_sem, in_sem, out_sem = refs[3 * count + 3 :]
+    triple, output, expand, shrink, recurrent, readout, gains, table = range(8)
+
+    passing = [
+        pltpu.make_async_copy(result_hbm, result_out, pass_sem.at[0]),
+        pltpu.make_async_copy(grad_hbm, grad_out, pass_sem.at[1]),
+    ]
+    units = [
+        (FEED_ONE, expand, 1),
+        (FEED_ONE, shrink, 1),
+        (ATTEND_ONE, output, 1),
+        (ATTEND_ONE, triple, 1),
+        (FEED_ZERO, expand, 0),
+        (FEED_ZERO, shrink, 0),
+        (ATTEND_ZERO, output, 0),
+        (ATTEND_ZERO, triple, 0),
+        (ATTEND_ZERO, recurrent, None),
+        (ATTEND_ZERO, readout, None),
+        (ATTEND_ZERO, gains, None),
+        (ATTEND_ZERO, table, None),
+    ]
+
+    def part(ref, layer):
+        return ref if layer is None else ref.at[layer]
+
+    def coming(index):
+        section, which, layer = units[index]
+        return [
+            pltpu.make_async_copy(
+                part(given[3 * which + i], layer), part(held[3 * which + i], layer), in_sem.at[index, i]
             )
-        )
-    return [jnp.stack(pair) for pair in zip(*out)]
+            for i in range(3)
+        ]
+
+    def going(index):
+        section, which, layer = units[index]
+        return [
+            pltpu.make_async_copy(
+                part(held[3 * which + i], layer), part(made[3 * which + i], layer), out_sem.at[index, i]
+            )
+            for i in range(3)
+        ]
+
+    def sums_in(section):
+        rows = pl.ds(places.starts[section], places.rows[section])
+        return pltpu.make_async_copy(sums_hbm.at[rows], sums.at[rows], sums_sem.at[section])
+
+    begun = set()
+    for index, (section, which, layer) in enumerate(units):
+        if section not in begun:
+            begun.add(section)
+            sums_in(section).start()
+        for copy in coming(index):
+            copy.start()
+    for copy in passing:
+        copy.start()
+
+    def change(which, at, summed):
+        weight, moment, average = held[3 * which : 3 * which + 3]
+        gradient = summed.astype(F32) * scale
+        velocity = MOMENTUM_RATE * moment[at] + gradient
+        updated = weight[at] - LEARN_RATE * (gradient + MOMENTUM_RATE * velocity)
+        average[at] = AVERAGE_DECAY * average[at] + (1.0 - AVERAGE_DECAY) * updated
+        weight[at] = updated
+        moment[at] = velocity
+
+    def change_blocks(which, layer, start, rows, cols):
+        step = 64
+
+        def body(i, unused):
+            row = pl.multiple_of(i * step, step)
+            for block in range(cols // LANES):
+                summed = sums[pl.ds(start + block * rows + row, step)]
+                change(which, (layer, pl.ds(row, step), half_lanes(block)), summed)
+
+        lax.fori_loop(0, rows // step, body, None)
+
+    for index, (section, which, layer) in enumerate(units):
+        if section in begun:
+            begun.remove(section)
+            sums_in(section).wait()
+        for copy in coming(index):
+            copy.wait()
+        if which == expand:
+            change_blocks(expand, layer, places.expand[layer], WIDTH, HIDDEN)
+        elif which == shrink:
+            change_blocks(shrink, layer, places.shrink[layer], HIDDEN, WIDTH)
+        elif which == output:
+            change_blocks(output, layer, places.output[layer], WIDTH, WIDTH)
+        elif which == triple:
+            change_blocks(triple, layer, places.triple[layer], WIDTH, 3 * WIDTH)
+        else:
+            for each in range(LAYERS):
+                at = places.small[each]
+                if which == recurrent:
+                    for block in range(3):
+                        lanes = slice(block * LANES, min((block + 1) * LANES, WIDTH + LATENT))
+                        rows = sums[pl.ds(at + block * LATENT, LATENT)]
+                        change(which, (each, slice(0, LATENT), lanes), rows[:, : lanes.stop - lanes.start])
+                elif which == readout:
+                    for block in range(2):
+                        rows = sums[pl.ds(at + 96 + block * LATENT, LATENT)]
+                        change(which, (each, slice(0, LATENT), half_lanes(block)), rows)
+                else:
+                    rows = sums[pl.ds(at + 160, 32)].astype(F32)
+                    if which == table:
+                        change(which, (each, slice(0, HEADS), slice(0, LANES)), rows[:8])
+                        change(which, (each, slice(0, HEADS), slice(LANES, PAIRS)), rows[8:16, : PAIRS - LANES])
+                    else:
+                        for norm in range(3):
+                            for block in range(2):
+                                row = 16 + block * 8 + norm
+                                at_one = (norm, slice(each, each + 1), half_lanes(block))
+                                change(which, at_one, rows[row : row + 1])
+        for copy in going(index):
+            copy.start()
+    for index in range(len(units)):
+        for copy in going(index):
+            copy.wait()
+    for copy in passing:
+        copy.wait()
+
+
+def update_step(sums, result, input_grad, parameters, scale, places):
+    anywhere = pl.BlockSpec(memory_space=pl.ANY)
+    like = lambda a: jax.ShapeDtypeStruct(a.shape, a.dtype)
+    return pl.pallas_call(
+        functools.partial(update_kernel, scale, places),
+        out_shape=(like(result), like(input_grad)) + tuple(like(a) for a in parameters),
+        in_specs=[anywhere] * (3 + len(parameters)),
+        out_specs=(anywhere,) * (2 + len(parameters)),
+        scratch_shapes=[pltpu.VMEM(sums.shape, BF16)]
+        + [pltpu.VMEM(a.shape, F32) for a in parameters]
+        + [
+            pltpu.SemaphoreType.DMA((len(places.rows),)),
+            pltpu.SemaphoreType.DMA((2,)),
+            pltpu.SemaphoreType.DMA((12, 3)),
+            pltpu.SemaphoreType.DMA((12, 3)),
+        ],
+        compiler_params=pltpu.CompilerParams(vmem_limit_bytes=48 * 1024 * 1024),
+        name="nesterov_step",
+    )(sums, result, input_grad, *parameters)
 
 
 def per_device(frames, latent_init, crop_band, cotangent, *parameters):
-    weights, moments, averages = parameters[0::3], parameters[1::3], parameters[2::3]
     shape = frames.shape
-    result, input_grad, grads = layers_step(
-        frames, latent_init, crop_band, cotangent, weights, lax.axis_size("lon")
+    lon_count, batch_count = lax.axis_size("lon"), lax.axis_size("batch")
+    places = Places(lon_count * batch_count)
+    turned = {4: (0, 2, 1), 6: (1, 0, 2)}
+    parameters = [
+        a.transpose(turned[i // 3]) if i // 3 in turned else a for i, a in enumerate(parameters)
+    ]
+    result, input_grad, sums = layers_step(
+        frames, latent_init, crop_band, cotangent, parameters[0::3], lon_count, batch_count, places
     )
-    grads = lax.psum(grads, ("lon", "batch")).astype(F32)
-    tokens = shape[0] * shape[1] * shape[2] * lax.axis_size("lon") * lax.axis_size("batch")
-    scale = float(tokens) ** (-0.5)
-    outs = [result.reshape(shape), input_grad.reshape(shape)]
-    for weight, moment, average, gradient in zip(weights, moments, averages, split_grads(grads)):
-        outs.extend(update(weight, moment, average, gradient * scale))
-    return tuple(outs)
+    tokens = shape[0] * shape[1] * shape[2] * lon_count * batch_count
+    result, input_grad, *updated = update_step(
+        sums, result, input_grad, parameters, float(tokens) ** (-0.5), places
+    )
+    updated = [a.transpose(turned[i // 3]) if i // 3 in turned else a for i, a in enumerate(updated)]
+    return (result.reshape(shape), input_grad.reshape(shape), *updated)
 
 
 def solution(mesh):

time: 279 us -> 121 us (0.43)
  waiting for transfers between devices: 139 us -> 0 us
  Pallas kernels: 65.8 us -> 117 us
  local copies, waits for them, and re-layouts: 44.1 us -> 2.33 us
  other arithmetic: 15.1 us -> 0 us
  between operations: 14.7 us -> 1.11 us
    psum x1 -> x0, waiting for transfers between devices: 139 us -> none  [per_device(): grads = lax.psum(grads, ('lon', 'batch')).astype(F32)]
    pallas_call x1 -> x2, Pallas kernels: 65.8 us -> 117 us  [the longest x1 103 us: layers_step(): pl.pallas_call(functools.partial(kernel, lon_count, batch_count, places),...]
    add x8 -> x0, other arithmetic: 14.2 us -> none  [update(): smoothed = AVERAGE_DECAY * average + (1.0 - AVERAGE_DECAY) * updated]
    slice x16 -> x0, local copies, waits for them, and re-layouts: 12.3 us -> none  [the longest x9 5.86 us: split_grads(): small[:72, i * LATENT:(i + 1) * LATENT]]
    another operation x7 -> x0, local copies, waits for them, and re-layouts: 9.14 us -> none  [split_grads(): return [jnp.stack(pair) for pair in zip(*out)]]
    transpose x6 -> x0, local copies, waits for them, and re-layouts: 8.43 us -> none  [unblock(): rows.reshape(width // LANES, height, LANES).transpose(1, 0, 2)]
    unnamed x107 -> x36, local copies, waits for them, and re-layouts: 9.86 us -> 2.33 us
    reshape x9 -> x0, local copies, waits for them, and re-layouts: 4.43 us -> none  [unblock(): rows.reshape(width // LANES, height, LANES).transpose(1, 0, 2)]
  transfers between devices with their start and end apart: 1 -> 0, of which waited for: 1 -> 0; matrix products, arithmetic and copies ran while one was open for 0% -> 0% of each run, Pallas kernels for 0% -> 0%
where the time goes in v2:
time: 121 us; the launch traced here: 120 us
  Pallas kernels  117 us (97%)
  local copies, waits for them, and re-layouts  2.33 us (2%)
    pallas_call x1, Pallas kernels, layers_step(): pl.pallas_call(functools.partial(kernel, lon_count, batch_count, places),...  103 us
    pallas_call x1, Pallas kernels, update_step(): pl.pallas_call(functools.partial(update_kernel, scale, places), out_shape...  13.7 us

profile of v2, /device:TPU:0, one launch (start us, length us, event | category | flops | bytes accessed | tf_op | source)
XLA Modules:
  0.0 120.1 jit_solution(13184888685636821594)
XLA Ops:
  0.7 0.0 copy-start
  0.7 0.0 copy-start.1
  0.7 0.0 copy-start.3
  0.7 0.0 copy-start.4
  0.7 0.0 copy-start.6
  0.7 0.0 copy-start.7
  0.7 0.0 copy-start.8
  0.7 0.0 copy-start.9
  0.8 0.0 copy-start.10
  0.8 0.0 copy-start.11
  0.8 0.0 copy-start.12
  0.8 0.0 copy-start.13
  0.8 0.0 copy-start.14
  0.8 0.0 copy-start.15
  0.8 0.0 copy-start.16
  0.8 0.0 copy-start.17
  0.8 103.0 %swin_step.1 = (bf16[1024,256]{1,0:T(8,128)(2,1)}, f32[1024,256]{1,0:T(8,128)}, bf16[12800,128]{1,0:T(8,128)(2,1)}) custom-call(s32[2,4]{1,0:T(2,128)} %bitcast.29, bf16[1024,256]{1,0:T(8,128)(2,1)} %bitcast.26, bf16[1024,32]{1,0:T(8,128)(2,1)} %bitcast.28, bf16[1024,256]{1,0:T(8,128)(2,1)} %bitcast.27, f32[2,256,768]{2,1,0:T(8,128)} %refs_0_.1, ...), custom_call_target="tpu_custom_call" | custom-call | tf_op jit(solution)/shard_map/swin_step/pallas_call | solution.py:841
  103.8 0.0 copy-done
  103.8 0.0 copy-done.1
  103.8 0.0 copy-done.3
  103.8 0.0 copy-done.4
  103.9 0.0 copy-done.6
  103.9 0.0 copy-done.7
  103.9 0.0 copy-done.8
  103.9 0.0 copy-done.9
  103.9 0.0 copy-done.10
  103.9 0.0 copy-done.11
  103.9 0.0 copy-done.12
  103.9 0.0 copy-done.13
  104.0 1.2 %copy-done.2 = f32[1024,256]{1,0:T(8,128)S(1)} copy-done((f32[1024,256]{1,0:T(8,128)S(1)}, f32[1024,256]{1,0:T(8,128)}, u32[]{:S(2)}) %copy-start.2) | copy-done | bytes 1048600
  105.2 1.0 copy-done.5
  106.2 13.7 %nesterov_step.1 = (bf16[1024,256]{1,0:T(8,128)(2,1)}, f32[1024,256]{1,0:T(8,128)}, f32[2,256,768]{2,1,0:T(8,128)}, f32[2,256,768]{2,1,0:T(8,128)}, f32[2,256,76...) custom-call(bf16[12800,128]{1,0:T(8,128)(2,1)} %get-tuple-element.55, ...), custom_call_target="tpu_custom_call" | custom-call | tf_op jit(solution)/shard_map/nesterov_step/pallas_call | solution.py:989
  (6 shorter events, 0.0 us)
Async XLA Ops:
  0.7 103.1 %copy-start = (f32[2,256,768]{2,1,0:T(8,128)S(1)}, f32[2,256,768]{2,1,0:T(8,128)}, u32[]{:S(2)}) copy-start(f32[2,256,768]{2,1,0:T(8,128)} %refs_0_.1) | copy-start | bytes 4718596
  0.7 103.1 %copy-start.1 = (f32[2,256,256]{2,1,0:T(8,128)S(1)}, f32[2,256,256]{2,1,0:T(8,128)}, u32[]{:S(2)}) copy-start(f32[2,256,256]{2,1,0:T(8,128)} %refs_3_.1) | copy-start | bytes 1572868
  0.7 103.1 %copy-start.3 = (f32[2,256,256]{2,1,0:T(8,128)S(1)}, f32[2,256,256]{2,1,0:T(8,128)}, u32[]{:S(2)}) copy-start(f32[2,256,256]{2,1,0:T(8,128)} %refs_4_.1) | copy-start | bytes 1572868
  0.7 103.1 %copy-start.4 = (f32[2,256,256]{2,1,0:T(8,128)S(1)}, f32[2,256,256]{2,1,0:T(8,128)}, u32[]{:S(2)}) copy-start(f32[2,256,256]{2,1,0:T(8,128)} %refs_5_.1) | copy-start | bytes 1572868
  0.7 103.1 %copy-start.6 = (f32[2,288,32]{1,2,0:T(8,128)S(1)}, f32[2,288,32]{1,2,0:T(8,128)}, u32[]{:S(2)}) copy-start(f32[2,288,32]{1,2,0:T(8,128)} %param.44) | copy-start | bytes 221188
  0.7 103.1 %copy-start.7 = (f32[2,32,256]{2,1,0:T(8,128)S(1)}, f32[2,32,256]{2,1,0:T(8,128)}, u32[]{:S(2)}) copy-start(f32[2,32,256]{2,1,0:T(8,128)} %refs_15_.1) | copy-start | bytes 196612
  0.7 103.1 %copy-start.8 = (f32[2,288,32]{1,2,0:T(8,128)S(1)}, f32[2,288,32]{1,2,0:T(8,128)}, u32[]{:S(2)}) copy-start(f32[2,288,32]{1,2,0:T(8,128)} %param.45) | copy-start | bytes 221188
  0.7 103.1 %copy-start.9 = (f32[2,288,32]{1,2,0:T(8,128)S(1)}, f32[2,288,32]{1,2,0:T(8,128)}, u32[]{:S(2)}) copy-start(f32[2,288,32]{1,2,0:T(8,128)} %param.46) | copy-start | bytes 221188
  0.8 103.1 %copy-start.10 = (f32[2,32,256]{2,1,0:T(8,128)S(1)}, f32[2,32,256]{2,1,0:T(8,128)}, u32[]{:S(2)}) copy-start(f32[2,32,256]{2,1,0:T(8,128)} %refs_16_.1) | copy-start | bytes 196612
  0.8 103.1 %copy-start.11 = (f32[2,32,256]{2,1,0:T(8,128)S(1)}, f32[2,32,256]{2,1,0:T(8,128)}, u32[]{:S(2)}) copy-start(f32[2,32,256]{2,1,0:T(8,128)} %refs_17_.1) | copy-start | bytes 196612
  0.8 103.1 %copy-start.12 = (f32[2,8,225]{2,1,0:T(8,128)S(1)}, f32[2,8,225]{2,1,0:T(8,128)}, u32[]{:S(2)}) copy-start(f32[2,8,225]{2,1,0:T(8,128)} %refs_21_.1) | copy-start | bytes 43204
  0.8 103.1 %copy-start.13 = (f32[2,3,256]{2,0,1:T(2,128)S(1)}, f32[2,3,256]{2,0,1:T(2,128)}, u32[]{:S(2)}) copy-start(f32[2,3,256]{2,0,1:T(2,128)} %param.50) | copy-start | bytes 18436
  0.8 103.1 %copy-start.14 = (f32[2,8,225]{2,1,0:T(8,128)S(1)}, f32[2,8,225]{2,1,0:T(8,128)}, u32[]{:S(2)}) copy-start(f32[2,8,225]{2,1,0:T(8,128)} %refs_22_.1) | copy-start | bytes 43204
  0.8 103.1 %copy-start.15 = (f32[2,8,225]{2,1,0:T(8,128)S(1)}, f32[2,8,225]{2,1,0:T(8,128)}, u32[]{:S(2)}) copy-start(f32[2,8,225]{2,1,0:T(8,128)} %refs_23_.1) | copy-start | bytes 43204
  0.8 103.1 %copy-start.16 = (f32[2,3,256]{2,0,1:T(2,128)S(1)}, f32[2,3,256]{2,0,1:T(2,128)}, u32[]{:S(2)}) copy-start(f32[2,3,256]{2,0,1:T(2,128)} %param.51) | copy-start | bytes 18436
  0.8 103.1 %copy-start.17 = (f32[2,3,256]{2,0,1:T(2,128)S(1)}, f32[2,3,256]{2,0,1:T(2,128)}, u32[]{:S(2)}) copy-start(f32[2,3,256]{2,0,1:T(2,128)} %param.52) | copy-start | bytes 18436
  104.0 1.2 %copy-start.2 = (f32[1024,256]{1,0:T(8,128)S(1)}, f32[1024,256]{1,0:T(8,128)}, u32[]{:S(2)}) copy-start(f32[1024,256]{1,0:T(8,128)} %get-tuple-element.57.grad_hbm) | copy-start | bytes 3145732
  105.2 1.0 copy-start.5

commit v3 on v1

v3 whole, which is shorter than its diff:
```python
import functools
import math

import jax
import jax.numpy as jnp
from jax import lax
from jax.experimental import pallas as pl
from jax.experimental.pallas import tpu as pltpu
from jax.sharding import PartitionSpec as P

WINDOW = 8
HALF = WINDOW // 2
SPAN = WINDOW * WINDOW
HEADS = 8
LANES = 128
LAYERS = 2
WIDTH = 256
HIDDEN = 1024
LATENT = 32
OFFSETS = 2 * WINDOW - 1
PAIRS = OFFSETS * OFFSETS

LEARN_RATE = 0.2
MOMENTUM_RATE = 0.9
AVERAGE_DECAY = 0.5
NORM_EPS = 1e-05
MASK_FILL = -100.0
HEAD_WIDTH = WIDTH // HEADS
HEADS_A_HALF = LANES // HEAD_WIDTH
SCALE = HEAD_WIDTH ** (-0.5)
GELU_C = 0.7978845608028654
GELU_A = 0.044715

F32 = jnp.float32
BF16 = jnp.bfloat16
MESH = pl.DeviceIdType.MESH

SMALL_ROWS = 256
FEED_ROWS = HIDDEN * WIDTH // LANES
OUTPUT_ROWS = WIDTH * WIDTH // LANES
TRIPLE_ROWS = 3 * OUTPUT_ROWS
SHRINK_ONE, EXPAND_ONE, ATTEND_ONE, SHRINK_ZERO, EXPAND_ZERO, OUTPUT_ZERO, TRIPLE_ZERO = range(7)
SECTION_ROWS = (
    FEED_ROWS,
    FEED_ROWS,
    OUTPUT_ROWS + TRIPLE_ROWS,
    FEED_ROWS,
    FEED_ROWS,
    2 * OUTPUT_ROWS + LAYERS * SMALL_ROWS,
    2 * OUTPUT_ROWS,
)
ROW_TILE = 16
EARLY_ROWS = 5 * LATENT
TABLE_ROWS = 16


SECTION_PHASES = (
    ("core", "up", "line"),
    ("core", "down", "line"),
    ("core", "up", "line"),
    ("core", "lon", "line"),
    ("core", "lon", "line"),
    ("core", "lon", "line"),
    ("core", "both"),
)


class Places:
    def __init__(self, lon_count, batch_count):
        self.lon_count, self.line_count = lon_count, batch_count // 2
        self.ahead = lon_count * batch_count <= 32
        self.grant = (85 if self.ahead else 96) * 2**19
        unit = ROW_TILE * lon_count * batch_count
        few = self.few = unit <= 512
        self.few_members = lon_count * self.line_count if few else 1
        groups = [[i] for i in range(7)] if few else [[0, 1], [2], [3, 4], [5, 6]]
        self.leader = [group[-1] for group in groups for _ in group]
        self.first = [group[0] for group in groups for _ in group]
        self.rows, starts, at = {}, {}, 0
        for group in groups:
            begin = at
            for i in group:
                starts[i] = at
                at += SECTION_ROWS[i]
            rows = -(-(at - begin) // unit) * unit
            self.rows[group[-1]] = rows
            at = begin + rows
        self.total = at
        self.starts = starts
        self.phases, self.inbox, self.sems = {}, {}, {}
        bits = [1 << i for i in range(lon_count.bit_length() - 1)]
        inbox = 0
        for section, rows in self.rows.items():
            phases = []
            for name in SECTION_PHASES[section]:
                if name == "up":
                    phases += [("bit", bit, 2) for bit in bits]
                elif name == "down":
                    phases += [("bit", bit, 2) for bit in reversed(bits)]
                elif name == "both" and few:
                    phases.append((name, 0, lon_count * self.line_count))
                elif name == "both":
                    phases += [("lon", 0, lon_count), ("line", 0, self.line_count)]
                else:
                    phases.append((name, 0, {"core": 2, "lon": lon_count, "line": batch_count // 2}[name]))
            self.phases[section] = phases
            self.inbox[section], self.sems[section], sem = [], [], 0
            for _, _, members in phases:
                rows //= members
                self.inbox[section].append(inbox)
                self.sems[section].append(sem)
                inbox += rows * (members - 1)
                sem += members - 1
            for _, _, members in reversed(phases):
                self.sems[section].append(sem)
                sem += members - 1
        self.inbox_rows = inbox
        self.most_sems = max(2 * sum(m - 1 for _, _, m in phases) for phases in self.phases.values())
        self.shrink = (starts[SHRINK_ZERO], starts[SHRINK_ONE])
        self.expand = (starts[EXPAND_ZERO], starts[EXPAND_ONE])
        self.output = (starts[OUTPUT_ZERO], starts[ATTEND_ONE])
        self.triple = (
            (starts[TRIPLE_ZERO], starts[TRIPLE_ZERO] + OUTPUT_ROWS, starts[OUTPUT_ZERO] + OUTPUT_ROWS),
            tuple(starts[ATTEND_ONE] + i * OUTPUT_ROWS for i in (1, 2, 3)),
        )
        small = starts[OUTPUT_ZERO] + 2 * OUTPUT_ROWS
        self.early = (small, small + SMALL_ROWS)
        table = self.total if few else starts[TRIPLE_ZERO] + SECTION_ROWS[TRIPLE_ZERO]
        self.table = (table, small + SMALL_ROWS + EARLY_ROWS)
        self.sum_rows = self.total + (TABLE_ROWS if few else 0)
        self.spare = {}
        for section, rows in self.rows.items():
            begin = starts[self.first[section]]
            used = starts[section] + SECTION_ROWS[section]
            if section == TRIPLE_ZERO and not few:
                used += TABLE_ROWS
            self.spare[section] = (used, begin + rows)


def dot(a, b):
    return jnp.dot(a, b, preferred_element_type=F32)


def dot_nt(a, b):
    return lax.dot_general(a, b, (((1,), (1,)), ((), ())), preferred_element_type=F32)


def dot_tn(a, b):
    return lax.dot_general(a, b, (((0,), (0,)), ((), ())), preferred_element_type=F32)


def norm_parts(stream):
    center = stream - jnp.mean(stream, axis=-1, keepdims=True)
    inverse = lax.rsqrt(jnp.mean(center * center, axis=-1, keepdims=True) + NORM_EPS)
    return center * inverse, inverse


def norm_back(upstream, gain_row, scaled, inverse):
    weighted = upstream * gain_row
    along = jnp.mean(weighted * scaled, axis=-1, keepdims=True)
    return inverse * (weighted - jnp.mean(weighted, axis=-1, keepdims=True) - scaled * along)


def lower_slots(shape):
    return lax.broadcasted_iota(jnp.int32, shape, 1) < HALF


def pack_half(own):
    tokens, features = own.shape
    rows = own.reshape(tokens // WINDOW, WINDOW, features)
    count = tokens // WINDOW // 2
    moved = pltpu.roll(rows[count:], HALF, axis=1)
    return jnp.where(lower_slots(moved.shape), rows[:count], moved).reshape(tokens // 2, features)


def unpack_half(packed, own):
    tokens, features = own.shape
    pairs = packed.reshape(tokens // WINDOW // 2, WINDOW, features)
    full = jnp.concatenate([pairs, pltpu.roll(pairs, HALF, axis=1)], axis=0)
    rows = own.reshape(tokens // WINDOW, WINDOW, features)
    return jnp.where(lower_slots(full.shape), full, rows).reshape(tokens, features)


def rows_ahead(value):
    cut = HALF * WINDOW
    return jnp.concatenate([value[cut:], value[:cut]], axis=0)


def rows_behind(value):
    cut = value.shape[0] - HALF * WINDOW
    return jnp.concatenate([value[cut:], value[:cut]], axis=0)


def head_of_lane(shape):
    return lax.broadcasted_iota(jnp.int32, shape, 1) // HEAD_WIDTH


def spread_heads(block):
    lane_head = head_of_lane(block.shape)
    zero = jnp.zeros_like(block)
    return jnp.concatenate(
        [jnp.where(lane_head == head, block, zero) for head in range(HEADS_A_HALF)], axis=0
    )


def gather_heads(stacked):
    count = stacked.shape[0] // HEADS_A_HALF
    lane_head = head_of_lane((count, LANES))
    out = stacked[:count]
    for head in range(1, HEADS_A_HALF):
        out = jnp.where(lane_head == head, stacked[head * count : (head + 1) * count], out)
    return out


def half_lanes(half):
    return slice(half * LANES, (half + 1) * LANES)


def half_scores(half):
    return slice(half * HEADS_A_HALF * SPAN, (half + 1) * HEADS_A_HALF * SPAN)


def score_mask(crop_start, crop_end, shifted, window, row_count):
    shape = (SPAN, HEADS_A_HALF * SPAN)
    key_row = lax.broadcasted_iota(jnp.int32, shape, 0) // WINDOW
    source = key_row + window * WINDOW
    if shifted:
        source = source + HALF
        if window == row_count // WINDOW - 1:
            source = jnp.where(source >= row_count, source - row_count, source)
    allowed = (source >= crop_start) & (source < crop_end)
    if shifted and window == row_count // WINDOW - 1:
        query_row = lax.broadcasted_iota(jnp.int32, shape, 1) % SPAN // WINDOW
        allowed = allowed & ((key_row < HALF) == (query_row < HALF))
    return jnp.where(allowed, 0.0, MASK_FILL).astype(F32)


def offset_onehot(shifted):
    shape = (WINDOW * LANES, WIDTH)
    row = lax.broadcasted_iota(jnp.int32, shape, 0)
    key_col = row // LANES
    row_offset = row % LANES // WINDOW
    query_col = row % WINDOW
    if shifted:
        key_col = (key_col + HALF) % WINDOW
        query_col = (query_col + HALF) % WINDOW
    target = row_offset * OFFSETS + query_col - key_col + WINDOW - 1
    target = jnp.where(row_offset < OFFSETS, target, -1)
    pair = lax.broadcasted_iota(jnp.int32, shape, 1)
    return jnp.where(pair == target, 1.0, 0.0).astype(BF16)


def three_parts(value):
    high = value.astype(BF16)
    rest = value - high.astype(F32)
    middle = rest.astype(BF16)
    low = (rest - middle.astype(F32)).astype(BF16)
    return jnp.concatenate([high.astype(F32), middle.astype(F32), low.astype(F32)], axis=0).astype(BF16)


def swap_groups(tiles):
    return [jnp.concatenate([tile[b : b + 1] for tile in tiles], axis=0) for b in range(8)]


def bias_of_table(table, onehot):
    spread = dot_nt(three_parts(table), onehot)
    spread = spread[:HEADS] + (spread[HEADS : 2 * HEADS] + spread[2 * HEADS :])
    tiles = swap_groups([spread[:, col * LANES : (col + 1) * LANES] for col in range(WINDOW)])
    lane = lax.broadcasted_iota(jnp.int32, (WINDOW, LANES), 1)
    blocks = []
    for key_row in range(WINDOW):
        back = (WINDOW - 1 - key_row) * WINDOW
        pieces = []
        for pair in range(HEADS // 2):
            even = pltpu.roll(tiles[2 * pair], (LANES - back) % LANES, axis=1)
            odd = pltpu.roll(tiles[2 * pair + 1], (LANES + SPAN - back) % LANES, axis=1)
            pieces.append(jnp.where(lane < SPAN, even, odd))
        blocks.append(jnp.concatenate(pieces, axis=1))
    return jnp.concatenate(blocks, axis=0)


def table_of_bias(gathered, onehot):
    lane = lax.broadcasted_iota(jnp.int32, (WINDOW, LANES), 1)
    zero = jnp.zeros((WINDOW, LANES), F32)
    tiles = []
    for head in range(HEADS):
        total = None
        for key_row in range(WINDOW):
            forth = (WINDOW - 1 - key_row) * WINDOW
            block = gathered[key_row * WINDOW : (key_row + 1) * WINDOW, half_lanes(head // 2)]
            if head % 2 == 0:
                moved = pltpu.roll(jnp.where(lane < SPAN, block, zero), forth, axis=1)
            else:
                moved = pltpu.roll(jnp.where(lane < SPAN, zero, block), (forth + SPAN) % LANES, axis=1)
            total = moved if total is None else total + moved
        tiles.append(total)
    spread = jnp.concatenate(swap_groups(tiles), axis=1)
    parts = dot(three_parts(spread), onehot)
    return parts[:HEADS] + (parts[HEADS : 2 * HEADS] + parts[2 * HEADS :])


def attend_forward(qkv, bias_ref, layer, crop, probs_ref, frame, row_count):
    shifted = layer % 2 == 1
    units = [(window, half) for window in range(row_count // WINDOW) for half in range(2)]
    piece = lambda which, window, half: qkv[
        window * SPAN : (window + 1) * SPAN, which * WIDTH + half * LANES : which * WIDTH + (half + 1) * LANES
    ]
    masks = [
        score_mask(crop[0], crop[1], shifted, window, row_count) for window in range(row_count // WINDOW)
    ]
    scores = [dot_nt(piece(1, *unit), spread_heads(piece(0, *unit))) for unit in units]
    probs = []
    for (window, half), score in zip(units, scores):
        score = score * SCALE + bias_ref[layer, :, half_scores(half)] + masks[window]
        exponent = jnp.exp(score - jnp.max(score, axis=0, keepdims=True))
        low = (exponent * (1.0 / jnp.sum(exponent, axis=0, keepdims=True))).astype(BF16)
        at = (frame * (row_count // WINDOW) + window) * SPAN
        probs_ref[layer, pl.ds(pl.multiple_of(at, SPAN), SPAN), half_scores(half)] = low
        probs.append(low)
    outs = [gather_heads(dot_tn(low, piece(2, *unit))) for unit, low in zip(units, probs)]
    return jnp.concatenate(
        [jnp.concatenate(outs[i : i + 2], axis=1) for i in range(0, len(outs), 2)], axis=0
    )


def value_grads(dcontext, layer, probs_ref, frame, row_count):
    windows = []
    for window in range(row_count // WINDOW):
        rows = slice(window * SPAN, (window + 1) * SPAN)
        at = (frame * (row_count // WINDOW) + window) * SPAN
        halves = []
        for half in range(2):
            low = probs_ref[layer, pl.ds(pl.multiple_of(at, SPAN), SPAN), half_scores(half)]
            halves.append(dot(low, spread_heads(dcontext[rows, half_lanes(half)])))
        windows.append(jnp.concatenate(halves, axis=1))
    return jnp.concatenate(windows, axis=0).astype(BF16)


def attend_backward(qkv, dcontext, layer, probs_ref, frame, gathered_ref, row_count):
    units = [(window, half) for window in range(row_count // WINDOW) for half in range(2)]
    piece = lambda which, window, half: qkv[
        window * SPAN : (window + 1) * SPAN, which * WIDTH + half * LANES : which * WIDTH + (half + 1) * LANES
    ]
    dprobs = [
        dot_nt(
            piece(2, window, half),
            spread_heads(dcontext[window * SPAN : (window + 1) * SPAN, half_lanes(half)]),
        )
        for window, half in units
    ]
    lows = []
    gathered = [None, None]
    for (window, half), dprob in zip(units, dprobs):
        at = (frame * (row_count // WINDOW) + window) * SPAN
        probs = probs_ref[layer, pl.ds(pl.multiple_of(at, SPAN), SPAN), half_scores(half)].astype(F32)
        dscores = probs * (dprob - jnp.sum(probs * dprob, axis=0, keepdims=True))
        gathered_ref[layer, :, half_scores(half)] += dscores
        lows.append(dscores.astype(BF16))
    dks = [dot(low, spread_heads(piece(0, *unit))) * SCALE for unit, low in zip(units, lows)]
    dqs = [gather_heads(dot_tn(low, piece(1, *unit))) * SCALE for unit, low in zip(units, lows)]
    return [
        jnp.concatenate(
            [jnp.concatenate(d[i : i + 2], axis=1) for i in range(0, len(d), 2)], axis=0
        ).astype(BF16)
        for d in (dqs, dks)
    ]


STEPS = {
    "second_middle_back": (),
    "second_back": (
        (0, SHRINK_ONE, 0),
        (0, EXPAND_ONE, 0),
        (2, SHRINK_ONE, 1),
        (2, EXPAND_ONE, 1),
    ),
    "first_feed_back": ((0, SHRINK_ONE, 2), (1, EXPAND_ONE, 2), (2, ATTEND_ONE, 0)),
    "after_shrink": (),
    "first_middle_back": (
        (0, SHRINK_ONE, 3),
        (0, ATTEND_ONE, 1),
        (1, EXPAND_ONE, 3),
        (2, SHRINK_ZERO, 0),
        (2, EXPAND_ZERO, 0),
        (3, ATTEND_ONE, 2),
    ),
    "after_output": ((SHRINK_ONE, 4), (EXPAND_ONE, 4)),
    "first_back": (
        (0, SHRINK_ZERO, 1),
        (0, OUTPUT_ZERO, 0),
        (0, ATTEND_ONE, 3),
        (1, SHRINK_ONE, 5),
        (1, EXPAND_ZERO, 1),
        (1, EXPAND_ONE, 5),
        (2, SHRINK_ZERO, 2),
        (2, ATTEND_ONE, 4),
        (3, SHRINK_ONE, 6),
        (3, OUTPUT_ZERO, 1),
        (3, EXPAND_ONE, 6),
        (3, EXPAND_ZERO, 2),
    ),
    "last_back": ((0, TRIPLE_ZERO, 0), (2, SHRINK_ZERO, 3), (3, EXPAND_ZERO, 3)),
    "last": (
        (OUTPUT_ZERO, 2),
        (ATTEND_ONE, 5),
        (SHRINK_ONE, 7),
        (EXPAND_ONE, 7),
        (TRIPLE_ZERO, 1),
        (OUTPUT_ZERO, 3),
        (SHRINK_ZERO, 4),
        (ATTEND_ONE, 6),
        (EXPAND_ZERO, 4),
        (ATTEND_ONE, 7),
        (OUTPUT_ZERO, 4),
        (TRIPLE_ZERO, 2),
        (SHRINK_ZERO, 5),
        (EXPAND_ZERO, 5),
        (OUTPUT_ZERO, 5),
        (TRIPLE_ZERO, 3),
    ),
}


def kernel(
    places,
    crop_ref,
    gains_ref,
    table_ref,
    frames_hbm,
    latent_hbm,
    cotangent_hbm,
    *refs,
):
    wide_hbm = refs[:12]
    recurrent_hbm, readout_hbm, act_out_hbm, input_grad_hbm, sums_ref = refs[12:17]
    held = refs[17 : 17 + (12 if places.ahead else 4)]
    (
        frames_ref,
        latent_ref,
        cotangent_ref,
        input_grad_ref,
        recurrent_wide,
        readout_wide,
        triple_low,
        output_low,
        expand_low,
        shrink_low,
        recurrent_low,
        readout_low,
        table_pad,
        bias_ref,
        gathered_ref,
        stream_in,
        stream_one,
        stream_two,
        normed_ref,
        qkv_ref,
        probs_ref,
        context_ref,
        cell_ref,
        bend_ref,
        state_ref,
        hidden_ref,
        active_ref,
        slope_ref,
        g_ref,
        gm_ref,
        gl_ref,
        gc_ref,
        gpre_ref,
        gstate_ref,
        dcontext_ref,
        dpacked_ref,
        out_halo,
        in_halo,
        grads_ref,
        sum_in,
        table_own,
        table_in,
        send_sem,
        recv_sem,
        sum_send_sem,
        sum_recv_sem,
        table_send_sem,
        table_recv_sem,
        weight_sem,
        token_sem,
        result_sem,
    ) = refs[17 + len(held) :]
    lon_count, line_count = places.lon_count, places.line_count
    frame_count = crop_ref.shape[1]
    tokens = frames_ref.shape[0] // frame_count
    row_count = tokens // WINDOW
    me_lon = lax.axis_index("lon")
    ahead = lax.rem(me_lon + 1, lon_count)
    behind = lax.rem(me_lon + lon_count - 1, lon_count)

    me_batch = lax.axis_index("batch")
    core, line = lax.rem(me_batch, 2), lax.div(me_batch, 2)
    lon_peers = [lax.rem(me_lon + by, lon_count) for by in range(1, lon_count)]
    line_peers = [lax.rem(line + by, line_count) for by in range(1, line_count)]
    neighbours = [{"batch": 2 * line + 1 - core}]
    if places.few:
        for i in range(1, lon_count * line_count):
            at = lax.rem(line + i % line_count, line_count)
            lon = lax.rem(me_lon + i // line_count, lon_count)
            neighbours.append({"lon": lon, "batch": 2 * at + core})
    else:
        neighbours += [{"lon": peer} for peer in lon_peers]
        neighbours += [{"batch": 2 * peer + core} for peer in line_peers]

    barrier = pltpu.get_barrier_semaphore()
    for peer in neighbours:
        pl.semaphore_signal(barrier, inc=1, device_id=peer, device_id_type=MESH)

    def row_span(start, rows):
        return pl.ds(pl.multiple_of(start, ROW_TILE), rows)

    def members_of(kind, bit):
        if kind == "core":
            return core, [(1 - core, neighbours[0])]
        if kind == "lon":
            return me_lon, [(peer, {"lon": peer}) for peer in lon_peers]
        if kind == "both":
            others = []
            for i in range(1, lon_count * line_count):
                lon = lax.rem(me_lon + i // line_count, lon_count)
                at = lax.rem(line + i % line_count, line_count)
                others.append((lon * line_count + at, {"lon": lon, "batch": 2 * at + core}))
            return me_lon * line_count + line, others
        if kind == "line":
            return line, [(peer, {"batch": 2 * peer + core}) for peer in line_peers]
        mine = lax.rem(lax.div(me_lon, bit), 2)
        return mine, [(1 - mine, {"lon": me_lon + bit - 2 * bit * mine})]

    def sum_range(section, depth):
        start, rows = places.starts[places.first[section]], places.rows[section]
        for kind, bit, members in places.phases[section][:depth]:
            rows //= members
            start = start + members_of(kind, bit)[0] * rows
        return start, rows

    def sum_copies(section, phase):
        phases = places.phases[section]
        back = phase >= len(phases)
        depth = 2 * len(phases) - 1 - phase if back else phase
        kind, bit, members = phases[depth]
        start, rows = sum_range(section, depth)
        piece = rows // members
        mine, others = members_of(kind, bit)
        copies = []
        for i, (place, device) in enumerate(others):
            if back:
                rows_out = row_span(start + mine * piece, piece)
                src, dst = sums_ref.at[rows_out], sums_ref.at[rows_out]
            else:
                src = grads_ref.at[row_span(start + place * piece, piece)]
                dst = sum_in.at[row_span(places.inbox[section][phase] + i * piece, piece)]
            sem = places.sems[section][phase] + i
            copies.append(
                pltpu.make_async_remote_copy(
                    src_ref=src,
                    dst_ref=dst,
                    send_sem=sum_send_sem.at[section, sem],
                    recv_sem=sum_recv_sem.at[section, sem],
                    device_id=device,
                    device_id_type=MESH,
                )
            )
        return copies

    def add_up(start, rows, source_at, count, target):
        step = math.gcd(rows, LANES)

        def body(i, unused):
            at = row_span(start + i * step, step)
            total = grads_ref[at].astype(F32)
            for k in range(count):
                total = total + sum_in[row_span(source_at + k * rows + i * step, step)].astype(F32)
            target[at] = total.astype(BF16)

        lax.fori_loop(0, rows // step, body, None)

    def sum_start(section, phase=0):
        if places.leader[section] == section:
            for copy in sum_copies(section, phase):
                copy.start()

    def sum_step(section, phase):
        if places.leader[section] != section:
            return
        for copy in sum_copies(section, phase):
            copy.wait_recv()
        depth = len(places.phases[section])
        if phase < depth:
            start, rows = sum_range(section, phase + 1)
            target = grads_ref if phase < depth - 1 else sums_ref
            add_up(start, rows, places.inbox[section][phase], places.phases[section][phase][2] - 1, target)
        if phase < 2 * depth - 1:
            sum_start(section, phase + 1)

    def sum_drain(section):
        for phase in range(2 * len(places.phases[section])):
            for copy in sum_copies(section, phase):
                copy.wait_send()

    def halo(exchange, frame):
        return pltpu.make_async_remote_copy(
            src_ref=out_halo.at[exchange % 2, frame],
            dst_ref=in_halo.at[exchange % 2, frame],
            send_sem=send_sem.at[exchange, frame],
            recv_sem=recv_sem.at[exchange, frame],
            device_id={"lon": behind if exchange % 2 == 0 else ahead},
            device_id_type=MESH,
        )

    def send_halo(exchange, frame, value):
        if exchange >= 2:
            halo(exchange - 2, frame).wait_send()
        out_halo[exchange % 2, frame] = pack_half(value).astype(BF16)
        halo(exchange, frame).start()

    def take_halo(exchange, frame, own):
        halo(exchange, frame).wait_recv()
        return unpack_half(in_halo[exchange % 2, frame].astype(F32), own)

    tokens_in = [
        pltpu.make_async_copy(hbm, ref, token_sem.at[i])
        for i, (hbm, ref) in enumerate(
            ((frames_hbm, frames_ref), (latent_hbm, latent_ref), (cotangent_hbm, cotangent_ref))
        )
    ]

    def wide_in(which, kind, layer):
        at = 3 * which + kind if places.ahead else which
        return pltpu.make_async_copy(
            wide_hbm[3 * which + kind].at[layer], held[at].at[layer], weight_sem.at[3 * which + kind, layer]
        )

    small_in = [
        pltpu.make_async_copy(recurrent_hbm, recurrent_wide, token_sem.at[3]),
        pltpu.make_async_copy(readout_hbm, readout_wide, token_sem.at[4]),
    ]

    def weights_take(which, layer):
        wide_in(which, 0, layer).wait()
        low = (triple_low, output_low, expand_low, shrink_low)[which]
        wide = held[3 * which if places.ahead else which]
        step = 64

        def body(i, unused):
            at = pl.ds(pl.multiple_of(i * step, step), step)
            low[layer, at] = wide[layer, at].astype(BF16)

        lax.fori_loop(0, wide.shape[1] // step, body, None)

    tokens_in[0].start()
    wide_in(0, 0, 0).start()
    tokens_in[1].start()
    for copy in small_in:
        copy.start()
    for which in (1, 2, 3):
        wide_in(which, 0, 0).start()
    for which in range(4):
        wide_in(which, 0, 1).start()
    tokens_in[2].start()

    for layer, onehot_ref in ((0, gm_ref), (1, gl_ref)):
        table_pad[...] = jnp.zeros_like(table_pad)
        table_pad[:, :PAIRS] = table_ref[layer]
        onehot_ref[...] = offset_onehot(layer % 2 == 1)
        bias_ref[layer] = bias_of_table(table_pad[...], onehot_ref[...])
    for copy in small_in:
        copy.wait()
    for layer in range(LAYERS):
        recurrent_low[layer] = recurrent_wide[layer].astype(BF16)
        readout_low[layer] = readout_wide[layer].astype(BF16)
    tokens_in[0].wait()
    tokens_in[1].wait()
    for which in range(4):
        weights_take(which, 0)
    pl.semaphore_wait(barrier, len(neighbours))
    gathered_ref[...] = jnp.zeros_like(gathered_ref)

    def span(frame):
        return pl.ds(pl.multiple_of(frame * tokens, tokens), tokens)

    def gain(layer, which):
        return gains_ref[which, layer : layer + 1, :]

    def attention_part(layer, frame, normed):
        at = span(frame)
        normed_ref[layer, at] = normed
        qkv = dot(normed, triple_low[layer]).astype(BF16)
        qkv_ref[layer, at] = qkv
        crop = (crop_ref[0, frame], crop_ref[1, frame])
        return attend_forward(qkv, bias_ref, layer, crop, probs_ref, frame, row_count)

    def middle(layer, frame, stream, context, latent):
        at = span(frame)
        context_ref[layer, at] = context
        one = stream + dot(context, output_low[layer])
        (stream_one, input_grad_ref)[layer][at] = one
        scaled, _ = norm_parts(one)
        cell = (scaled * gain(layer, 2)).astype(BF16)
        cell_ref[layer, at] = cell
        preact = dot_nt(cell, recurrent_low[layer, :, :WIDTH]) + dot_nt(latent, recurrent_low[layer, :, WIDTH:])
        tangent = jnp.tanh(preact)
        bend_ref[layer, at] = (1.0 - tangent * tangent).astype(BF16)
        state = tangent.astype(BF16)
        state_ref[layer, at] = state
        two = one + dot(state, readout_low[layer])
        (stream_two, g_ref)[layer][at] = two
        scaled, _ = norm_parts(two)
        hidden = (scaled * gain(layer, 1)).astype(BF16)
        hidden_ref[layer, at] = hidden
        for block in range(HIDDEN // WIDTH):
            cols = slice(block * WIDTH, (block + 1) * WIDTH)
            inner = dot(hidden, expand_low[layer, :, cols])
            square = inner * inner
            bend = GELU_C * (1.0 + GELU_A * square)
            gate = 0.5 * (1.0 + jnp.tanh(inner * bend))
            active = inner * gate
            slope = gate + active * (1.0 - gate) * (2.0 * GELU_C + 6.0 * GELU_C * GELU_A * square)
            active_ref[layer, at, cols] = active.astype(BF16)
            slope_ref[layer, at, cols] = slope.astype(BF16)
        return two + dot(active_ref[layer, at], shrink_low[layer])

    def feed_back(layer, frame, g):
        at = span(frame)
        gm = g.astype(BF16)
        gm_ref[at] = gm
        for block in range(HIDDEN // WIDTH):
            cols = slice(block * WIDTH, (block + 1) * WIDTH)
            dactive = dot_nt(gm, shrink_low[layer, cols])
            slope_ref[layer, at, cols] = (dactive * slope_ref[layer, at, cols].astype(F32)).astype(BF16)

    def middle_back(layer, frame, g, gstate):
        at = span(frame)
        dhidden = dot_nt(slope_ref[layer, at], expand_low[layer])
        scaled, inverse = norm_parts((stream_two, g_ref)[layer][at])
        g = g + norm_back(dhidden, gain(layer, 1), scaled, inverse)
        gl = g.astype(BF16)
        gl_ref[at] = gl
        dstate = dot_nt(gl, readout_low[layer])
        if gstate is not None:
            dstate = dstate + gstate
        gpre = (dstate * bend_ref[layer, at].astype(F32)).astype(BF16)
        gpre_ref[at] = gpre
        if layer > 0:
            gstate_ref[at] = dot(gpre, recurrent_low[layer, :, WIDTH:])
        scaled, inverse = norm_parts((stream_one, input_grad_ref)[layer][at])
        dcell = dot(gpre, recurrent_low[layer, :, :WIDTH])
        g = g + norm_back(dcell, gain(layer, 2), scaled, inverse)
        gc = g.astype(BF16)
        gc_ref[at] = gc
        g_ref[at] = g
        return dot_nt(gc, output_low[layer])

    def values_back(layer, frame, dcontext):
        dpacked_ref[span(frame), 2 * WIDTH :] = value_grads(dcontext, layer, probs_ref, frame, row_count)

    def attention_back(layer, frame, dcontext):
        at = span(frame)
        pieces = attend_backward(
            qkv_ref[layer, at], dcontext, layer, probs_ref, frame, gathered_ref, row_count
        )
        for which in range(2):
            dpacked_ref[at, which * WIDTH : (which + 1) * WIDTH] = pieces[which]

    def packed_back(layer, frame):
        return dot_nt(dpacked_ref[span(frame)], triple_low[layer])

    def stream_back(layer, frame, g, stream, dnormed):
        scaled, inverse = norm_parts(stream)
        return g + norm_back(dnormed, gain(layer, 0), scaled, inverse)

    def put_blocks(start, value):
        rows = value.shape[0]
        for block in range(value.shape[1] // LANES):
            grads_ref[start + block * rows : start + (block + 1) * rows] = value[
                :, half_lanes(block)
            ].astype(BF16)

    def put_rows(start, total_rows, row, value):
        rows = value.shape[0]
        for block in range(value.shape[1] // LANES):
            at = start + block * total_rows + row
            grads_ref[at : at + rows] = value[:, half_lanes(block)].astype(BF16)

    def shrink_grads(layer):
        for block in range(HIDDEN // WIDTH):
            cols = slice(block * WIDTH, (block + 1) * WIDTH)
            put_rows(
                places.shrink[layer], HIDDEN, block * WIDTH, dot_tn(active_ref[layer, :, cols], gm_ref[...])
            )

    def expand_grads(layer):
        for block in range(HIDDEN // WIDTH):
            cols = slice(block * WIDTH, (block + 1) * WIDTH)
            put_blocks(
                places.expand[layer] + 2 * block * WIDTH, dot_tn(hidden_ref[layer], slope_ref[layer, :, cols])
            )

    def small_grads(layer, latent):
        near = dot_tn(gpre_ref[...], cell_ref[layer])
        far = dot_tn(gpre_ref[...], latent)
        far = jnp.concatenate([far, jnp.zeros((LATENT, LANES - LATENT), F32)], axis=1)
        readout = dot_tn(state_ref[layer], gl_ref[...])
        return [near[:, :LANES], near[:, LANES:], far, readout[:, :LANES], readout[:, LANES:]]

    def table_pieces(layer):
        gm_ref[...] = offset_onehot(layer % 2 == 1)
        table = table_of_bias(gathered_ref[layer], gm_ref[...])
        return [table[:, :LANES], table[:, LANES:]]

    def put_pieces(start, pieces):
        used = sum(piece.shape[0] for piece in pieces)
        value = jnp.concatenate(pieces, axis=0).astype(BF16)
        grads_ref[start : start + used] = value
        return start + used

    def clear_spare(section):
        if section in places.spare:
            clear_rows(*places.spare[section])

    def clear_rows(start, stop):
        if stop > start:
            grads_ref[start:stop] = jnp.zeros((stop - start, LANES), BF16)

    def output_grads(layer):
        put_blocks(places.output[layer], dot_tn(context_ref[layer], gc_ref[...]))

    def triple_grads(layer, blocks):
        for block in blocks:
            cols = slice(block * WIDTH, (block + 1) * WIDTH)
            put_blocks(places.triple[layer][block], dot_tn(normed_ref[layer], dpacked_ref[:, cols]))

    def table_core():
        here = row_span(0, TABLE_ROWS)
        return pltpu.make_async_remote_copy(
            src_ref=table_own.at[here],
            dst_ref=table_in.at[row_span(members * TABLE_ROWS, TABLE_ROWS)],
            send_sem=table_send_sem.at[0],
            recv_sem=table_recv_sem.at[0],
            device_id=neighbours[0],
            device_id_type=MESH,
        )

    members = lon_count * line_count

    def table_copies():
        mine = row_span((me_lon * line_count + line) * TABLE_ROWS, TABLE_ROWS)
        return [
            pltpu.make_async_remote_copy(
                src_ref=table_in.at[mine],
                dst_ref=table_in.at[mine],
                send_sem=table_send_sem.at[1 + i],
                recv_sem=table_recv_sem.at[1 + i],
                device_id=device,
                device_id_type=MESH,
            )
            for i, (_, device) in enumerate(members_of("both", 0)[1])
        ]

    def table_start():
        table_own[...] = jnp.concatenate(table_pieces(0), axis=0).astype(BF16)
        table_core().start()

    def table_spread():
        table_core().wait_recv()
        other = table_in[members * TABLE_ROWS : (members + 1) * TABLE_ROWS].astype(F32)
        mine = row_span((me_lon * line_count + line) * TABLE_ROWS, TABLE_ROWS)
        table_in[mine] = (table_own[...].astype(F32) + other).astype(BF16)
        for copy in table_copies():
            copy.start()

    def table_take():
        for copy in table_copies():
            copy.wait_recv()
        total = table_in[:TABLE_ROWS].astype(F32)
        for i in range(1, members):
            total = total + table_in[i * TABLE_ROWS : (i + 1) * TABLE_ROWS].astype(F32)
        sums_ref[places.table[0] : places.table[0] + TABLE_ROWS] = total.astype(BF16)

    def loop(body, steps=()):
        def whole(frame, unused):
            body(frame)
            for after in range(frame_count):
                here = [(section, phase) for when, section, phase in steps if when == after]
                if here:

                    @pl.when(frame == after)
                    def _(here=here):
                        for section, phase in here:
                            sum_step(section, phase)

        lax.fori_loop(0, frame_count, whole, None)

    def sum_steps(*steps):
        for section, phase in steps:
            sum_step(section, phase)

    def first_layer(frame):
        at = span(frame)
        stream = frames_ref[at].astype(F32)
        scaled, _ = norm_parts(stream)
        normed = (scaled * gain(0, 0)).astype(BF16)
        context = attention_part(0, frame, normed).astype(BF16)
        stream = middle(0, frame, stream, context, latent_ref[at])
        stream_in[at] = stream
        scaled, _ = norm_parts(stream)
        normed = scaled * gain(1, 0)
        normed_ref[1, at] = normed.astype(BF16)
        send_halo(0, frame, normed)

    loop(first_layer)
    for which in range(4):
        weights_take(which, 1)
    if places.ahead:
        for layer in (1, 0):
            for which in range(4):
                for kind in (1, 2):
                    wide_in(which, kind, layer).start()

    def second_attention(frame):
        at = span(frame)
        normed = take_halo(0, frame, normed_ref[1, at].astype(F32))
        context = attention_part(1, frame, rows_ahead(normed).astype(BF16))
        context = rows_behind(context)
        context_ref[1, at] = context.astype(BF16)
        send_halo(1, frame, context)

    loop(second_attention)
    tokens_in[2].wait()

    def second_middle(frame):
        at = span(frame)
        context = take_halo(1, frame, context_ref[1, at].astype(F32)).astype(BF16)
        stream = middle(1, frame, stream_in[at], context, state_ref[0, at])
        feed_back(1, frame, cotangent_ref[at].astype(F32))
        cotangent_ref[at] = stream.astype(BF16)

    loop(second_middle)
    act_out = pltpu.make_async_copy(cotangent_ref, act_out_hbm, result_sem.at[frame_count])
    act_out.start()
    shrink_grads(1)
    sum_start(SHRINK_ONE)
    expand_grads(1)
    sum_start(EXPAND_ONE)

    def second_middle_back(frame):
        at = span(frame)
        dcontext = middle_back(1, frame, gm_ref[at].astype(F32), None)
        dcontext_ref[at] = dcontext.astype(BF16)
        send_halo(2, frame, dcontext)

    loop(second_middle_back, STEPS["second_middle_back"])
    output_grads(1)
    early_one = put_pieces(places.early[1], small_grads(1, state_ref[0]))

    def second_back(frame):
        at = span(frame)
        dcontext = take_halo(2, frame, dcontext_ref[at].astype(F32))
        dcontext = rows_ahead(dcontext).astype(BF16)
        values_back(1, frame, dcontext)
        attention_back(1, frame, dcontext)
        dnormed = rows_behind(packed_back(1, frame))
        dcontext_ref[at] = dnormed.astype(BF16)
        send_halo(3, frame, dnormed)

    loop(second_back, STEPS["second_back"])
    triple_grads(1, (0, 1, 2))
    clear_spare(ATTEND_ONE)
    sum_start(ATTEND_ONE)

    def first_feed_back(frame):
        at = span(frame)
        dnormed = take_halo(3, frame, dcontext_ref[at].astype(F32))
        g = stream_back(1, frame, g_ref[at], stream_in[at], dnormed)
        g_ref[at] = g
        feed_back(0, frame, g)

    loop(first_feed_back, STEPS["first_feed_back"])
    shrink_grads(0)
    sum_start(SHRINK_ZERO)
    sum_steps(*STEPS["after_shrink"])
    expand_grads(0)
    sum_start(EXPAND_ZERO)

    def first_middle_back(frame):
        at = span(frame)
        dcontext = middle_back(0, frame, g_ref[at], gstate_ref[at]).astype(BF16)
        dcontext_ref[at] = dcontext
        values_back(0, frame, dcontext)

    loop(first_middle_back, STEPS["first_middle_back"])
    output_grads(0)
    triple_grads(0, (2,))
    clear_rows(put_pieces(early_one, table_pieces(1)), places.early[1] + SMALL_ROWS)
    clear_rows(put_pieces(places.early[0], small_grads(0, latent_ref[...])), places.early[1])
    clear_spare(OUTPUT_ZERO)
    sum_start(OUTPUT_ZERO)
    sum_steps(*STEPS["after_output"])

    def grad_out(frame):
        at = span(frame)
        return pltpu.make_async_copy(input_grad_ref.at[at], input_grad_hbm.at[at], result_sem.at[frame])

    def first_back(frame):
        attention_back(0, frame, dcontext_ref[span(frame)])

    loop(first_back, STEPS["first_back"])
    triple_grads(0, (0, 1))
    if not places.few:
        put_pieces(places.table[0], table_pieces(0))
        clear_spare(TRIPLE_ZERO)
    sum_start(TRIPLE_ZERO)
    if places.few:
        table_start()

    def last_back(frame):
        at = span(frame)
        stream = frames_ref[at].astype(F32)
        input_grad_ref[at] = stream_back(0, frame, g_ref[at], stream, packed_back(0, frame))
        grad_out(frame).start()

    loop(last_back, STEPS["last_back"])
    if places.few:
        table_spread()
    sum_steps(*STEPS["last"])
    if places.few:
        table_take()
        table_core().wait_send()
        for copy in table_copies():
            copy.wait_send()

    def drain(frame, unused):
        for exchange in (2, 3):
            halo(exchange, frame).wait_send()
        grad_out(frame).wait()

    lax.fori_loop(0, frame_count, drain, None)
    act_out.wait()
    if places.ahead:
        for layer in (1, 0):
            for which in range(4):
                for kind in (1, 2):
                    wide_in(which, kind, layer).wait()
    for section in places.rows:
        sum_drain(section)


def flat_tokens(array):
    return array.reshape(-1, array.shape[-1])


def in_hbm(array):
    return pltpu.with_memory_space_constraint(array, pltpu.HBM)


def layers_step(frames, latent, crop_band, cotangent, parameters, places):
    frame_count, row_count, col_count, features = frames.shape
    count = frame_count * row_count * col_count
    tokens = row_count * col_count
    vmem = pl.BlockSpec(memory_space=pltpu.VMEM)
    hbm = pl.BlockSpec(memory_space=pltpu.HBM)
    both = lambda *shape: pltpu.VMEM((LAYERS,) + shape, BF16)
    one = lambda *shape: pltpu.VMEM(shape, BF16)
    wide = lambda *shape: pltpu.VMEM(shape, F32)
    scratch = [
        one(count, WIDTH),
        one(count, LATENT),
        one(count, WIDTH),
        wide(count, WIDTH),
        wide(LAYERS, LATENT, WIDTH + LATENT),
        wide(LAYERS, LATENT, WIDTH),
        both(WIDTH, 3 * WIDTH),
        both(WIDTH, WIDTH),
        both(WIDTH, HIDDEN),
        both(HIDDEN, WIDTH),
        both(LATENT, WIDTH + LATENT),
        both(LATENT, WIDTH),
        wide(HEADS, WIDTH),
        wide(LAYERS, SPAN, HEADS * SPAN),
        wide(LAYERS, SPAN, HEADS * SPAN),
        wide(count, WIDTH),
        wide(count, WIDTH),
        wide(count, WIDTH),
        both(count, WIDTH),
        both(count, 3 * WIDTH),
        both(count, HEADS * SPAN),
        both(count, WIDTH),
        both(count, WIDTH),
        both(count, LATENT),
        both(count, LATENT),
        both(count, WIDTH),
        both(count, HIDDEN),
        both(count, HIDDEN),
        wide(count, WIDTH),
        one(count, WIDTH),
        one(count, WIDTH),
        one(count, WIDTH),
        one(count, LATENT),
        wide(count, LATENT),
        one(count, WIDTH),
        one(count, 3 * WIDTH),
        one(2, frame_count, tokens // 2, WIDTH),
        one(2, frame_count, tokens // 2, WIDTH),
        one(places.total, LANES),
        one(places.inbox_rows, LANES),
        one(TABLE_ROWS, LANES),
        one((places.few_members + 1) * TABLE_ROWS, LANES),
        pltpu.SemaphoreType.DMA((4, frame_count)),
        pltpu.SemaphoreType.DMA((4, frame_count)),
        pltpu.SemaphoreType.DMA((len(SECTION_ROWS), places.most_sems)),
        pltpu.SemaphoreType.DMA((len(SECTION_ROWS), places.most_sems)),
        pltpu.SemaphoreType.DMA((places.few_members,)),
        pltpu.SemaphoreType.DMA((places.few_members,)),
        pltpu.SemaphoreType.DMA((12, LAYERS)),
        pltpu.SemaphoreType.DMA((5,)),
        pltpu.SemaphoreType.DMA((frame_count + 1,)),
    ]
    wide_parameters = parameters[:12]
    recurrent, readout, gains, table = parameters[12::3]
    held = [a for i, a in enumerate(wide_parameters) if places.ahead or i % 3 == 0]
    given = (frames, latent, cotangent)
    outs = pl.pallas_call(
        functools.partial(kernel, places),
        out_shape=(
            pltpu.HBM((count, WIDTH), BF16),
            pltpu.HBM((count, WIDTH), F32),
            pltpu.VMEM((places.sum_rows, LANES), BF16),
        )
        + tuple(pltpu.VMEM(a.shape, F32) for a in held),
        in_specs=[pl.BlockSpec(memory_space=pltpu.SMEM), vmem, vmem] + [hbm] * 17,
        out_specs=(hbm, hbm, vmem) + (vmem,) * len(held),
        scratch_shapes=scratch,
        compiler_params=pltpu.CompilerParams(
            collective_id=0, has_side_effects=True, vmem_limit_bytes=places.grant
        ),
        name="swin_step",
    )(
        crop_band.T,
        gains,
        table,
        *(in_hbm(flat_tokens(a)) for a in given),
        *(in_hbm(a) for a in wide_parameters),
        in_hbm(recurrent),
        in_hbm(readout),
    )
    return outs[0], outs[1], outs[2], outs[3:]


def update_kernel(scale, places, sums, result_hbm, grad_hbm, *refs):
    count = 24
    given, result_out, grad_out = refs[:count], refs[count], refs[count + 1]
    made, held = refs[count + 2 : 2 * count + 2], refs[2 * count + 2 : 3 * count + 2]
    result_held, products, pass_sem, in_sem, out_sem = refs[3 * count + 2 :]
    triple, output, expand, shrink, recurrent, readout, gains, table = range(8)
    grad_held = held[3 * shrink].at[0]

    passing_in = [
        pltpu.make_async_copy(result_hbm, result_held, pass_sem.at[0]),
        pltpu.make_async_copy(grad_hbm, grad_held, pass_sem.at[1]),
    ]
    passing_out = [
        pltpu.make_async_copy(result_held, result_out, pass_sem.at[2]),
        pltpu.make_async_copy(grad_held, grad_out, pass_sem.at[3]),
    ]
    units = [
        (shrink, 1),
        (expand, 1),
        (triple, 1),
        (output, 1),
        (shrink, 0),
        (expand, 0),
        (output, 0),
        (triple, 0),
        (recurrent, None),
        (readout, None),
        (table, None),
        (gains, None),
    ]

    def part(ref, layer):
        return ref if layer is None else ref.at[layer]

    def is_held(which, kind):
        return which < recurrent and (places.ahead or kind == 0)

    def coming(index):
        which, layer = units[index]
        return [
            pltpu.make_async_copy(
                part(given[3 * which + i], layer), part(held[3 * which + i], layer), in_sem.at[index, i]
            )
            for i in range(3)
            if not is_held(which, i)
        ]

    def going(index):
        which, layer = units[index]
        return [
            pltpu.make_async_copy(
                part(held[3 * which + i], layer), part(made[3 * which + i], layer), out_sem.at[index, i]
            )
            for i in range(3)
        ]

    for index in range(len(units)):
        for copy in coming(index):
            copy.start()
    for copy in passing_in:
        copy.start()

    def change(which, at, summed):
        old = [(given if is_held(which, i) else held)[3 * which + i][at] for i in range(3)]
        weight, moment, average = held[3 * which : 3 * which + 3]
        gradient = summed.astype(F32) * scale
        velocity = MOMENTUM_RATE * old[1] + gradient
        updated = old[0] - LEARN_RATE * (gradient + MOMENTUM_RATE * velocity)
        average[at] = AVERAGE_DECAY * old[2] + (1.0 - AVERAGE_DECAY) * updated
        weight[at] = updated
        moment[at] = velocity
        return old[0].astype(BF16).astype(F32) * gradient

    def change_blocks(which, layer, starts, rows, norm=None):
        step = 32

        def body(i, unused):
            row = pl.multiple_of(i * step, step)
            total = None
            for block, start in enumerate(starts):
                summed = sums[pl.ds(start + row, step)]
                product = change(which, (layer, pl.ds(row, step), half_lanes(block)), summed)
                total = product if total is None else total + product
            if norm is not None:
                products[layer, norm, pl.ds(row, step)] = total

        lax.fori_loop(0, rows // step, body, None)

    def sum_lanes(ones, value):
        rows = value.shape[0]
        parts = three_parts(value)
        sums_of = [dot_nt(ones, parts[i * rows : (i + 1) * rows])[:1] for i in range(3)]
        return sums_of[0] + (sums_of[1] + sums_of[2])

    cell_rows = []

    def blocks_at(start, rows, count):
        return [start + i * rows for i in range(count)]

    for index, (which, layer) in enumerate(units):
        for copy in coming(index):
            copy.wait()
        if which == expand:
            change_blocks(expand, layer, blocks_at(places.expand[layer], WIDTH, HIDDEN // LANES), WIDTH, 1)
        elif which == shrink:
            change_blocks(shrink, layer, blocks_at(places.shrink[layer], HIDDEN, 2), HIDDEN)
        elif which == output:
            change_blocks(output, layer, blocks_at(places.output[layer], WIDTH, 2), WIDTH)
        elif which == triple:
            starts = [at for start in places.triple[layer] for at in blocks_at(start, WIDTH, 2)]
            change_blocks(triple, layer, starts, WIDTH, 0)
        else:
            for each in range(LAYERS):
                at = places.early[each]
                if which == recurrent:
                    rows = []
                    for block in range(3):
                        lanes = slice(block * LANES, min((block + 1) * LANES, WIDTH + LATENT))
                        summed = sums[pl.ds(at + block * LATENT, LATENT)][:, : lanes.stop - lanes.start]
                        product = change(which, (each, slice(0, LATENT), lanes), summed)
                        rows.append(jnp.sum(product, axis=0, keepdims=True))
                    cell_rows.append(jnp.concatenate(rows[:2], axis=1))
                elif which == readout:
                    for block in range(2):
                        rows = sums[pl.ds(at + 96 + block * LATENT, LATENT)]
                        change(which, (each, slice(0, LATENT), half_lanes(block)), rows)
                elif which == table:
                    rows = sums[pl.ds(places.table[each], TABLE_ROWS)].astype(F32)
                    change(which, (each, slice(0, HEADS), slice(0, LANES)), rows[:8])
                    change(which, (each, slice(0, HEADS), slice(LANES, PAIRS)), rows[8:16, : PAIRS - LANES])
                else:
                    ones = jnp.ones((8, LANES), BF16)
                    for norm in range(3):
                        gain_row = held[3 * gains][norm, each : each + 1, :]
                        if norm == 2:
                            total = cell_rows[each]
                        else:
                            total = sum_lanes(ones, products[each, norm])
                        change(which, (norm, slice(each, each + 1)), total / (gain_row * scale))
        for copy in going(index):
            copy.start()
        if index == 1:
            for copy in passing_in:
                copy.wait()
            for copy in passing_out:
                copy.start()
        if index == 3:
            for copy in passing_out:
                copy.wait()
    for index in range(len(units)):
        for copy in going(index):
            copy.wait()


def update_step(sums, result, input_grad, held, parameters, scale, places):
    hbm = pl.BlockSpec(memory_space=pltpu.HBM)
    vmem = pl.BlockSpec(memory_space=pltpu.VMEM)
    in_vmem = lambda a: pltpu.with_memory_space_constraint(a, pltpu.VMEM)
    held = list(held)
    given, specs = [], []
    for i, a in enumerate(parameters):
        if i < 12 and (places.ahead or i % 3 == 0):
            given.append(in_vmem(held.pop(0)))
            specs.append(vmem)
        else:
            given.append(in_hbm(a))
            specs.append(hbm)
    like = lambda a: pltpu.HBM(a.shape, a.dtype)
    return pl.pallas_call(
        functools.partial(update_kernel, scale, places),
        out_shape=(like(result), like(input_grad)) + tuple(like(a) for a in parameters),
        in_specs=[vmem, hbm, hbm] + specs,
        out_specs=(hbm,) * (2 + len(parameters)),
        scratch_shapes=[pltpu.VMEM(a.shape, F32) for a in parameters]
        + [
            pltpu.VMEM(result.shape, result.dtype),
            pltpu.VMEM((LAYERS, 2, WIDTH, LANES), F32),
            pltpu.SemaphoreType.DMA((4,)),
            pltpu.SemaphoreType.DMA((12, 3)),
            pltpu.SemaphoreType.DMA((12, 3)),
        ],
        compiler_params=pltpu.CompilerParams(vmem_limit_bytes=20 * 2**20),
        name="nesterov_step",
    )(in_vmem(sums), in_hbm(result), in_hbm(input_grad), *given)


def per_device(frames, latent_init, crop_band, cotangent, *parameters):
    shape = frames.shape
    lon_count, batch_count = lax.axis_size("lon"), lax.axis_size("batch")
    places = Places(lon_count, batch_count)
    turned = {4: (0, 2, 1), 6: (1, 0, 2)}
    parameters = [
        a.transpose(turned[i // 3]) if i // 3 in turned else a for i, a in enumerate(parameters)
    ]
    result, input_grad, sums, held = layers_step(
        frames, latent_init, crop_band, cotangent, parameters, places
    )
    tokens = shape[0] * shape[1] * shape[2] * lon_count * batch_count
    result, input_grad, *updated = update_step(
        sums, result, input_grad, held, parameters, float(tokens) ** (-0.5), places
    )
    updated = [a.transpose(turned[i // 3]) if i // 3 in turned else a for i, a in enumerate(updated)]
    return (result.reshape(shape), input_grad.reshape(shape), *updated)


def solution(mesh):
    split = P("batch", None, "lon", None)
    return jax.shard_map(
        per_device,
        mesh=mesh,
        in_specs=(split, split, P("batch", None), split) + (P(),) * 24,
        out_specs=(split, split) + (P(),) * 24,
        check_vma=False,
    )
```

time: 279 us -> 106 us (0.38)
  waiting for transfers between devices: 139 us -> 0 us
  local copies, waits for them, and re-layouts: 44.1 us -> 0 us
  Pallas kernels: 65.8 us -> 105 us
  other arithmetic: 15.1 us -> 0 us
  between operations: 14.7 us -> 0.84 us
    psum x1 -> x0, waiting for transfers between devices: 139 us -> none  [per_device(): grads = lax.psum(grads, ('lon', 'batch')).astype(F32)]
    pallas_call x1 -> x2, Pallas kernels: 65.8 us -> 105 us  [the longest x1 95.9 us: layers_step(): pl.pallas_call(functools.partial(kernel, places), out_shape=(pltpu.HBM((c...]
    add x8 -> x0, other arithmetic: 14.2 us -> none  [update(): smoothed = AVERAGE_DECAY * average + (1.0 - AVERAGE_DECAY) * updated]
    slice x16 -> x0, local copies, waits for them, and re-layouts: 12.3 us -> none  [the longest x9 5.86 us: split_grads(): small[:72, i * LATENT:(i + 1) * LATENT]]
    unnamed x107 -> x0, local copies, waits for them, and re-layouts: 9.86 us -> none
    another operation x7 -> x0, local copies, waits for them, and re-layouts: 9.14 us -> none  [split_grads(): return [jnp.stack(pair) for pair in zip(*out)]]
    transpose x6 -> x0, local copies, waits for them, and re-layouts: 8.43 us -> none  [unblock(): rows.reshape(width // LANES, height, LANES).transpose(1, 0, 2)]
    reshape x9 -> x0, local copies, waits for them, and re-layouts: 4.43 us -> none  [unblock(): rows.reshape(width // LANES, height, LANES).transpose(1, 0, 2)]
  transfers between devices with their start and end apart: 1 -> 0, of which waited for: 1 -> 0; matrix products, arithmetic and copies ran while one was open for 0% -> 0% of each run, Pallas kernels for 0% -> 0%
where the time goes in v3:
time: 106 us
  Pallas kernels  105 us (99%)
    pallas_call x1, Pallas kernels, layers_step(): pl.pallas_call(functools.partial(kernel, places), out_shape=(pltpu.HBM((c...  95.9 us
    pallas_call x1, Pallas kernels, update_step(): pl.pallas_call(functools.partial(update_kernel, scale, places), out_shape...  8.86 us

profile of v3, /device:TPU:0, one launch (start us, length us, event | category | flops | bytes accessed | tf_op | source)
XLA Modules:
  0.0 105.7 jit_solution(5902048917157935796)
XLA Ops:
  0.7 95.9 %swin_step.1 = (bf16[1024,256]{1,0:T(8,128)(2,1)}, f32[1024,256]{1,0:T(8,128)}, bf16[12816,128]{1,0:T(8,128)(2,1)S(1)}, f32[2,256,768]{2,1,0:T(8,128)S(1)}, f32[...) custom-call(s32[2,4]{1,0:T(2,128)} %bitcast.29, ...), custom_call_target="tpu_custom_call" | custom-call | tf_op jit(solution)/shard_map/swin_step/pallas_call | solution.py:1128
  96.6 8.9 %nesterov_step.1 = (bf16[1024,256]{1,0:T(8,128)(2,1)}, f32[1024,256]{1,0:T(8,128)}, f32[2,256,768]{2,1,0:T(8,128)}, f32[2,256,768]{2,1,0:T(8,128)}, f32[2,256,76...) custom-call(bf16[12816,128]{1,0:T(8,128)(2,1)S(1)} %get-tuple-elemen, ...), custom_call_target="tpu_custom_call" | custom-call | tf_op jit(solution)/shard_map/nesterov_step/pallas_call | solution.py:1323

commit v4 on v3

--- a/solution.py
+++ b/solution.py
@@ -39,13 +39,15 @@
 FEED_ROWS = HIDDEN * WIDTH // LANES
 OUTPUT_ROWS = WIDTH * WIDTH // LANES
 TRIPLE_ROWS = 3 * OUTPUT_ROWS
-SHRINK_ONE, EXPAND_ONE, ATTEND_ONE, SHRINK_ZERO, EXPAND_ZERO, OUTPUT_ZERO, TRIPLE_ZERO = range(7)
+SHRINK_ONE, EXPAND_ONE, ATTEND_ONE, SHRINK_ZERO, SHRINK_MORE, EXPAND_ZERO, EXPAND_MORE, OUTPUT_ZERO, TRIPLE_ZERO = range(9)
 SECTION_ROWS = (
     FEED_ROWS,
     FEED_ROWS,
     OUTPUT_ROWS + TRIPLE_ROWS,
-    FEED_ROWS,
-    FEED_ROWS,
+    FEED_ROWS // 2,
+    FEED_ROWS // 2,
+    FEED_ROWS // 2,
+    FEED_ROWS // 2,
     2 * OUTPUT_ROWS + LAYERS * SMALL_ROWS,
     2 * OUTPUT_ROWS,
 )
@@ -55,13 +57,15 @@
 
 
 SECTION_PHASES = (
-    ("core", "up", "line"),
-    ("core", "down", "line"),
-    ("core", "up", "line"),
+    ("core", "lon", "line"),
+    ("core", "line", "x", "y"),
+    ("core", "lon", "line sum"),
     ("core", "lon", "line"),
     ("core", "lon", "line"),
     ("core", "lon", "line"),
-    ("core", "both"),
+    ("core", "lon", "line sum"),
+    ("core", "lon", "line"),
+    ("core", "lon", "line sum"),
 )
 
 
@@ -69,11 +73,11 @@
     def __init__(self, lon_count, batch_count):
         self.lon_count, self.line_count = lon_count, batch_count // 2
         self.ahead = lon_count * batch_count <= 32
-        self.grant = (85 if self.ahead else 96) * 2**19
+        self.grant = (171 if self.ahead else 192) * 2**18
         unit = ROW_TILE * lon_count * batch_count
         few = self.few = unit <= 512
         self.few_members = lon_count * self.line_count if few else 1
-        groups = [[i] for i in range(7)] if few else [[0, 1], [2], [3, 4], [5, 6]]
+        groups = [[i] for i in range(9)] if few else [[0, 1], [2], [3, 4, 5, 6], [7, 8]]
         self.leader = [group[-1] for group in groups for _ in group]
         self.first = [group[0] for group in groups for _ in group]
         self.rows, starts, at = {}, {}, 0
@@ -87,35 +91,46 @@
             at = begin + rows
         self.total = at
         self.starts = starts
-        self.phases, self.inbox, self.sems = {}, {}, {}
+        self.phases, self.back, self.inbox, self.sems = {}, {}, {}, {}
+        self.most_sems = 0
         bits = [1 << i for i in range(lon_count.bit_length() - 1)]
         inbox = 0
         for section, rows in self.rows.items():
             phases = []
-            for name in SECTION_PHASES[section]:
-                if name == "up":
-                    phases += [("bit", bit, 2) for bit in bits]
-                elif name == "down":
-                    phases += [("bit", bit, 2) for bit in reversed(bits)]
+            names = SECTION_PHASES[section]
+            for name in names:
+                if name == "x":
+                    phases += [("bit", bit, 2) for bit in bits[:1]]
+                elif name == "y":
+                    phases += [("bit", bit, 2) for bit in bits[1:]]
                 elif name == "both" and few:
                     phases.append((name, 0, lon_count * self.line_count))
                 elif name == "both":
                     phases += [("lon", 0, lon_count), ("line", 0, self.line_count)]
-                else:
+                elif name == "line sum":
+                    phases.append(("gather", 0, self.line_count))
+                elif name != "at once":
                     phases.append((name, 0, {"core": 2, "lon": lon_count, "line": batch_count // 2}[name]))
             self.phases[section] = phases
+            back = [phase + (depth,) for depth, phase in enumerate(phases, 1) if phase[0] != "gather"][::-1]
+            if few and "at once" in names:
+                back = [("both", 0, lon_count * self.line_count, len(phases)), back[-1]]
+            self.back[section] = back
             self.inbox[section], self.sems[section], sem = [], [], 0
-            for _, _, members in phases:
-                rows //= members
+            for kind, _, members in phases:
                 self.inbox[section].append(inbox)
                 self.sems[section].append(sem)
-                inbox += rows * (members - 1)
+                if kind == "gather":
+                    inbox += rows * members
+                else:
+                    rows //= members
+                    inbox += rows * (members - 1)
                 sem += members - 1
-            for _, _, members in reversed(phases):
+            for _, _, members, _ in back:
                 self.sems[section].append(sem)
                 sem += members - 1
+            self.most_sems = max(self.most_sems, sem)
         self.inbox_rows = inbox
-        self.most_sems = max(2 * sum(m - 1 for _, _, m in phases) for phases in self.phases.values())
         self.shrink = (starts[SHRINK_ZERO], starts[SHRINK_ONE])
         self.expand = (starts[EXPAND_ZERO], starts[EXPAND_ONE])
         self.output = (starts[OUTPUT_ZERO], starts[ATTEND_ONE])
@@ -368,55 +383,25 @@
 
 STEPS = {
     "second_middle_back": (),
-    "second_back": (
-        (0, SHRINK_ONE, 0),
-        (0, EXPAND_ONE, 0),
-        (2, SHRINK_ONE, 1),
-        (2, EXPAND_ONE, 1),
-    ),
-    "first_feed_back": ((0, SHRINK_ONE, 2), (1, EXPAND_ONE, 2), (2, ATTEND_ONE, 0)),
+    "before_second_back": (),
+    "second_back": ((0, SHRINK_ONE), (0, EXPAND_ONE)),
+    "before_first_feed_back": (),
+    "first_feed_back": ((1, ATTEND_ONE), (1, SHRINK_ONE), (2, EXPAND_ONE)),
     "after_shrink": (),
     "first_middle_back": (
-        (0, SHRINK_ONE, 3),
-        (0, ATTEND_ONE, 1),
-        (1, EXPAND_ONE, 3),
-        (2, SHRINK_ZERO, 0),
-        (2, EXPAND_ZERO, 0),
-        (3, ATTEND_ONE, 2),
+        (0, SHRINK_ZERO), (0, SHRINK_MORE), (0, SHRINK_ONE), (0, EXPAND_ZERO), (0, EXPAND_MORE),
+        (0, ATTEND_ONE), (0, EXPAND_ONE),
     ),
-    "after_output": ((SHRINK_ONE, 4), (EXPAND_ONE, 4)),
-    "first_back": (
-        (0, SHRINK_ZERO, 1),
-        (0, OUTPUT_ZERO, 0),
-        (0, ATTEND_ONE, 3),
-        (1, SHRINK_ONE, 5),
-        (1, EXPAND_ZERO, 1),
-        (1, EXPAND_ONE, 5),
-        (2, SHRINK_ZERO, 2),
-        (2, ATTEND_ONE, 4),
-        (3, SHRINK_ONE, 6),
-        (3, OUTPUT_ZERO, 1),
-        (3, EXPAND_ONE, 6),
-        (3, EXPAND_ZERO, 2),
-    ),
-    "last_back": ((0, TRIPLE_ZERO, 0), (2, SHRINK_ZERO, 3), (3, EXPAND_ZERO, 3)),
+    "after_output": (),
+    "first_back": ((2, OUTPUT_ZERO), (2, SHRINK_ZERO), (3, SHRINK_ONE)),
+    "first_back_more": (),
+    "last_back": ((0, SHRINK_MORE), (1, EXPAND_ZERO), (1, TRIPLE_ZERO), (3, EXPAND_ONE), (3, EXPAND_MORE)),
     "last": (
-        (OUTPUT_ZERO, 2),
-        (ATTEND_ONE, 5),
-        (SHRINK_ONE, 7),
-        (EXPAND_ONE, 7),
-        (TRIPLE_ZERO, 1),
-        (OUTPUT_ZERO, 3),
-        (SHRINK_ZERO, 4),
-        (ATTEND_ONE, 6),
-        (EXPAND_ZERO, 4),
-        (ATTEND_ONE, 7),
-        (OUTPUT_ZERO, 4),
-        (TRIPLE_ZERO, 2),
-        (SHRINK_ZERO, 5),
-        (EXPAND_ZERO, 5),
-        (OUTPUT_ZERO, 5),
-        (TRIPLE_ZERO, 3),
+        ATTEND_ONE, OUTPUT_ZERO, SHRINK_ZERO, SHRINK_MORE, EXPAND_ZERO, SHRINK_ONE, EXPAND_ONE, SHRINK_ONE,
+        TRIPLE_ZERO, EXPAND_MORE, OUTPUT_ZERO, SHRINK_ZERO, SHRINK_MORE, EXPAND_ONE, ATTEND_ONE, EXPAND_ZERO,
+        ATTEND_ONE, EXPAND_MORE, EXPAND_MORE, TRIPLE_ZERO, SHRINK_ZERO, OUTPUT_ZERO, SHRINK_ZERO,
+        SHRINK_MORE, SHRINK_MORE, EXPAND_ZERO, EXPAND_ZERO, TRIPLE_ZERO, TRIPLE_ZERO, OUTPUT_ZERO,
+        EXPAND_ONE, OUTPUT_ZERO, EXPAND_ONE,
     ),
 }
 
@@ -437,7 +422,6 @@
     (
         frames_ref,
         latent_ref,
-        cotangent_ref,
         input_grad_ref,
         recurrent_wide,
         readout_wide,
@@ -469,7 +453,6 @@
         gc_ref,
         gpre_ref,
         gstate_ref,
-        dcontext_ref,
         dpacked_ref,
         out_halo,
         in_halo,
@@ -528,7 +511,7 @@
                 at = lax.rem(line + i % line_count, line_count)
                 others.append((lon * line_count + at, {"lon": lon, "batch": 2 * at + core}))
             return me_lon * line_count + line, others
-        if kind == "line":
+        if kind in ("line", "gather"):
             return line, [(peer, {"batch": 2 * peer + core}) for peer in line_peers]
         mine = lax.rem(lax.div(me_lon, bit), 2)
         return mine, [(1 - mine, {"lon": me_lon + bit - 2 * bit * mine})]
@@ -536,24 +519,29 @@
     def sum_range(section, depth):
         start, rows = places.starts[places.first[section]], places.rows[section]
         for kind, bit, members in places.phases[section][:depth]:
-            rows //= members
-            start = start + members_of(kind, bit)[0] * rows
+            if kind != "gather":
+                rows //= members
+                start = start + members_of(kind, bit)[0] * rows
         return start, rows
 
     def sum_copies(section, phase):
-        phases = places.phases[section]
-        back = phase >= len(phases)
-        depth = 2 * len(phases) - 1 - phase if back else phase
-        kind, bit, members = phases[depth]
+        depth = len(places.phases[section])
+        back = phase >= depth
+        if back:
+            kind, bit, members, depth = places.back[section][phase - depth]
+        else:
+            kind, bit, members = places.phases[section][phase]
+            depth = phase
         start, rows = sum_range(section, depth)
-        piece = rows // members
-        mine, others = members_of(kind, bit)
         copies = []
-        for i, (place, device) in enumerate(others):
+        for i, (place, device) in enumerate(members_of(kind, bit)[1]):
             if back:
-                rows_out = row_span(start + mine * piece, piece)
-                src, dst = sums_ref.at[rows_out], sums_ref.at[rows_out]
+                src, dst = sums_ref.at[row_span(start, rows)], sums_ref.at[row_span(start, rows)]
+            elif kind == "gather":
+                own = row_span(places.inbox[section][phase] + line * rows, rows)
+                src, dst = sum_in.at[own], sum_in.at[own]
             else:
+                piece = rows // members
                 src = grads_ref.at[row_span(start + place * piece, piece)]
                 dst = sum_in.at[row_span(places.inbox[section][phase] + i * piece, piece)]
             sem = places.sems[section][phase] + i
@@ -569,38 +557,57 @@
             )
         return copies
 
-    def add_up(start, rows, source_at, count, target):
+    def add_up(start, rows, source_at, count, target, own=True):
         step = math.gcd(rows, LANES)
 
         def body(i, unused):
             at = row_span(start + i * step, step)
-            total = grads_ref[at].astype(F32)
-            for k in range(count):
-                total = total + sum_in[row_span(source_at + k * rows + i * step, step)].astype(F32)
+            terms = [grads_ref[at]] if own else []
+            terms += [sum_in[row_span(source_at + k * rows + i * step, step)] for k in range(count)]
+            total = terms[0].astype(F32)
+            for term in terms[1:]:
+                total = total + term.astype(F32)
             target[at] = total.astype(BF16)
 
         lax.fori_loop(0, rows // step, body, None)
 
-    def sum_start(section, phase=0):
+    begun = {}
+
+    def sum_send(section, phase):
+        depth = len(places.phases[section])
+        if phase < depth and places.phases[section][phase][0] == "gather":
+            start, rows = sum_range(section, phase)
+            sum_in[row_span(places.inbox[section][phase] + line * rows, rows)] = grads_ref[row_span(start, rows)]
+        for copy in sum_copies(section, phase):
+            copy.start()
+
+    def sum_start(section):
         if places.leader[section] == section:
-            for copy in sum_copies(section, phase):
-                copy.start()
-
-    def sum_step(section, phase):
-        if places.leader[section] != section:
+            begun[section] = 0
+            sum_send(section, 0)
+
+    def sum_left(section):
+        return len(places.phases[section]) + len(places.back[section]) - begun[section]
+
+    def sum_step(section):
+        if section not in begun or sum_left(section) == 0:
             return
+        phase = begun[section]
         for copy in sum_copies(section, phase):
             copy.wait_recv()
         depth = len(places.phases[section])
         if phase < depth:
             start, rows = sum_range(section, phase + 1)
             target = grads_ref if phase < depth - 1 else sums_ref
-            add_up(start, rows, places.inbox[section][phase], places.phases[section][phase][2] - 1, target)
-        if phase < 2 * depth - 1:
-            sum_start(section, phase + 1)
+            kind, _, members = places.phases[section][phase]
+            whole = kind == "gather"
+            add_up(start, rows, places.inbox[section][phase], members - (not whole), target, not whole)
+        begun[section] = phase + 1
+        if sum_left(section):
+            sum_send(section, phase + 1)
 
     def sum_drain(section):
-        for phase in range(2 * len(places.phases[section])):
+        for phase in range(len(places.phases[section]) + len(places.back[section])):
             for copy in sum_copies(section, phase):
                 copy.wait_send()
 
@@ -627,7 +634,7 @@
     tokens_in = [
         pltpu.make_async_copy(hbm, ref, token_sem.at[i])
         for i, (hbm, ref) in enumerate(
-            ((frames_hbm, frames_ref), (latent_hbm, latent_ref), (cotangent_hbm, cotangent_ref))
+            ((frames_hbm, frames_ref), (latent_hbm, latent_ref), (cotangent_hbm, gm_ref))
         )
     ]
 
@@ -661,15 +668,14 @@
         copy.start()
     for which in (1, 2, 3):
         wide_in(which, 0, 0).start()
-    for which in range(4):
-        wide_in(which, 0, 1).start()
-    tokens_in[2].start()
-
-    for layer, onehot_ref in ((0, gm_ref), (1, gl_ref)):
+
+    def make_bias(layer):
         table_pad[...] = jnp.zeros_like(table_pad)
         table_pad[:, :PAIRS] = table_ref[layer]
-        onehot_ref[...] = offset_onehot(layer % 2 == 1)
-        bias_ref[layer] = bias_of_table(table_pad[...], onehot_ref[...])
+        gl_ref[...] = offset_onehot(layer % 2 == 1)
+        bias_ref[layer] = bias_of_table(table_pad[...], gl_ref[...])
+
+    make_bias(0)
     for copy in small_in:
         copy.wait()
     for layer in range(LAYERS):
@@ -679,7 +685,9 @@
     tokens_in[1].wait()
     for which in range(4):
         weights_take(which, 0)
-    pl.semaphore_wait(barrier, len(neighbours))
+    for which in range(4):
+        wide_in(which, 0, 1).start()
+    tokens_in[2].start()
     gathered_ref[...] = jnp.zeros_like(gathered_ref)
 
     def span(frame):
@@ -696,8 +704,7 @@
         crop = (crop_ref[0, frame], crop_ref[1, frame])
         return attend_forward(qkv, bias_ref, layer, crop, probs_ref, frame, row_count)
 
-    def middle(layer, frame, stream, context, latent):
-        at = span(frame)
+    def middle(layer, at, stream, context, latent):
         context_ref[layer, at] = context
         one = stream + dot(context, output_low[layer])
         (stream_one, input_grad_ref)[layer][at] = one
@@ -718,40 +725,42 @@
             cols = slice(block * WIDTH, (block + 1) * WIDTH)
             inner = dot(hidden, expand_low[layer, :, cols])
             square = inner * inner
-            bend = GELU_C * (1.0 + GELU_A * square)
-            gate = 0.5 * (1.0 + jnp.tanh(inner * bend))
+            gate = 0.5 + 0.5 * jnp.tanh(inner * (GELU_C + (GELU_C * GELU_A) * square))
             active = inner * gate
-            slope = gate + active * (1.0 - gate) * (2.0 * GELU_C + 6.0 * GELU_C * GELU_A * square)
+            slope = gate + active * (1.0 - gate) * (2.0 * GELU_C + (6.0 * GELU_C * GELU_A) * square)
             active_ref[layer, at, cols] = active.astype(BF16)
+            if layer == LAYERS - 1:
+                slope = slope * slope_ref[layer, at, cols].astype(F32)
             slope_ref[layer, at, cols] = slope.astype(BF16)
         return two + dot(active_ref[layer, at], shrink_low[layer])
 
-    def feed_back(layer, frame, g):
-        at = span(frame)
-        gm = g.astype(BF16)
-        gm_ref[at] = gm
+    def feed_back(layer, at, g):
+        if layer < LAYERS - 1:
+            gm_ref[at] = g.astype(BF16)
+        gm = gm_ref[at]
         for block in range(HIDDEN // WIDTH):
             cols = slice(block * WIDTH, (block + 1) * WIDTH)
             dactive = dot_nt(gm, shrink_low[layer, cols])
-            slope_ref[layer, at, cols] = (dactive * slope_ref[layer, at, cols].astype(F32)).astype(BF16)
-
-    def middle_back(layer, frame, g, gstate):
-        at = span(frame)
+            if layer < LAYERS - 1:
+                dactive = dactive * slope_ref[layer, at, cols].astype(F32)
+            slope_ref[layer, at, cols] = dactive.astype(BF16)
+
+    def middle_back(layer, at, g, gstate):
         dhidden = dot_nt(slope_ref[layer, at], expand_low[layer])
         scaled, inverse = norm_parts((stream_two, g_ref)[layer][at])
+        scaled_one, inverse_one = norm_parts((stream_one, input_grad_ref)[layer][at])
         g = g + norm_back(dhidden, gain(layer, 1), scaled, inverse)
         gl = g.astype(BF16)
         gl_ref[at] = gl
         dstate = dot_nt(gl, readout_low[layer])
         if gstate is not None:
-            dstate = dstate + gstate
+            dstate = dstate + gstate.astype(F32)
         gpre = (dstate * bend_ref[layer, at].astype(F32)).astype(BF16)
         gpre_ref[at] = gpre
         if layer > 0:
-            gstate_ref[at] = dot(gpre, recurrent_low[layer, :, WIDTH:])
-        scaled, inverse = norm_parts((stream_one, input_grad_ref)[layer][at])
+            gstate_ref[at] = dot(gpre, recurrent_low[layer, :, WIDTH:]).astype(BF16)
         dcell = dot(gpre, recurrent_low[layer, :, :WIDTH])
-        g = g + norm_back(dcell, gain(layer, 2), scaled, inverse)
+        g = g + norm_back(dcell, gain(layer, 2), scaled_one, inverse_one)
         gc = g.astype(BF16)
         gc_ref[at] = gc
         g_ref[at] = g
@@ -810,8 +819,8 @@
         return [near[:, :LANES], near[:, LANES:], far, readout[:, :LANES], readout[:, LANES:]]
 
     def table_pieces(layer):
-        gm_ref[...] = offset_onehot(layer % 2 == 1)
-        table = table_of_bias(gathered_ref[layer], gm_ref[...])
+        gl_ref[...] = offset_onehot(layer % 2 == 1)
+        table = table_of_bias(gathered_ref[layer], gl_ref[...])
         return [table[:, :LANES], table[:, LANES:]]
 
     def put_pieces(start, pieces):
@@ -883,40 +892,58 @@
             total = total + table_in[i * TABLE_ROWS : (i + 1) * TABLE_ROWS].astype(F32)
         sums_ref[places.table[0] : places.table[0] + TABLE_ROWS] = total.astype(BF16)
 
-    def loop(body, steps=()):
+    def loop(body, steps=(), count=frame_count):
         def whole(frame, unused):
             body(frame)
-            for after in range(frame_count):
-                here = [(section, phase) for when, section, phase in steps if when == after]
+            for after in range(count):
+                here = [section for when, section in steps if when == after]
                 if here:
 
                     @pl.when(frame == after)
                     def _(here=here):
-                        for section, phase in here:
-                            sum_step(section, phase)
-
-        lax.fori_loop(0, frame_count, whole, None)
-
-    def sum_steps(*steps):
-        for section, phase in steps:
-            sum_step(section, phase)
-
-    def first_layer(frame):
-        at = span(frame)
+                        sum_steps(*here)
+
+        lax.fori_loop(0, count, whole, None)
+
+    def sum_steps(*sections):
+        for section in sections:
+            sum_step(section)
+
+    paired = 2 - frame_count % 2
+    pairs = frame_count // paired
+
+    def pair_span(pair):
+        return pl.ds(pl.multiple_of(pair * paired * tokens, paired * tokens), paired * tokens)
+
+    def frames_of(pair):
+        return [(pair * paired + i, slice(i * tokens, (i + 1) * tokens)) for i in range(paired)]
+
+    def first_layer(pair):
+        at = pair_span(pair)
         stream = frames_ref[at].astype(F32)
         scaled, _ = norm_parts(stream)
         normed = (scaled * gain(0, 0)).astype(BF16)
-        context = attention_part(0, frame, normed).astype(BF16)
-        stream = middle(0, frame, stream, context, latent_ref[at])
+        context = jnp.concatenate(
+            [attention_part(0, frame, normed[rows]).astype(BF16) for frame, rows in frames_of(pair)], axis=0
+        )
+        stream = middle(0, at, stream, context, latent_ref[at])
         stream_in[at] = stream
         scaled, _ = norm_parts(stream)
         normed = scaled * gain(1, 0)
         normed_ref[1, at] = normed.astype(BF16)
-        send_halo(0, frame, normed)
-
-    loop(first_layer)
+
+        @pl.when(pair == 0)
+        def _():
+            pl.semaphore_wait(barrier, len(neighbours))
+
+        for frame, rows in frames_of(pair):
+            send_halo(0, frame, normed[rows])
+
+    loop(first_layer, count=pairs)
+    make_bias(1)
     for which in range(4):
         weights_take(which, 1)
+    tokens_in[2].wait()
     if places.ahead:
         for layer in (1, 0):
             for which in range(4):
@@ -932,72 +959,87 @@
         send_halo(1, frame, context)
 
     loop(second_attention)
-    tokens_in[2].wait()
-
-    def second_middle(frame):
-        at = span(frame)
-        context = take_halo(1, frame, context_ref[1, at].astype(F32)).astype(BF16)
-        stream = middle(1, frame, stream_in[at], context, state_ref[0, at])
-        feed_back(1, frame, cotangent_ref[at].astype(F32))
-        cotangent_ref[at] = stream.astype(BF16)
-
-    loop(second_middle)
-    act_out = pltpu.make_async_copy(cotangent_ref, act_out_hbm, result_sem.at[frame_count])
+
+    def second_feed_back(pair):
+        feed_back(1, pair_span(pair), None)
+
+    loop(second_feed_back, count=pairs)
+
+    def second_middle(pair):
+        at = pair_span(pair)
+        context = jnp.concatenate(
+            [
+                take_halo(1, frame, context_ref[1, span(frame)].astype(F32)).astype(BF16)
+                for frame, _ in frames_of(pair)
+            ],
+            axis=0,
+        )
+        dpacked_ref[at, WIDTH : 2 * WIDTH] = middle(1, at, stream_in[at], context, state_ref[0, at]).astype(BF16)
+
+    loop(second_middle, count=pairs)
+    act_out = pltpu.make_async_copy(dpacked_ref.at[:, pl.ds(WIDTH, WIDTH)], act_out_hbm, result_sem.at[frame_count])
     act_out.start()
+
+    def second_middle_back(pair):
+        at = pair_span(pair)
+        dcontext = middle_back(1, at, gm_ref[at].astype(F32), None)
+        dpacked_ref[at, :WIDTH] = dcontext.astype(BF16)
+        for frame, rows in frames_of(pair):
+            send_halo(2, frame, dcontext[rows])
+
+    loop(second_middle_back, STEPS["second_middle_back"], pairs)
     shrink_grads(1)
     sum_start(SHRINK_ONE)
     expand_grads(1)
     sum_start(EXPAND_ONE)
-
-    def second_middle_back(frame):
-        at = span(frame)
-        dcontext = middle_back(1, frame, gm_ref[at].astype(F32), None)
-        dcontext_ref[at] = dcontext.astype(BF16)
-        send_halo(2, frame, dcontext)
-
-    loop(second_middle_back, STEPS["second_middle_back"])
     output_grads(1)
     early_one = put_pieces(places.early[1], small_grads(1, state_ref[0]))
+    sum_steps(*STEPS["before_second_back"])
+    act_out.wait()
 
     def second_back(frame):
         at = span(frame)
-        dcontext = take_halo(2, frame, dcontext_ref[at].astype(F32))
+        dcontext = take_halo(2, frame, dpacked_ref[at, :WIDTH].astype(F32))
         dcontext = rows_ahead(dcontext).astype(BF16)
         values_back(1, frame, dcontext)
         attention_back(1, frame, dcontext)
         dnormed = rows_behind(packed_back(1, frame))
-        dcontext_ref[at] = dnormed.astype(BF16)
+        gc_ref[at] = dnormed.astype(BF16)
         send_halo(3, frame, dnormed)
 
     loop(second_back, STEPS["second_back"])
     triple_grads(1, (0, 1, 2))
     clear_spare(ATTEND_ONE)
     sum_start(ATTEND_ONE)
+    clear_rows(put_pieces(early_one, table_pieces(1)), places.early[1] + SMALL_ROWS)
+    sum_steps(*STEPS["before_first_feed_back"])
 
     def first_feed_back(frame):
         at = span(frame)
-        dnormed = take_halo(3, frame, dcontext_ref[at].astype(F32))
+        dnormed = take_halo(3, frame, gc_ref[at].astype(F32))
         g = stream_back(1, frame, g_ref[at], stream_in[at], dnormed)
         g_ref[at] = g
-        feed_back(0, frame, g)
+        feed_back(0, at, g)
 
     loop(first_feed_back, STEPS["first_feed_back"])
     shrink_grads(0)
     sum_start(SHRINK_ZERO)
+    sum_start(SHRINK_MORE)
     sum_steps(*STEPS["after_shrink"])
     expand_grads(0)
     sum_start(EXPAND_ZERO)
-
-    def first_middle_back(frame):
-        at = span(frame)
-        dcontext = middle_back(0, frame, g_ref[at], gstate_ref[at]).astype(BF16)
-        dcontext_ref[at] = dcontext
-        values_back(0, frame, dcontext)
-
-    loop(first_middle_back, STEPS["first_middle_back"])
+    sum_start(EXPAND_MORE)
+
+    def first_middle_back(pair):
+        at = pair_span(pair)
+        dcontext = middle_back(0, at, g_ref[at], gstate_ref[at]).astype(BF16)
+        dpacked_ref[at, :WIDTH] = dcontext
+        for frame, rows in frames_of(pair):
+            values_back(0, frame, dcontext[rows])
+
+    loop(first_middle_back, STEPS["first_middle_back"], pairs)
     output_grads(0)
     triple_grads(0, (2,))
-    clear_rows(put_pieces(early_one, table_pieces(1)), places.early[1] + SMALL_ROWS)
     clear_rows(put_pieces(places.early[0], small_grads(0, latent_ref[...])), places.early[1])
     clear_spare(OUTPUT_ZERO)
     sum_start(OUTPUT_ZERO)
@@ -1008,7 +1050,7 @@
         return pltpu.make_async_copy(input_grad_ref.at[at], input_grad_hbm.at[at], result_sem.at[frame])
 
     def first_back(frame):
-        attention_back(0, frame, dcontext_ref[span(frame)])
+        attention_back(0, frame, dpacked_ref[span(frame), :WIDTH])
 
     loop(first_back, STEPS["first_back"])
     triple_grads(0, (0, 1))
@@ -1029,6 +1071,8 @@
     if places.few:
         table_spread()
     sum_steps(*STEPS["last"])
+    while any(sum_left(section) for section in begun):
+        sum_steps(*begun)
     if places.few:
         table_take()
         table_core().wait_send()
@@ -1041,7 +1085,6 @@
         grad_out(frame).wait()
 
     lax.fori_loop(0, frame_count, drain, None)
-    act_out.wait()
     if places.ahead:
         for layer in (1, 0):
             for which in range(4):
@@ -1071,7 +1114,6 @@
     scratch = [
         one(count, WIDTH),
         one(count, LATENT),
-        one(count, WIDTH),
         wide(count, WIDTH),
         wide(LAYERS, LATENT, WIDTH + LATENT),
         wide(LAYERS, LATENT, WIDTH),
@@ -1102,8 +1144,7 @@
         one(count, WIDTH),
         one(count, WIDTH),
         one(count, LATENT),
-        wide(count, LATENT),
-        one(count, WIDTH),
+        one(count, LATENT),
         one(count, 3 * WIDTH),
         one(2, frame_count, tokens // 2, WIDTH),
         one(2, frame_count, tokens // 2, WIDTH),
@@ -1226,7 +1267,8 @@
         return old[0].astype(BF16).astype(F32) * gradient
 
     def change_blocks(which, layer, starts, rows, norm=None):
-        step = 32
+        step = 256 // len(starts)
+        step = 32 if step < 64 else min(step, 128)
 
         def body(i, unused):
             row = pl.multiple_of(i * step, step)

time: 106 us -> 93.5 us (0.88)
  Pallas kernels: 105 us -> 92.3 us
    pallas_call x1, Pallas kernels: 95.9 us -> 83.9 us  [layers_step(): pl.pallas_call(functools.partial(kernel, places), out_shape=(pltpu.HBM((c...]
where the time goes in v4:
time: 93.5 us; the launch traced here: 93.2 us
  Pallas kernels  92.3 us (99%)
    pallas_call x1, Pallas kernels, layers_step(): pl.pallas_call(functools.partial(kernel, places), out_shape=(pltpu.HBM((c...  83.9 us
    pallas_call x1, Pallas kernels, update_step(): pl.pallas_call(functools.partial(update_kernel, scale, places), out_shape...  8.42 us

profile of v4, /device:TPU:0, one launch (start us, length us, event | category | flops | bytes accessed | tf_op | source)
XLA Modules:
  0.0 93.2 jit_solution(17861518880885736274)
XLA Ops:
  0.7 83.9 %swin_step.1 = (bf16[1024,256]{1,0:T(8,128)(2,1)}, f32[1024,256]{1,0:T(8,128)}, bf16[12816,128]{1,0:T(8,128)(2,1)S(1)}, f32[2,256,768]{2,1,0:T(8,128)S(1)}, f32[...) custom-call(s32[2,4]{1,0:T(2,128)} %bitcast.29, ...), custom_call_target="tpu_custom_call" | custom-call | tf_op jit(solution)/shard_map/swin_step/pallas_call | solution.py:1169
  84.6 8.4 %nesterov_step.1 = (bf16[1024,256]{1,0:T(8,128)(2,1)}, f32[1024,256]{1,0:T(8,128)}, f32[2,256,768]{2,1,0:T(8,128)}, f32[2,256,768]{2,1,0:T(8,128)}, f32[2,256,76...) custom-call(bf16[12816,128]{1,0:T(8,128)(2,1)S(1)} %get-tuple-elemen, ...), custom_call_target="tpu_custom_call" | custom-call | tf_op jit(solution)/shard_map/nesterov_step/pallas_call | solution.py:1365

commit v5 on v4

--- a/solution.py
+++ b/solution.py
@@ -381,6 +381,7 @@
     ]
 
 
+LAST_STEPS = 6
 STEPS = {
     "second_middle_back": (),
     "before_second_back": (),
@@ -393,9 +394,9 @@
         (0, ATTEND_ONE), (0, EXPAND_ONE),
     ),
     "after_output": (),
-    "first_back": ((2, OUTPUT_ZERO), (2, SHRINK_ZERO), (3, SHRINK_ONE)),
+    "first_back": ((2, OUTPUT_ZERO), (2, SHRINK_ZERO), (2, SHRINK_ONE), (3, SHRINK_MORE)),
     "first_back_more": (),
-    "last_back": ((0, SHRINK_MORE), (1, EXPAND_ZERO), (1, TRIPLE_ZERO), (3, EXPAND_ONE), (3, EXPAND_MORE)),
+    "last_back": ((0, EXPAND_ZERO), (1, TRIPLE_ZERO), (3, EXPAND_ONE), (3, EXPAND_MORE)),
     "last": (
         ATTEND_ONE, OUTPUT_ZERO, SHRINK_ZERO, SHRINK_MORE, EXPAND_ZERO, SHRINK_ONE, EXPAND_ONE, SHRINK_ONE,
         TRIPLE_ZERO, EXPAND_MORE, OUTPUT_ZERO, SHRINK_ZERO, SHRINK_MORE, EXPAND_ONE, ATTEND_ONE, EXPAND_ZERO,
@@ -606,10 +607,13 @@
         if sum_left(section):
             sum_send(section, phase + 1)
 
+    drained = {}
+
     def sum_drain(section):
-        for phase in range(len(places.phases[section]) + len(places.back[section])):
+        for phase in range(drained.get(section, 0), begun[section]):
             for copy in sum_copies(section, phase):
                 copy.wait_send()
+        drained[section] = begun[section]
 
     def halo(exchange, frame):
         return pltpu.make_async_remote_copy(
@@ -1070,27 +1074,30 @@
     loop(last_back, STEPS["last_back"])
     if places.few:
         table_spread()
-    sum_steps(*STEPS["last"])
-    while any(sum_left(section) for section in begun):
-        sum_steps(*begun)
+    sum_steps(*STEPS["last"][:-LAST_STEPS])
+
+    def drain(frame, unused):
+        for exchange in (2, 3):
+            halo(exchange, frame).wait_send()
+        grad_out(frame).wait()
+
+    lax.fori_loop(0, frame_count, drain, None)
     if places.few:
         table_take()
         table_core().wait_send()
         for copy in table_copies():
             copy.wait_send()
-
-    def drain(frame, unused):
-        for exchange in (2, 3):
-            halo(exchange, frame).wait_send()
-        grad_out(frame).wait()
-
-    lax.fori_loop(0, frame_count, drain, None)
     if places.ahead:
         for layer in (1, 0):
             for which in range(4):
                 for kind in (1, 2):
                     wide_in(which, kind, layer).wait()
-    for section in places.rows:
+    for section in begun:
+        sum_drain(section)
+    sum_steps(*STEPS["last"][-LAST_STEPS:])
+    while any(sum_left(section) for section in begun):
+        sum_steps(*begun)
+    for section in begun:
         sum_drain(section)
 
 

time: 93.5 us -> 92.6 us (level)
  no operation moved by 1% of the time
where the time goes in v5:
time: 92.6 us; the launch traced here: 92.3 us
  Pallas kernels  91.5 us (99%)
    pallas_call x1, Pallas kernels, layers_step(): pl.pallas_call(functools.partial(kernel, places), out_shape=(pltpu.HBM((c...  83.1 us
    pallas_call x1, Pallas kernels, update_step(): pl.pallas_call(functools.partial(update_kernel, scale, places), out_shape...  8.42 us

profile of v5, /device:TPU:0, one launch (start us, length us, event | category | flops | bytes accessed | tf_op | source)
XLA Modules:
  0.0 92.3 jit_solution(12164769344435577499)
XLA Ops:
  0.7 83.1 %swin_step.1 = (bf16[1024,256]{1,0:T(8,128)(2,1)}, f32[1024,256]{1,0:T(8,128)}, bf16[12816,128]{1,0:T(8,128)(2,1)S(1)}, f32[2,256,768]{2,1,0:T(8,128)S(1)}, f32[...) custom-call(s32[2,4]{1,0:T(2,128)} %bitcast.29, ...), custom_call_target="tpu_custom_call" | custom-call | tf_op jit(solution)/shard_map/swin_step/pallas_call | solution.py:1176
  83.8 8.4 %nesterov_step.1 = (bf16[1024,256]{1,0:T(8,128)(2,1)}, f32[1024,256]{1,0:T(8,128)}, f32[2,256,768]{2,1,0:T(8,128)}, f32[2,256,768]{2,1,0:T(8,128)}, f32[2,256,76...) custom-call(bf16[12816,128]{1,0:T(8,128)(2,1)S(1)} %get-tuple-elemen, ...), custom_call_target="tpu_custom_call" | custom-call | tf_op jit(solution)/shard_map/nesterov_step/pallas_call | solution.py:1372
